TPU v7x, 512 devices: a whole 4x8x8 slice. The times are simulated.
512 devices in a mesh: rep: 128 (over z, y, core), shard: 4 (over x).
Axes of the slice: x: 4, y: 8, z: 8, core: 2. Of those that a mesh axis runs over, the one named last changes fastest.
Arguments:
- grad_query: bfloat16 [128, 128, 8192], P('rep', 'shard'), may hold values from -24 to 24
- error_query: bfloat16 [128, 128, 8192], P('rep', 'shard'), may hold values from -4 to 4
- q_query: float32 [64, 8192], P(None, ('rep', 'shard')), may hold values from -6 to 6
- grad_down: bfloat16 [128, 256, 8192], P('rep', 'shard'), may hold values from -24 to 24
- error_down: bfloat16 [128, 256, 8192], P('rep', 'shard'), may hold values from -4 to 4
- q_down: float32 [64, 8192], P(None, ('rep', 'shard')), may hold values from -6 to 6
Outputs:
- error_query_new: bfloat16 [128, 128, 8192], P('rep', 'shard')
- basis_query: float32 [128, 64], P('shard')
- q_query_new: float32 [64, 8192], P(None, ('rep', 'shard'))
- error_down_new: bfloat16 [128, 256, 8192], P('rep', 'shard')
- basis_down: float32 [256, 64], P('shard')
- q_down_new: float32 [64, 8192], P(None, ('rep', 'shard'))
All inputs are finite; a program needn't handle non-finite values.
Results may differ from a plain program's by a relative error of at most 0.001.
Values sent between devices are 32-bit elements; how exact they have to be, the bound alone decides.
No kernel may reach another device: no remote copies, remote signals or barrier semaphores. Data moves between devices by JAX's collectives and lax.ppermute only.
A program may use at most 64 MiB of HBM per device.

v0:
```python
import jax
import jax.numpy as jnp
from jax import lax
from jax.sharding import PartitionSpec as P


def local_factor(merged, q_whole):
    return jnp.dot(merged, q_whole.T, precision=lax.Precision.HIGHEST)


def gram_of(factor):
    return jnp.dot(factor.T, factor, precision=lax.Precision.HIGHEST)


def basis_of(gram, factor):
    lower = jnp.linalg.cholesky(gram)
    return jax.scipy.linalg.solve_triangular(lower, factor.T, lower=True).T


def on_device(grad_query, error_query, q_query, grad_down, error_down, q_down):
    high = lax.Precision.HIGHEST
    rep_count = lax.axis_size("rep")
    shard_count = lax.axis_size("shard")
    shard_index = lax.axis_index("shard")
    q_whole_query, q_whole_down = (
        lax.all_gather(q_query, ("rep", "shard"), axis=1, tiled=True),
        lax.all_gather(q_down, ("rep", "shard"), axis=1, tiled=True),
    )
    merged_query = grad_query[0].astype(jnp.float32) + error_query[0].astype(jnp.float32)
    merged_down = grad_down[0].astype(jnp.float32) + error_down[0].astype(jnp.float32)
    factor_query = local_factor(merged_query, q_whole_query)
    factor_down = local_factor(merged_down, q_whole_down)
    factor_query, factor_down = lax.psum((factor_query, factor_down), "rep")
    gram_query, gram_down = lax.psum((gram_of(factor_query), gram_of(factor_down)), "shard")
    basis_query = basis_of(gram_query, factor_query)
    basis_down = basis_of(gram_down, factor_down)
    term_query = jnp.dot(basis_query.T, merged_query, precision=high)
    term_down = jnp.dot(basis_down.T, merged_down, precision=high)
    total_query, total_down = lax.psum((term_query, term_down), ("rep", "shard"))
    q_new_query = total_query / rep_count
    q_new_down = total_down / rep_count
    width = q_query.shape[1]
    block = lax.axis_index("rep") * shard_count + shard_index
    q_query_new = lax.dynamic_slice_in_dim(q_new_query, block * width, width, 1)
    q_down_new = lax.dynamic_slice_in_dim(q_new_down, block * width, width, 1)
    approx_query = jnp.dot(basis_query, q_new_query, precision=high)
    approx_down = jnp.dot(basis_down, q_new_down, precision=high)
    error_query_new = (merged_query - approx_query).astype(jnp.bfloat16)[None]
    error_down_new = (merged_down - approx_down).astype(jnp.bfloat16)[None]
    return (error_query_new, basis_query, q_query_new, error_down_new, basis_down, q_down_new)


def solution(mesh):
    in_specs = (
        P("rep", "shard", None),
        P("rep", "shard", None),
        P(None, ("rep", "shard")),
        P("rep", "shard", None),
        P("rep", "shard", None),
        P(None, ("rep", "shard")),
    )
    out_specs = (
        P("rep", "shard", None),
        P("shard", None),
        P(None, ("rep", "shard")),
        P("rep", "shard", None),
        P("shard", None),
        P(None, ("rep", "shard")),
    )
    return jax.shard_map(
        on_device, mesh=mesh, in_specs=in_specs, out_specs=out_specs, check_vma=False
    )
```

profile of v0, /device:TPU:1, one launch (start us, length us, event | category | flops | bytes accessed | tf_op | source)
XLA Modules:
  0.0 1096.8 jit_solution(17381167058529380360)
XLA Ops:
  7.2 0.7 all-gather.5.cloned.1.call-update
  7.9 0.7 all-gather.3.cloned.1.call-update
  8.7 128.0 %all-gather.5.cloned.1.call-done = f32[64,8192]{0,1:T(8,128)} async-done(((f32[64,16]{0,1:T(8,128)}), f32[64,8192]{0,1:T(8,128)}) %all-gather.5.cloned.1.call-update) | async-done | bytes 2097168 | tf_op jit(solution)/shard_map/all_gather | solution.py:27
  136.8 5.7 fusion.6
  142.5 113.4 %all-gather.3.cloned.1.call-done = f32[64,8192]{0,1:T(8,128)} async-done(((f32[64,16]{0,1:T(8,128)}), f32[64,8192]{0,1:T(8,128)}) %all-gather.3.cloned.1.call-update) | async-done | bytes 2097168 | tf_op jit(solution)/shard_map/all_gather | solution.py:26
  255.9 4.1 fusion.10
  260.0 488.8 %all-reduce.1 = (f32[32,64]{1,0:T(8,128)S(1)}, f32[64,64]{1,0:T(8,128)S(1)}) all-reduce(f32[32,64]{1,0:T(8,128)S(1)} %fusion.10, f32[64,64]{1,0:T(8,128)S(1)} %fusion.6), channel_id=1, replica_groups=mesh['rep'=128,'shard'=4] {'rep'}, use_global_device_ids=true, to_apply=%region_0.0 | all-reduce | flops 6144 | bytes 49152 | tf_op jit(solution)/shard_map/psum | solution.py:33
  748.8 0.2 fusion.20
  749.0 0.2 fusion.21
  749.3 13.1 %all-reduce.2 = (f32[64,64]{0,1:T(8,128)S(1)}, f32[64,64]{0,1:T(8,128)S(1)}) all-reduce(f32[64,64]{0,1:T(8,128)S(1)} %fusion.20, f32[64,64]{0,1:T(8,128)S(1)} %fusion.21), channel_id=1, replica_groups=mesh['rep'=128,'shard'=4] {'shard'}, use_global_device_ids=true, to_apply=%region_1.0 | all-reduce | flops 8192 | bytes 65536 | tf_op jit(solution)/shard_map/psum | solution.py:34
  762.6 5.8 cholesky.55
  768.4 0.6 compare_reduce_fusion
  769.1 0.7 fusion.13
  769.8 4.9 custom-call.11
  774.6 0.2 fusion.14
  774.9 3.2 fusion.4
  778.1 5.8 cholesky.44
  784.0 0.6 compare_reduce_fusion.1
  784.7 0.7 fusion.12
  785.3 4.9 custom-call.10
  790.2 0.2 fusion.17
  790.4 3.2 fusion.8
  793.6 0.7 copy.17
  794.3 285.4 %all-reduce.5.cloned.1.call-done = (f32[64,8192]{1,0:T(8,128)}, f32[64,8192]{1,0:T(8,128)}) async-done(((f32[64,8192]{1,0:T(8,128)}, f32[64,8192]{1,0:T(8,128)}), (f32[64,8192]{1,0:T(8,128)}, f32[64,8192]{1,0:T(8,128)})) %all-reduce.5.cloned.1.call-update) | async-done | bytes 4194320 | tf_op jit(solution)/shard_map/psum | solution.py:39
  1079.7 3.2 broadcast_multiply_fusion
  1082.9 3.0 fusion.1
  1085.9 0.2 broadcast_multiply_fusion.1
  1086.0 2.0 fusion.3
  1088.0 0.1 constant_dynamic-slice_fusion.1
  1088.1 0.7 copy.16
  1088.8 0.8 constant_dynamic-slice_fusion
  1089.6 0.7 copy.18
  (23 shorter events, 0.4 us)
Async XLA Ops:
  7.2 129.6 %all-gather.5.cloned.1.call-start = ((), (), s32[]{:S(2)}) async-start(), calls=%async_computation.1 | async-start | bytes 4202496 | tf_op jit(solution)/shard_map/all_gather | solution.py:27
  7.9 248.0 %all-gather.3.cloned.1.call-start = ((), (), s32[]{:S(2)}) async-start(), calls=%async_computation | async-start | bytes 4202496 | tf_op jit(solution)/shard_map/all_gather | solution.py:26
  8.7 247.2 %copy-start.4 = (bf16[1,32,8192]{2,1,0:T(8,128)(2,1)S(1)}, bf16[1,32,8192]{2,1,0:T(8,128)(2,1)}, u32[]{:S(2)}) copy-start(bf16[1,32,8192]{2,1,0:T(8,128)(2,1)} %param.8) | copy-start | bytes 1572868
  8.7 247.2 %copy-start.5 = (bf16[1,32,8192]{2,1,0:T(8,128)(2,1)S(1)}, bf16[1,32,8192]{2,1,0:T(8,128)(2,1)}, u32[]{:S(2)}) copy-start(bf16[1,32,8192]{2,1,0:T(8,128)(2,1)} %param.7) | copy-start | bytes 1572868
  8.7 1071.0 %all-reduce.5.cloned.1.call-start = ((), (), s32[]{:S(2)}) async-start(), calls=%async_computation.2 | async-start | bytes 8388608 | tf_op jit(solution)/shard_map/psum | solution.py:39
  142.4 632.5 %copy-start = (bf16[1,64,8192]{2,1,0:T(8,128)(2,1)S(1)}, bf16[1,64,8192]{2,1,0:T(8,128)(2,1)}, u32[]{:S(2)}) copy-start(bf16[1,64,8192]{2,1,0:T(8,128)(2,1)} %param.11) | copy-start | bytes 3145732
  142.5 632.5 %copy-start.1 = (bf16[1,64,8192]{2,1,0:T(8,128)(2,1)S(1)}, bf16[1,64,8192]{2,1,0:T(8,128)(2,1)}, u32[]{:S(2)}) copy-start(bf16[1,64,8192]{2,1,0:T(8,128)(2,1)} %param.10) | copy-start | bytes 3145732
  790.4 295.6 %copy-start.6 = (f32[64,32]{0,1:T(8,128)}, f32[64,32]{0,1:T(8,128)S(1)}, u32[]{:S(2)}) copy-start(f32[64,32]{0,1:T(8,128)S(1)} %fusion.17) | copy-start | bytes 24580
  1079.7 3.2 copy-start.3
  1082.9 3.0 copy-start.2
Sparse Core Ops, SparseCore 0:
  12.2 124.5 all-gather.4
  140.9 114.8 all-gather.2
  793.7 285.9 all-reduce.4
where the time goes:
time: 1100 us
  waiting for transfers between devices  528 us (48%)
  blocking collectives  502 us (46%)
  other arithmetic  27.5 us (2%)
  matrix products  22 us (2%)
  between operations  13.9 us (1%)
    psum x1, blocking collectives, on_device(): factor_query, factor_down = lax.psum((factor_query, factor_down), 'rep')  489 us
    psum x1, waiting for transfers between devices, on_device(): lax.psum((term_query, term_down), ('rep', 'shard'))  285 us
    all_gather x1, waiting for transfers between devices, on_device(): lax.all_gather(q_down, ('rep', 'shard'), axis=1, tiled=True)  128 us
    all_gather x1, waiting for transfers between devices, on_device(): lax.all_gather(q_query, ('rep', 'shard'), axis=1, tiled=True)  113 us
  transfers between devices with their start and end apart: 3, of which 3 were waited for; matrix products, arithmetic and copies ran while one was open for 1% of the time, Pallas kernels for 0%

commit v1 on v0

v1 whole, which is shorter than its diff:
```python
import jax
import jax.numpy as jnp
from jax import lax
from jax.experimental import pallas as pl
from jax.experimental.pallas import tpu as pltpu
from jax.sharding import Mesh, PartitionSpec as P

NZ, NY, NC, NX = 8, 8, 2, 4
AXES = ("z", "y", "core", "x")
RANK = 64
LANES = 128
QH, DH = 16, 32
HALF = QH + DH
PACK = HALF // 2
HIGH = lax.Precision.HIGHEST
PARAMS = pltpu.CompilerParams(vmem_limit_bytes=40 * 1024 * 1024)


def device_of(z, y, core, x):
    return ((z * NY + y) * NC + core) * NX + x


def split_groups(core_along_y):
    groups = []
    for core in range(NC):
        for x in range(NX):
            for fixed in range(8):
                if core == core_along_y:
                    groups.append([device_of(fixed, v, core, x) for v in range(8)])
                else:
                    groups.append([device_of(v, fixed, core, x) for v in range(8)])
    return groups


WIDE = split_groups(0)
NARROW = split_groups(1)


def exchange(x, groups):
    return lax.all_to_all(x, AXES, 0, 0, axis_index_groups=groups, tiled=True)


def column_of(core, i, j):
    block = jnp.where(core == 0, j * NY + i, i * NY + j)
    return pl.multiple_of(block * LANES, LANES)


def merge_kernel(core_ref, gq, eq, gd, ed, qq, qd, send, keep, qpack):
    core = core_ref[0]
    f32 = jnp.float32
    for out, owner in ((send, 1 - core), (keep, core)):
        rq = pl.ds(pl.multiple_of(owner * QH, QH), QH)
        rd = pl.ds(pl.multiple_of(owner * DH, DH), DH)
        for i in range(8):
            for j in range(8):
                cols = pl.ds(column_of(owner, i, j), LANES)
                out[i, j, 0:QH, :] = gq[rq, cols].astype(f32) + eq[rq, cols].astype(f32)
                out[i, j, QH:HALF, :] = gd[rd, cols].astype(f32) + ed[rd, cols].astype(f32)
    qpack[...] = jnp.concatenate([qq[...], qd[...]], axis=1)


def factor_kernel(parts, qpack, s_ref, f_ref):
    s = parts[0]
    for i in range(1, 8):
        s = s + parts[i]
    s_ref[...] = s
    r = jnp.dot(s, qpack[...], precision=HIGH, preferred_element_type=jnp.float32)
    low = jnp.concatenate([r[0:QH], pltpu.roll(r[40:48], RANK, 1)], axis=0)
    lane = lax.broadcasted_iota(jnp.int32, (PACK, LANES), 1)
    packed = jnp.where(lane < RANK, low, r[QH:40])
    for i in range(8):
        f_ref[i] = packed


def unpack_factor(p):
    lane_q = lax.broadcasted_iota(jnp.int32, (QH, LANES), 1)
    lane_d = lax.broadcasted_iota(jnp.int32, (DH, LANES), 1)
    fq = jnp.where(lane_q < RANK, p[0:QH], 0.0)
    fd = jnp.where(lane_d >= RANK, jnp.concatenate([p, pltpu.roll(p[QH:PACK], RANK, 1)], axis=0), 0.0)
    return fq, fd


def inverse_lower(gram):
    row = lax.broadcasted_iota(jnp.int32, (8, LANES), 0)
    lane = lax.broadcasted_iota(jnp.int32, (8, LANES), 1)
    nb = RANK // 8
    q, d = [], []
    for b in range(nb):
        eye_q = jnp.where(lane - RANK == row + 8 * b, 1.0, 0.0)
        eye_d = jnp.where(lane == row + 8 * b, 1.0, 0.0)
        q.append(jnp.where(lane < RANK, gram[8 * b:8 * b + 8], eye_q))
        d.append(jnp.where(lane >= RANK, gram[RANK + 8 * b:RANK + 8 * b + 8], eye_d))
    for k in range(RANK):
        b0, s = divmod(k, 8)
        for m, at in ((q, k), (d, RANK + k)):
            inv = lax.rsqrt(m[b0][s:s + 1, at:at + 1])
            top = m[b0][s:s + 1, :] * inv
            for b in range(b0, nb):
                col = m[b][:, at:at + 1] * inv
                if b == b0:
                    col = jnp.where(row > s, col, 0.0)
                    m[b] = jnp.where(row == s, top, m[b] - col * top)
                else:
                    m[b] = m[b] - col * top
    zero = jnp.zeros((8, LANES), jnp.float32)
    out = [jnp.where(lane < RANK, pltpu.roll(m, RANK, 1), zero) for m in q]
    out += [jnp.where(lane >= RANK, pltpu.roll(m, RANK, 1), zero) for m in d]
    return jnp.concatenate(out, axis=0)


def contract(a, b, dims):
    return lax.dot_general(a, b, (dims, ((), ())), precision=HIGH, preferred_element_type=jnp.float32)


def solve_kernel(where_ref, all_ref, basis_q, basis_d, qn_q, qn_d, approx, qn_scratch):
    core, x = where_ref[0], where_ref[1]
    f_rows, s_rows = [], []
    for g in range(8):
        fq, fd = unpack_factor(all_ref[g, 0:PACK])
        f_rows += [fq, fd]
        s_rows.append(all_ref[g, PACK:PACK + HALF])
    f = jnp.concatenate(f_rows, axis=0)
    s = jnp.concatenate(s_rows, axis=0)
    rows = ((0,), (0,))
    lanes = ((1,), (1,))
    gram = contract(f, f, rows)
    cross = contract(s, f, rows)
    inv = inverse_lower(gram)
    qn = contract(cross, inv, lanes) * (1.0 / (NZ * NY * NC))
    qn_scratch[0] = qn
    qn_scratch[1] = pltpu.roll(qn, RANK, 1)
    own = pl.ds(pl.multiple_of(core * 64 + x * 16, 16), 16)
    qn_q[...] = qn_scratch[0, own, 0:RANK]
    qn_d[...] = qn_scratch[1, own, 0:RANK]
    halves = []
    for c in range(NC):
        fq, fd = unpack_factor(all_ref[c * NX + x, 0:PACK])
        b = contract(jnp.concatenate([fq, fd], axis=0), inv, lanes)
        halves.append(b)
        basis_q[c * QH:(c + 1) * QH, :] = b[0:QH, 0:RANK]
        basis_d[c * DH:(c + 1) * DH, :] = pltpu.roll(b[QH:HALF], RANK, 1)[:, 0:RANK]
    mine = jnp.where(core == 0, halves[0], halves[1])
    a = contract(mine, qn, lanes)
    for i in range(8):
        approx[i] = a


def error_kernel(core_ref, gq, eq, gd, ed, own, other, out_q, out_d):
    core = core_ref[0]
    f32 = jnp.float32
    for src, owner in ((own, core), (other, 1 - core)):
        rq = pl.ds(pl.multiple_of(owner * QH, QH), QH)
        rd = pl.ds(pl.multiple_of(owner * DH, DH), DH)
        for i in range(8):
            for j in range(8):
                cols = pl.ds(column_of(owner, i, j), LANES)
                mq = gq[rq, cols].astype(f32) + eq[rq, cols].astype(f32)
                md = gd[rd, cols].astype(f32) + ed[rd, cols].astype(f32)
                out_q[rq, cols] = (mq - src[i, j, 0:QH, :]).astype(jnp.bfloat16)
                out_d[rd, cols] = (md - src[i, j, QH:HALF, :]).astype(jnp.bfloat16)


def shape(*dims, dtype=jnp.float32):
    return jax.ShapeDtypeStruct(dims, dtype)


def call(kernel, n_in, out_shape, scalars=0, scratch=()):
    vmem = pl.BlockSpec(memory_space=pltpu.VMEM)
    smem = pl.BlockSpec(memory_space=pltpu.SMEM)
    return pl.pallas_call(
        kernel,
        out_shape=out_shape,
        in_specs=[smem] * scalars + [vmem] * n_in,
        out_specs=jax.tree.map(lambda _: vmem, out_shape),
        scratch_shapes=list(scratch),
        compiler_params=PARAMS,
    )


def swap_cores(x):
    return lax.ppermute(x, "core", [(0, 1), (1, 0)])


def on_device(grad_query, error_query, q_query, grad_down, error_down, q_down):
    core = lax.axis_index("core").astype(jnp.int32)
    place = jnp.stack([core, lax.axis_index("x").astype(jnp.int32)])
    half = shape(8, 8, HALF, LANES)
    grads = (grad_query[0], error_query[0], grad_down[0], error_down[0])
    send, keep, qpack = call(merge_kernel, 6, (half, half, shape(16, LANES)), 1)(
        place, *grads, q_query.T, q_down.T
    )
    q_all = lax.all_to_all(
        jnp.broadcast_to(qpack[None], (8, 16, LANES)), ("core", "x"), 0, 0, tiled=True
    ).reshape(LANES, LANES)
    part = exchange(keep + swap_cores(send), WIDE)
    part = exchange(jnp.sum(part, axis=0), NARROW)
    s_own, f = call(factor_kernel, 2, (shape(HALF, LANES), shape(8, PACK, LANES)))(part, q_all)
    f = exchange(f, NARROW)
    f = jnp.broadcast_to(jnp.sum(f, axis=0)[None], (8, PACK, LANES))
    f = jnp.sum(exchange(f, WIDE), axis=0)
    both = jnp.concatenate([f, s_own], axis=0)
    both = lax.all_to_all(
        jnp.broadcast_to(both[None], (8, PACK + HALF, LANES)), ("core", "x"), 0, 0, tiled=True
    )
    basis_q, basis_d, qn_q, qn_d, approx = call(
        solve_kernel,
        1,
        (shape(2 * QH, RANK), shape(2 * DH, RANK), shape(16, RANK), shape(16, RANK), shape(8, HALF, LANES)),
        1,
        [pltpu.VMEM((2, LANES, LANES), jnp.float32)],
    )(place, both)
    approx = exchange(approx, NARROW)
    own = exchange(jnp.broadcast_to(approx[None], (8, 8, HALF, LANES)), WIDE)
    other = swap_cores(own)
    err_q, err_d = call(
        error_kernel, 6, (shape(2 * QH, 8192, dtype=jnp.bfloat16), shape(2 * DH, 8192, dtype=jnp.bfloat16)), 1
    )(place, *grads, own, other)
    return (err_q[None], basis_q, qn_q.T, err_d[None], basis_d, qn_d.T)


def solution(mesh):
    torus = Mesh(mesh.devices.reshape(NZ, NY, NC, NX), AXES)
    rep = ("z", "y", "core")
    big = P(rep, "x", None)
    right = P(None, AXES)
    left = P("x", None)
    return jax.shard_map(
        on_device,
        mesh=torus,
        in_specs=(big, big, right, big, big, right),
        out_specs=(big, left, right, big, left, right),
        check_vma=False,
    )
```

time: 1100 us -> 165 us (0.15)
  waiting for transfers between devices: 528 us -> 10.9 us
  blocking collectives: 502 us -> 116 us
  other arithmetic: 27.5 us -> 0.44 us
  matrix products: 22 us -> 0 us
  starting transfers between devices: 0.11 us -> 17.8 us
  between operations: 13.9 us -> 0.75 us
  Pallas kernels: 0 us -> 11.9 us
    psum x2 -> x0, blocking collectives: 502 us -> none  [the longest x1 489 us: on_device(): factor_query, factor_down = lax.psum((factor_query, factor_down), 'rep')]
    psum x1 -> x0, waiting for transfers between devices: 285 us -> none  [on_device(): lax.psum((term_query, term_down), ('rep', 'shard'))]
    all_gather x2 -> x0, waiting for transfers between devices: 241 us -> none  [the longest x1 128 us: on_device(): lax.all_gather(q_down, ('rep', 'shard'), axis=1, tiled=True)]
    all_to_all x0 -> x7, blocking collectives: none -> 116 us  [the longest x6 102 us: exchange(): return lax.all_to_all(x, AXES, 0, 0, axis_index_groups=groups, tiled=True)]
    another operation x10 -> x1, other arithmetic: 24.1 us -> 0.08 us  [on_device(): place = jnp.stack([core, lax.axis_index('x').astype(jnp.int32)])]
    dot_general x8 -> x0, matrix products: 21.6 us -> none  [the longest x2 9.79 us: local_factor(): return jnp.dot(merged, q_whole.T, precision=lax.Precision.HIGHEST)]
    ppermute x0 -> x2, starting transfers between devices: none -> 13.4 us  [swap_cores(): return lax.ppermute(x, 'core', [(0, 1), (1, 0)])]
    pallas_call x0 -> x4, Pallas kernels: none -> 11.9 us  [the longest x1 7.78 us: on_device(): call(solve_kernel, 1, (shape(2 * QH, RANK), shape(2 * DH, RANK), shape(16...]
  transfers between devices with their start and end apart: 3 -> 3, of which waited for: 3 -> 3; matrix products, arithmetic and copies ran while one was open for 1% -> 0% of each run, Pallas kernels for 0% -> 0%
where the time goes in v1:
time: 165 us; the launch traced here: 164 us
  blocking collectives  116 us (70%)
  starting transfers between devices  17.8 us (11%)
  Pallas kernels  11.9 us (7%)
  waiting for transfers between devices  10.9 us (7%)
  local copies, waits for them, and re-layouts  6.73 us (4%)
    all_to_all x6, blocking collectives, exchange(): return lax.all_to_all(x, AXES, 0, 0, axis_index_groups=groups, tiled=True)  102 us
    all_to_all x1, blocking collectives, on_device(): lax.all_to_all(jnp.broadcast_to(both[None], (8, PACK + HALF, LANES)), ('c...  13.9 us
    ppermute x2, starting transfers between devices, swap_cores(): return lax.ppermute(x, 'core', [(0, 1), (1, 0)])  13.4 us
    pallas_call x1, Pallas kernels, on_device(): call(solve_kernel, 1, (shape(2 * QH, RANK), shape(2 * DH, RANK), shape(16...  7.78 us
    ppermute x2, waiting for transfers between devices, swap_cores(): return lax.ppermute(x, 'core', [(0, 1), (1, 0)])  6.03 us
    unnamed x20, local copies, waits for them, and re-layouts  5.95 us
    all_to_all x1, waiting for transfers between devices, on_device(): lax.all_to_all(jnp.broadcast_to(qpack[None], (8, 16, LANES)), ('core', 'x...  4.88 us
    all_to_all x1, starting transfers between devices, on_device(): lax.all_to_all(jnp.broadcast_to(qpack[None], (8, 16, LANES)), ('core', 'x...  4.41 us
  transfers between devices with their start and end apart: 3, of which 3 were waited for; matrix products, arithmetic and copies ran while one was open for 0% of the time, Pallas kernels for 0%

profile of v1, /device:TPU:1, one launch (start us, length us, event | category | flops | bytes accessed | tf_op | source)
XLA Modules:
  0.0 164.3 jit_solution(15320292055660329169)
XLA Ops:
  0.6 0.1 pad_add_fusion.core_ref.where_ref
  0.7 1.2 copy-done
  1.9 1.2 copy-done.2
  3.2 1.0 copy-done.4
  4.2 1.0 copy-done.6
  5.2 0.7 copy-done.8
  5.9 0.7 copy-done.9
  6.6 1.3 shard_map.109
  7.9 8.8 %collective-permute-start = (f32[8,8,48,128]{3,2,1,0:T(8,128)S(1)}, f32[8,8,48,128]{3,2,1,0:T(8,128)S(1)}, u32[]{:S(2)}, u32[]{:S(2)}) collective-permute-start(f32[8,8,48,128]{3,2,1,0:T(8,128)S(1)} %get-tuple-element.19), channel_id=1, source_target_pairs={{0,4},{4,0},{1,5},{5,1},{2,6},{6,2},{3,7},{7,3},{8,12},{12,8},{9,1... | collective-permute-start | bytes 4718600 | tf_op jit(solution)/shard_map/ppermute | solution.py:181
  16.7 3.0 %collective-permute-done = f32[8,8,48,128]{3,2,1,0:T(8,128)S(1)} collective-permute-done((f32[8,8,48,128]{3,2,1,0:T(8,128)S(1)}, f32[8,8,48,128]{3,2,1,0:T(8,128)S(1)}, u32[]{:S(2)}, u32[]{:S(2)}) %collective-permute-start) | collective-permute-done | bytes 1572896 | tf_op jit(solution)/shard_map/ppermute | solution.py:181
  19.7 0.2 add.3
  20.0 27.8 %all_to_all.40 = f32[8,8,48,128]{3,2,1,0:T(8,128)S(1)} all-to-all(f32[8,8,48,128]{3,2,1,0:T(8,128)S(1)} %add.3), channel_id=1, replica_groups={{0,8,16,24,32,40,48,56},{64,72,80,88,96,104,112,120},{128,136,144,152,1..., dimensions={0} | all-to-all | bytes 3145728 | tf_op jit(solution)/shard_map/all_to_all | solution.py:40
  47.8 0.6 broadcast_in_dim.12
  48.5 4.4 %all-to-all-start.2 = ((f32[8,16,128]{2,1,0:T(8,128)}), f32[8,16,128]{2,1,0:T(8,128)S(1)}, u32[]{:S(2)}, u32[]{:S(2)}) async-start(f32[8,16,128]{2,1,0:T(8,128)} %broadcast_in_dim.12), calls=%async_computation.2 | async-start | bytes 131072 | tf_op jit(solution)/shard_map/all_to_all | solution.py:192
  52.9 0.1 reduce_sum.27
  53.0 4.9 %all-to-all-done.2 = f32[8,16,128]{2,1,0:T(8,128)S(1)} async-done(((f32[8,16,128]{2,1,0:T(8,128)}), f32[8,16,128]{2,1,0:T(8,128)S(1)}, u32[]{:S(2)}, u32[]{:S(2)}) %all-to-all-start.2) | async-done | bytes 65568 | tf_op jit(solution)/shard_map/all_to_all | solution.py:192
  57.8 15.2 %all_to_all.41.parts = f32[8,48,128]{2,1,0:T(8,128)S(1)} all-to-all(f32[8,48,128]{2,1,0:T(8,128)S(1)} %reduce_sum.27), channel_id=1, replica_groups={{0,64,128,192,256,320,384,448},{8,72,136,200,264,328,392,456},{16,80,14..., dimensions={0} | all-to-all | bytes 393216 | tf_op jit(solution)/shard_map/all_to_all | solution.py:40
  73.1 0.2 shard_map.110
  73.3 10.0 %all_to_all.42 = f32[8,24,128]{2,1,0:T(8,128)S(1)} all-to-all(f32[8,24,128]{2,1,0:T(8,128)S(1)} %get-tuple-element.21), channel_id=1, replica_groups={{0,64,128,192,256,320,384,448},{8,72,136,200,264,328,392,456},{16,80,14..., dimensions={0} | all-to-all | bytes 196608 | tf_op jit(solution)/shard_map/all_to_all | solution.py:40
  83.3 11.8 %all_to_all.43 = f32[8,24,128]{2,1,0:T(8,128)S(1)} all-to-all(f32[8,24,128]{2,1,0:T(8,128)S(1)} %broadcast_in_dim.13), channel_id=1, replica_groups={{0,8,16,24,32,40,48,56},{64,72,80,88,96,104,112,120},{128,136,144,152,1..., dimensions={0} | all-to-all | bytes 196608 | tf_op jit(solution)/shard_map/all_to_all | solution.py:40
  95.1 13.9 %all_to_all.44.all_ref = f32[8,72,128]{2,1,0:T(8,128)S(1)} all-to-all(f32[8,72,128]{2,1,0:T(8,128)S(1)} %broadcast_in_dim.14), channel_id=1, replica_groups=mesh['z'=8,'y'=8,'core'=2,'x'=4] {'core','x'}, dimensions={0} | all-to-all | bytes 589824 | tf_op jit(solution)/shard_map/all_to_all | solution.py:202
  109.0 7.8 %shard_map.111 = (f32[32,64]{1,0:T(8,128)}, f32[64,64]{1,0:T(8,128)}, f32[16,64]{1,0:T(8,128)}, f32[16,64]{1,0:T(8,128)}, f32[8,48,128]{2,1,0:T(8,128)S(1)}) custom-call(s32[2]{0:T(128)S(1)} %pad_add_fusion.core_ref.where_ref, f32[8,72,128]{2,1,0:T(8,128)S(1)} %all_to_all.44.all_ref), custom_call_target="tpu_custom_call" | custom-call | tf_op jit(solution)/shard_map/pallas_call | solution.py:205
  116.8 11.0 %all_to_all.45 = f32[8,48,128]{2,1,0:T(8,128)S(1)} all-to-all(f32[8,48,128]{2,1,0:T(8,128)S(1)} %get-tuple-element.23), channel_id=1, replica_groups={{0,64,128,192,256,320,384,448},{8,72,136,200,264,328,392,456},{16,80,14..., dimensions={0} | all-to-all | bytes 393216 | tf_op jit(solution)/shard_map/all_to_all | solution.py:40
  127.8 0.1 broadcast_in_dim.15
  127.9 0.0 copy-start.1
  127.9 0.0 copy-start.3
  127.9 0.0 copy-start.5
  128.0 0.0 copy-start.7
  128.0 26.1 %all_to_all.46.own = f32[8,8,48,128]{3,2,1,0:T(8,128)S(1)} all-to-all(f32[8,8,48,128]{3,2,1,0:T(8,128)S(1)} %broadcast_in_dim.15), channel_id=1, replica_groups={{0,8,16,24,32,40,48,56},{64,72,80,88,96,104,112,120},{128,136,144,152,1..., dimensions={0} | all-to-all | bytes 3145728 | tf_op jit(solution)/shard_map/all_to_all | solution.py:40
  154.0 4.6 %collective-permute-start.1 = (f32[8,8,48,128]{3,2,1,0:T(8,128)S(1)}, f32[8,8,48,128]{3,2,1,0:T(8,128)S(1)}, u32[]{:S(2)}, u32[]{:S(2)}) collective-permute-start(f32[8,8,48,128]{3,2,1,0:T(8,128)S(1)} %all_to_all.46.own), channel_id=1, source_target_pairs={{0,4},{4,0},{1,5},{5,1},{2,6},{6,2},{3,7},{7,3},{8,12},{12,8},{9,1... | collective-permute-start | bytes 4718600 | tf_op jit(solution)/shard_map/ppermute | solution.py:181
  158.6 3.0 %collective-permute-done.1.other = f32[8,8,48,128]{3,2,1,0:T(8,128)S(1)} collective-permute-done((f32[8,8,48,128]{3,2,1,0:T(8,128)S(1)}, f32[8,8,48,128]{3,2,1,0:T(8,128)S(1)}, u32[]{:S(2)}, u32[]{:S(2)}) %collective-permute-start.1) | collective-permute-done | bytes 1572896 | tf_op jit(solution)/shard_map/ppermute | solution.py:181
  161.7 2.6 %shard_map.112 = (bf16[32,8192]{1,0:T(8,128)(2,1)}, bf16[64,8192]{1,0:T(8,128)(2,1)}) custom-call(s32[2]{0:T(128)S(1)} %pad_add_fusion.core_ref.where_ref, bf16[32,8192]{1,0:T(8,128)(2,1)S(1)} %bitcast.18, bf16[32,8192]{1,0:T(8,128)(2,1)S(1)} %bitcast.20, bf16[64,8192]{1,0:T(8,128)(2,1)S(1)} %bitcast.14, bf16[64,8192]{1,0:T(8,128)(2,1)S(1)} %bitcast.16, ...), custom_call_target="tpu_custom_call" | custom-call | tf_op jit(solution)/shard_map/pallas_call | solution.py:215
  (15 shorter events, 0.1 us)
Async XLA Ops:
  0.7 1.2 copy-start
  1.9 1.2 copy-start.2
  3.2 1.0 copy-start.4
  4.2 1.0 copy-start.6
  5.2 0.7 copy-start.8
  5.9 0.7 copy-start.9
  7.9 11.8 %collective-permute-start = (f32[8,8,48,128]{3,2,1,0:T(8,128)S(1)}, f32[8,8,48,128]{3,2,1,0:T(8,128)S(1)}, u32[]{:S(2)}, u32[]{:S(2)}) collective-permute-start(f32[8,8,48,128]{3,2,1,0:T(8,128)S(1)} %get-tuple-element.19), channel_id=1, source_target_pairs={{0,4},{4,0},{1,5},{5,1},{2,6},{6,2},{3,7},{7,3},{8,12},{12,8},{9,1... | collective-permute-start | bytes 4718600 | tf_op jit(solution)/shard_map/ppermute | solution.py:181
  48.5 9.4 %all-to-all-start.2 = ((f32[8,16,128]{2,1,0:T(8,128)}), f32[8,16,128]{2,1,0:T(8,128)S(1)}, u32[]{:S(2)}, u32[]{:S(2)}) async-start(f32[8,16,128]{2,1,0:T(8,128)} %broadcast_in_dim.12), calls=%async_computation.2 | async-start | bytes 131072 | tf_op jit(solution)/shard_map/all_to_all | solution.py:192
  127.9 33.7 %copy-start.1 = (bf16[1,64,8192]{2,1,0:T(8,128)(2,1)S(1)}, bf16[1,64,8192]{2,1,0:T(8,128)(2,1)}, u32[]{:S(2)}) copy-start(bf16[1,64,8192]{2,1,0:T(8,128)(2,1)} %param.9) | copy-start | bytes 3145732
  127.9 33.7 %copy-start.3 = (bf16[1,64,8192]{2,1,0:T(8,128)(2,1)S(1)}, bf16[1,64,8192]{2,1,0:T(8,128)(2,1)}, u32[]{:S(2)}) copy-start(bf16[1,64,8192]{2,1,0:T(8,128)(2,1)} %param.10) | copy-start | bytes 3145732
  127.9 33.7 %copy-start.5 = (bf16[1,32,8192]{2,1,0:T(8,128)(2,1)S(1)}, bf16[1,32,8192]{2,1,0:T(8,128)(2,1)}, u32[]{:S(2)}) copy-start(bf16[1,32,8192]{2,1,0:T(8,128)(2,1)} %param.6) | copy-start | bytes 1572868
  128.0 33.7 %copy-start.7 = (bf16[1,32,8192]{2,1,0:T(8,128)(2,1)S(1)}, bf16[1,32,8192]{2,1,0:T(8,128)(2,1)}, u32[]{:S(2)}) copy-start(bf16[1,32,8192]{2,1,0:T(8,128)(2,1)} %param.7) | copy-start | bytes 1572868
  154.0 7.6 %collective-permute-start.1 = (f32[8,8,48,128]{3,2,1,0:T(8,128)S(1)}, f32[8,8,48,128]{3,2,1,0:T(8,128)S(1)}, u32[]{:S(2)}, u32[]{:S(2)}) collective-permute-start(f32[8,8,48,128]{3,2,1,0:T(8,128)S(1)} %all_to_all.46.own), channel_id=1, source_target_pairs={{0,4},{4,0},{1,5},{5,1},{2,6},{6,2},{3,7},{7,3},{8,12},{12,8},{9,1... | collective-permute-start | bytes 4718600 | tf_op jit(solution)/shard_map/ppermute | solution.py:181

commit v2 on v1

--- a/solution.py
+++ b/solution.py
@@ -13,7 +13,12 @@
 HALF = QH + DH
 PACK = HALF // 2
 HIGH = lax.Precision.HIGHEST
-PARAMS = pltpu.CompilerParams(vmem_limit_bytes=40 * 1024 * 1024)
+WIDTH = 8192
+CHUNK = 2048
+CHUNKS = WIDTH // CHUNK
+QPAD = 256
+MIB = 1024 * 1024
+SEND_VMEM, KEEP_VMEM, FACTOR_VMEM = 62, 59, 63.25
 
 
 def device_of(z, y, core, x):
@@ -40,31 +45,62 @@
     return lax.all_to_all(x, AXES, 0, 0, axis_index_groups=groups, tiled=True)
 
 
-def column_of(core, i, j):
-    block = jnp.where(core == 0, j * NY + i, i * NY + j)
-    return pl.multiple_of(block * LANES, LANES)
-
-
-def merge_kernel(core_ref, gq, eq, gd, ed, qq, qd, send, keep, qpack):
-    core = core_ref[0]
+def slot(owner, block):
+    z, y = divmod(block, NY)
+    return jnp.where(owner == 0, y, z), jnp.where(owner == 0, z, y)
+
+
+def merge_half(owner, sources, bufs, sems, out):
     f32 = jnp.float32
-    for out, owner in ((send, 1 - core), (keep, core)):
-        rq = pl.ds(pl.multiple_of(owner * QH, QH), QH)
-        rd = pl.ds(pl.multiple_of(owner * DH, DH), DH)
-        for i in range(8):
-            for j in range(8):
-                cols = pl.ds(column_of(owner, i, j), LANES)
-                out[i, j, 0:QH, :] = gq[rq, cols].astype(f32) + eq[rq, cols].astype(f32)
-                out[i, j, QH:HALF, :] = gd[rd, cols].astype(f32) + ed[rd, cols].astype(f32)
-    qpack[...] = jnp.concatenate([qq[...], qd[...]], axis=1)
-
-
-def factor_kernel(parts, qpack, s_ref, f_ref):
+    copies = []
+    for ch in range(CHUNKS):
+        cols = pl.ds(ch * CHUNK, CHUNK)
+        part = []
+        for a, (src, buf) in enumerate(zip(sources, bufs)):
+            n = buf.shape[0]
+            rows = pl.ds(pl.multiple_of(owner * n, n), n)
+            part.append(pltpu.make_async_copy(src.at[rows, cols], buf.at[:, cols], sems.at[ch, a]))
+        copies.append(part)
+        for c in part:
+            c.start()
+    gq, eq, gd, ed = bufs
+    per = CHUNK // LANES
+    for ch in range(CHUNKS):
+        for c in copies[ch]:
+            c.wait()
+        for block in range(ch * per, (ch + 1) * per):
+            i, j = slot(owner, block)
+            cols = pl.ds(block * LANES, LANES)
+            out[i, j, 0:QH, :] = gq[:, cols].astype(f32) + eq[:, cols].astype(f32)
+            out[i, j, QH:HALF, :] = gd[:, cols].astype(f32) + ed[:, cols].astype(f32)
+
+
+def send_kernel(core_ref, gq, eq, gd, ed, out, bq, cq, bd, cd, sems):
+    merge_half(1 - core_ref[0], (gq, eq, gd, ed), (bq, cq, bd, cd), sems, out)
+
+
+def keep_kernel(core_ref, gq, eq, gd, ed, qq, qd, out, qpack, bq, cq, bd, cd, sems, qbuf, qsems):
+    q_copies = [pltpu.make_async_copy(r, qbuf.at[k], qsems.at[k]) for k, r in enumerate((qq, qd))]
+    for c in q_copies:
+        c.start()
+    qpack[16:QPAD, :] = jnp.zeros((QPAD - 16, LANES), jnp.float32)
+    for c in q_copies:
+        c.wait()
+    qpack[0:16, :] = jnp.concatenate([qbuf[0], qbuf[1]], axis=1)
+    merge_half(core_ref[0], (gq, eq, gd, ed), (bq, cq, bd, cd), sems, out)
+
+
+def factor_kernel(parts, q_all, s_ref, f_ref, qbuf, qsems):
+    copies = [pltpu.make_async_copy(q_all.at[g, 0:16], qbuf.at[g], qsems.at[g]) for g in range(8)]
+    for c in copies:
+        c.start()
     s = parts[0]
     for i in range(1, 8):
         s = s + parts[i]
     s_ref[...] = s
-    r = jnp.dot(s, qpack[...], precision=HIGH, preferred_element_type=jnp.float32)
+    for c in copies:
+        c.wait()
+    r = jnp.dot(s, qbuf[...].reshape(LANES, LANES), precision=HIGH, preferred_element_type=jnp.float32)
     low = jnp.concatenate([r[0:QH], pltpu.roll(r[40:48], RANK, 1)], axis=0)
     lane = lax.broadcasted_iota(jnp.int32, (PACK, LANES), 1)
     packed = jnp.where(lane < RANK, low, r[QH:40])
@@ -90,18 +126,36 @@
         eye_d = jnp.where(lane == row + 8 * b, 1.0, 0.0)
         q.append(jnp.where(lane < RANK, gram[8 * b:8 * b + 8], eye_q))
         d.append(jnp.where(lane >= RANK, gram[RANK + 8 * b:RANK + 8 * b + 8], eye_d))
-    for k in range(RANK):
-        b0, s = divmod(k, 8)
-        for m, at in ((q, k), (d, RANK + k)):
-            inv = lax.rsqrt(m[b0][s:s + 1, at:at + 1])
-            top = m[b0][s:s + 1, :] * inv
-            for b in range(b0, nb):
-                col = m[b][:, at:at + 1] * inv
-                if b == b0:
-                    col = jnp.where(row > s, col, 0.0)
-                    m[b] = jnp.where(row == s, top, m[b] - col * top)
-                else:
-                    m[b] = m[b] - col * top
+
+    def spread_row(v, s):
+        return jnp.broadcast_to(v[s:s + 1, :], (8, LANES))
+
+    def spread_lane(v, at):
+        return jnp.broadcast_to(v[:, at:at + 1], (8, LANES))
+
+    for b in range(nb):
+        for m, base in ((q, 0), (d, RANK)):
+            at = base + 8 * b
+            top = m[b]
+            col = [spread_lane(top, at + t) for t in range(8)]
+            below = [(i, [spread_lane(m[i], at + t) for t in range(8)]) for i in range(b + 1, nb)]
+            pivots = jnp.ones((8, LANES), jnp.float32)
+            for s in range(8):
+                p = spread_row(col[s], s)
+                pivots = jnp.where(row == s, p, pivots)
+                r = 1.0 / p
+                pivot_row = spread_row(top, s)
+                upper = {t: spread_row(col[t], s) for t in range(s + 1, 8)}
+                f = jnp.where(row > s, col[s] * r, 0.0)
+                top = top - f * pivot_row
+                for t in upper:
+                    col[t] = col[t] - f * upper[t]
+                for i, c in below:
+                    g = c[s] * r
+                    m[i] = m[i] - g * pivot_row
+                    for t in upper:
+                        c[t] = c[t] - g * upper[t]
+            m[b] = top * lax.rsqrt(pivots)
     zero = jnp.zeros((8, LANES), jnp.float32)
     out = [jnp.where(lane < RANK, pltpu.roll(m, RANK, 1), zero) for m in q]
     out += [jnp.where(lane >= RANK, pltpu.roll(m, RANK, 1), zero) for m in d]
@@ -145,35 +199,56 @@
         approx[i] = a
 
 
-def error_kernel(core_ref, gq, eq, gd, ed, own, other, out_q, out_d):
-    core = core_ref[0]
+def error_half(owner, gq, eq, gd, ed, src, out_q, out_d, buf_q, buf_d, sems):
     f32 = jnp.float32
-    for src, owner in ((own, core), (other, 1 - core)):
-        rq = pl.ds(pl.multiple_of(owner * QH, QH), QH)
-        rd = pl.ds(pl.multiple_of(owner * DH, DH), DH)
-        for i in range(8):
-            for j in range(8):
-                cols = pl.ds(column_of(owner, i, j), LANES)
-                mq = gq[rq, cols].astype(f32) + eq[rq, cols].astype(f32)
-                md = gd[rd, cols].astype(f32) + ed[rd, cols].astype(f32)
-                out_q[rq, cols] = (mq - src[i, j, 0:QH, :]).astype(jnp.bfloat16)
-                out_d[rd, cols] = (md - src[i, j, QH:HALF, :]).astype(jnp.bfloat16)
+    rq = pl.ds(pl.multiple_of(owner * QH, QH), QH)
+    rd = pl.ds(pl.multiple_of(owner * DH, DH), DH)
+    per = CHUNK // LANES
+    copies = []
+    for ch in range(CHUNKS):
+        for block in range(ch * per, (ch + 1) * per):
+            i, j = slot(owner, block)
+            cols = pl.ds(block * LANES, LANES)
+            mq = gq[rq, cols].astype(f32) + eq[rq, cols].astype(f32)
+            md = gd[rd, cols].astype(f32) + ed[rd, cols].astype(f32)
+            buf_q[:, cols] = (mq - src[i, j, 0:QH, :]).astype(jnp.bfloat16)
+            buf_d[:, cols] = (md - src[i, j, QH:HALF, :]).astype(jnp.bfloat16)
+        cols = pl.ds(ch * CHUNK, CHUNK)
+        for a, (buf, out, rows) in enumerate(((buf_q, out_q, rq), (buf_d, out_d, rd))):
+            c = pltpu.make_async_copy(buf.at[:, cols], out.at[rows, cols], sems.at[ch, a])
+            c.start()
+            copies.append(c)
+    for c in copies:
+        c.wait()
+
+
+def own_error_kernel(core_ref, gq, eq, gd, ed, src, out_q, out_d, buf_q, buf_d, sems):
+    error_half(core_ref[0], gq, eq, gd, ed, src, out_q, out_d, buf_q, buf_d, sems)
+
+
+def other_error_kernel(core_ref, gq, eq, gd, ed, src, in_q, in_d, out_q, out_d, buf_q, buf_d, sems):
+    error_half(1 - core_ref[0], gq, eq, gd, ed, src, out_q, out_d, buf_q, buf_d, sems)
 
 
 def shape(*dims, dtype=jnp.float32):
     return jax.ShapeDtypeStruct(dims, dtype)
 
 
-def call(kernel, n_in, out_shape, scalars=0, scratch=()):
-    vmem = pl.BlockSpec(memory_space=pltpu.VMEM)
-    smem = pl.BlockSpec(memory_space=pltpu.SMEM)
+VM = pl.BlockSpec(memory_space=pltpu.VMEM)
+SM = pl.BlockSpec(memory_space=pltpu.SMEM)
+HB = pl.BlockSpec(memory_space=pltpu.HBM)
+
+
+def call(kernel, in_specs, out_shape, out_specs, scratch=(), moved=0, aliases=None, vmem=24):
     return pl.pallas_call(
         kernel,
         out_shape=out_shape,
-        in_specs=[smem] * scalars + [vmem] * n_in,
-        out_specs=jax.tree.map(lambda _: vmem, out_shape),
+        in_specs=in_specs,
+        out_specs=out_specs,
         scratch_shapes=list(scratch),
-        compiler_params=PARAMS,
+        input_output_aliases=aliases or {},
+        cost_estimate=pl.CostEstimate(flops=moved, bytes_accessed=moved, transcendentals=0),
+        compiler_params=pltpu.CompilerParams(vmem_limit_bytes=int(vmem * MIB)),
     )
 
 
@@ -185,16 +260,33 @@
     core = lax.axis_index("core").astype(jnp.int32)
     place = jnp.stack([core, lax.axis_index("x").astype(jnp.int32)])
     half = shape(8, 8, HALF, LANES)
+    bf16 = jnp.bfloat16
+    dma = pltpu.SemaphoreType.DMA
+    half_bufs = [pltpu.VMEM((n, WIDTH), bf16) for n in (QH, QH, DH, DH)] + [dma((CHUNKS, 4))]
     grads = (grad_query[0], error_query[0], grad_down[0], error_down[0])
-    send, keep, qpack = call(merge_kernel, 6, (half, half, shape(16, LANES)), 1)(
-        place, *grads, q_query.T, q_down.T
-    )
-    q_all = lax.all_to_all(
-        jnp.broadcast_to(qpack[None], (8, 16, LANES)), ("core", "x"), 0, 0, tiled=True
-    ).reshape(LANES, LANES)
-    part = exchange(keep + swap_cores(send), WIDE)
+    send = call(send_kernel, [SM] + [HB] * 4, half, VM, half_bufs, 3 << 20, vmem=SEND_VMEM)(place, *grads)
+    other = swap_cores(send)
+    keep, qpack = call(
+        keep_kernel,
+        [SM] + [HB] * 6,
+        (half, shape(QPAD, LANES)),
+        (VM, VM),
+        half_bufs + [pltpu.VMEM((2, 16, RANK), jnp.float32), dma((2,))],
+        3 << 20,
+        vmem=KEEP_VMEM,
+    )(place, *grads, q_query.T, q_down.T)
+    q_all = lax.all_gather(qpack[None], ("core", "x"), axis=0, tiled=True)
+    part = exchange(keep + other, WIDE)
     part = exchange(jnp.sum(part, axis=0), NARROW)
-    s_own, f = call(factor_kernel, 2, (shape(HALF, LANES), shape(8, PACK, LANES)))(part, q_all)
+    s_own, f = call(
+        factor_kernel,
+        [VM, HB],
+        (shape(HALF, LANES), shape(8, PACK, LANES)),
+        (VM, VM),
+        [pltpu.VMEM((8, 16, LANES), jnp.float32), dma((8,))],
+        1 << 18,
+        vmem=FACTOR_VMEM,
+    )(part, q_all)
     f = exchange(f, NARROW)
     f = jnp.broadcast_to(jnp.sum(f, axis=0)[None], (8, PACK, LANES))
     f = jnp.sum(exchange(f, WIDE), axis=0)
@@ -204,17 +296,21 @@
     )
     basis_q, basis_d, qn_q, qn_d, approx = call(
         solve_kernel,
-        1,
+        [SM, VM],
         (shape(2 * QH, RANK), shape(2 * DH, RANK), shape(16, RANK), shape(16, RANK), shape(8, HALF, LANES)),
-        1,
+        (VM,) * 5,
         [pltpu.VMEM((2, LANES, LANES), jnp.float32)],
+        1 << 20,
     )(place, both)
     approx = exchange(approx, NARROW)
     own = exchange(jnp.broadcast_to(approx[None], (8, 8, HALF, LANES)), WIDE)
     other = swap_cores(own)
+    errors = (shape(2 * QH, WIDTH, dtype=bf16), shape(2 * DH, WIDTH, dtype=bf16))
+    bufs = [pltpu.VMEM((n, WIDTH), bf16) for n in (QH, DH)] + [dma((CHUNKS, 2))]
+    first = call(own_error_kernel, [SM] + [VM] * 5, errors, (HB, HB), bufs, 4 << 20)(place, *grads, own)
     err_q, err_d = call(
-        error_kernel, 6, (shape(2 * QH, 8192, dtype=jnp.bfloat16), shape(2 * DH, 8192, dtype=jnp.bfloat16)), 1
-    )(place, *grads, own, other)
+        other_error_kernel, [SM] + [VM] * 5 + [HB] * 2, errors, (HB, HB), bufs, 4 << 20, {6: 0, 7: 1}
+    )(place, *grads, other, *first)
     return (err_q[None], basis_q, qn_q.T, err_d[None], basis_d, qn_d.T)
 
 

time: 165 us -> 171 us (1.036)
  blocking collectives: 116 us -> 74.5 us
  waiting for transfers between devices: 10.9 us -> 33.4 us
  between operations: 0.75 us -> 14.2 us
  starting transfers between devices: 17.8 us -> 24.9 us
  Pallas kernels: 11.9 us -> 17.9 us
  local copies, waits for them, and re-layouts: 6.73 us -> 0.86 us
  other arithmetic: 0.44 us -> 4.86 us
    all_to_all x6 -> x4, blocking collectives: 102 us -> 59.8 us  [exchange(): return lax.all_to_all(x, AXES, 0, 0, axis_index_groups=groups, tiled=True)]
    all_to_all x1 -> x2, waiting for transfers between devices: 4.88 us -> 28.3 us  [exchange(): return lax.all_to_all(x, AXES, 0, 0, axis_index_groups=groups, tiled=True)]
    all_to_all x1 -> x2, starting transfers between devices: 4.41 us -> 11.5 us  [exchange(): return lax.all_to_all(x, AXES, 0, 0, axis_index_groups=groups, tiled=True)]
    pallas_call x4 -> x6, Pallas kernels: 11.9 us -> 17.9 us  [the longest x1 4.44 us: on_device(): call(solve_kernel, [SM, VM], (shape(2 * QH, RANK), shape(2 * DH, RANK), s...]
    unnamed x20 -> x12, local copies, waits for them, and re-layouts: 5.95 us -> 0.71 us
    ppermute x2, waiting for transfers between devices: 6.03 us -> 1.42 us  [swap_cores(): return lax.ppermute(x, 'core', [(0, 1), (1, 0)])]
    all_gather x0 -> x1, waiting for transfers between devices: none -> 3.01 us  [on_device(): q_all = lax.all_gather(qpack[None], ('core', 'x'), axis=0, tiled=True)]
    add x1, other arithmetic: 0.25 us -> 2.75 us  [on_device(): part = exchange(keep + other, WIDE)]
  transfers between devices with their start and end apart: 3 -> 5, of which waited for: 3 -> 4; matrix products, arithmetic and copies ran while one was open for 0% -> 0% of each run, Pallas kernels for 0% -> 3%
where the time goes in v2:
time: 171 us
  blocking collectives  74.5 us (44%)
  waiting for transfers between devices  33.4 us (20%)
  starting transfers between devices  24.9 us (15%)
  Pallas kernels  17.9 us (10%)
  between operations  14.2 us (8%)
  other arithmetic  4.86 us (3%)
    all_to_all x4, blocking collectives, exchange(): return lax.all_to_all(x, AXES, 0, 0, axis_index_groups=groups, tiled=True)  59.8 us
    all_to_all x2, waiting for transfers between devices, exchange(): return lax.all_to_all(x, AXES, 0, 0, axis_index_groups=groups, tiled=True)  28.3 us
    all_to_all x1, blocking collectives, on_device(): lax.all_to_all(jnp.broadcast_to(both[None], (8, PACK + HALF, LANES)), ('c...  14.7 us
    ppermute x2, starting transfers between devices, swap_cores(): return lax.ppermute(x, 'core', [(0, 1), (1, 0)])  13.4 us
    all_to_all x2, starting transfers between devices, exchange(): return lax.all_to_all(x, AXES, 0, 0, axis_index_groups=groups, tiled=True)  11.5 us
    pallas_call x1, Pallas kernels, on_device(): call(solve_kernel, [SM, VM], (shape(2 * QH, RANK), shape(2 * DH, RANK), s...  4.44 us
    pallas_call x1, Pallas kernels, on_device(): call(keep_kernel, [SM] + [HB] * 6, (half, shape(QPAD, LANES)), (VM, VM),...  4.2 us
    pallas_call x1, Pallas kernels, on_device(): call(send_kernel, [SM] + [HB] * 4, half, VM, half_bufs, 3 << 20, vmem=SEN...  3.45 us
  transfers between devices with their start and end apart: 5, of which 4 were waited for; matrix products, arithmetic and copies ran while one was open for 0% of the time, Pallas kernels for 3%

profile of v2, /device:TPU:1, one launch (start us, length us, event | category | flops | bytes accessed | tf_op | source)
XLA Modules:
  0.0 170.6 jit_solution(12124613753053949934)
XLA Ops:
  7.2 0.6 pad_add_fusion.core_ref.where_ref
  7.8 3.5 %shard_map.110 = f32[8,8,48,128]{3,2,1,0:T(8,128)} custom-call(s32[2]{0:T(128)} %pad_add_fusion.core_ref.where_ref, bf16[32,8192]{1,0:T(8,128)(2,1)} %bitcast.21, bf16[32,8192]{1,0:T(8,128)(2,1)} %bitcast.25, bf16[64,8192]{1,0:T(8,128)(2,1)} %bitcast.13, bf16[64,8192]{1,0:T(8,128)(2,1)} %bitcast.17), custom_call_target="tpu_custom_call" | custom-call | flops 3145728 | bytes 3145728 | tf_op jit(solution)/shard_map/pallas_call | solution.py:267
  11.2 8.8 %collective-permute-start = (f32[8,8,48,128]{3,2,1,0:T(8,128)}, f32[8,8,48,128]{3,2,1,0:T(8,128)S(1)}, u32[]{:S(2)}, u32[]{:S(2)}) collective-permute-start(f32[8,8,48,128]{3,2,1,0:T(8,128)} %shard_map.110), channel_id=1, source_target_pairs={{0,4},{4,0},{1,5},{5,1},{2,6},{6,2},{3,7},{7,3},{8,12},{12,8},{9,1... | collective-permute-start | bytes 4718600 | tf_op jit(solution)/shard_map/ppermute | solution.py:256
  20.0 4.2 %shard_map.109 = (f32[8,8,48,128]{3,2,1,0:T(8,128)}, f32[256,128]{1,0:T(8,128)}) custom-call(s32[2]{0:T(128)} %pad_add_fusion.core_ref.where_ref, bf16[32,8192]{1,0:T(8,128)(2,1)} %bitcast.22, bf16[32,8192]{1,0:T(8,128)(2,1)} %bitcast.26, bf16[64,8192]{1,0:T(8,128)(2,1)} %bitcast.14, bf16[64,8192]{1,0:T(8,128)(2,1)} %bitcast.18, f32[16,64]{1,0:T(8,128)} %bitcast.32, ...), custom_call_target="tpu_custom_call" | custom-call | flops 3145728 | bytes 3145728 | tf_op jit(solution)/shard_map/pallas_call | solution.py:269
  24.2 0.0 collective-permute-done
  24.2 2.7 %add.3 = f32[8,8,48,128]{3,2,1,0:T(8,128)} add(f32[8,8,48,128]{3,2,1,0:T(8,128)} %get-tuple-element.19, f32[8,8,48,128]{3,2,1,0:T(8,128)S(1)} %collective-permute-done) | non-fusion elementwise | flops 393216 | bytes 4718592 | tf_op jit(solution)/shard_map/add | solution.py:279
  27.0 4.7 %all-to-all-start = ((f32[8,8,48,128]{3,2,1,0:T(8,128)}), f32[8,8,48,128]{3,2,1,0:T(8,128)S(1)}, u32[]{:S(2)}, u32[]{:S(2)}) async-start(f32[8,8,48,128]{3,2,1,0:T(8,128)} %add.3), calls=%async_computation | async-start | bytes 3145728 | tf_op jit(solution)/shard_map/all_to_all | solution.py:45
  31.6 0.0 all-gather.3.cloned.1.call-start
  31.7 0.7 all-gather.3.cloned.1.call-update
  32.4 22.7 %all-to-all-done = f32[8,8,48,128]{3,2,1,0:T(8,128)S(1)} async-done(((f32[8,8,48,128]{3,2,1,0:T(8,128)}), f32[8,8,48,128]{3,2,1,0:T(8,128)S(1)}, u32[]{:S(2)}, u32[]{:S(2)}) %all-to-all-start) | async-done | bytes 1572896 | tf_op jit(solution)/shard_map/all_to_all | solution.py:45
  55.1 0.8 reduce_sum.27
  55.8 6.8 %all-to-all-start.1 = ((f32[8,48,128]{2,1,0:T(8,128)}), f32[8,48,128]{2,1,0:T(8,128)S(1)}, u32[]{:S(2)}, u32[]{:S(2)}) async-start(f32[8,48,128]{2,1,0:T(8,128)} %reduce_sum.27), calls=%async_computation.1 | async-start | bytes 393216 | tf_op jit(solution)/shard_map/all_to_all | solution.py:45
  62.7 3.0 %all-gather.3.cloned.1.call-done = f32[2048,128]{1,0:T(8,128)} async-done(((f32[256,128]{1,0:T(8,128)}), f32[2048,128]{1,0:T(8,128)}) %all-gather.3.cloned.1.call-update) | async-done | bytes 1048592 | tf_op jit(solution)/shard_map/all_gather | solution.py:278
  65.7 5.6 %all-to-all-done.1.parts = f32[8,48,128]{2,1,0:T(8,128)S(1)} async-done(((f32[8,48,128]{2,1,0:T(8,128)}), f32[8,48,128]{2,1,0:T(8,128)S(1)}, u32[]{:S(2)}, u32[]{:S(2)}) %all-to-all-start.1) | async-done | bytes 196640 | tf_op jit(solution)/shard_map/all_to_all | solution.py:45
  71.3 0.7 copy-done.5
  72.0 2.7 %shard_map.111 = (f32[48,128]{1,0:T(8,128)}, f32[8,24,128]{2,1,0:T(8,128)}) custom-call(f32[8,48,128]{2,1,0:T(8,128)} %copy-done.5, f32[8,256,128]{2,1,0:T(8,128)} %bitcast.30), custom_call_target="tpu_custom_call" | custom-call | flops 262144 | bytes 262144 | tf_op jit(solution)/shard_map/pallas_call | solution.py:281
  74.7 10.8 %all_to_all.35 = f32[8,24,128]{2,1,0:T(8,128)S(1)} all-to-all(f32[8,24,128]{2,1,0:T(8,128)} %get-tuple-element.21), channel_id=1, replica_groups={{0,64,128,192,256,320,384,448},{8,72,136,200,264,328,392,456},{16,80,14..., dimensions={0} | all-to-all | bytes 196608 | tf_op jit(solution)/shard_map/all_to_all | solution.py:45
  85.5 11.9 %all_to_all.36 = f32[8,24,128]{2,1,0:T(8,128)S(1)} all-to-all(f32[8,24,128]{2,1,0:T(8,128)S(1)} %broadcast_in_dim.13), channel_id=1, replica_groups={{0,8,16,24,32,40,48,56},{64,72,80,88,96,104,112,120},{128,136,144,152,1..., dimensions={0} | all-to-all | bytes 196608 | tf_op jit(solution)/shard_map/all_to_all | solution.py:45
  97.4 0.7 pad_maximum_fusion
  98.2 14.7 %all_to_all.37.all_ref = f32[8,72,128]{2,1,0:T(8,128)S(1)} all-to-all(f32[8,72,128]{2,1,0:T(8,128)S(1)} %broadcast_in_dim.14), channel_id=1, replica_groups=mesh['z'=8,'y'=8,'core'=2,'x'=4] {'core','x'}, dimensions={0} | all-to-all | bytes 589824 | tf_op jit(solution)/shard_map/all_to_all | solution.py:294
  112.9 4.4 %shard_map.112 = (f32[32,64]{1,0:T(8,128)}, f32[64,64]{1,0:T(8,128)}, f32[16,64]{1,0:T(8,128)}, f32[16,64]{1,0:T(8,128)}, f32[8,48,128]{2,1,0:T(8,128)S(1)}) custom-call(s32[2]{0:T(128)S(1)} %copy-done.4, f32[8,72,128]{2,1,0:T(8,128)S(1)} %all_to_all.37.all_ref), custom_call_target="tpu_custom_call" | custom-call | flops 1048576 | bytes 1048576 | tf_op jit(solution)/shard_map/pallas_call | solution.py:297
  117.3 11.0 %all_to_all.38 = f32[8,48,128]{2,1,0:T(8,128)S(1)} all-to-all(f32[8,48,128]{2,1,0:T(8,128)S(1)} %get-tuple-element.23), channel_id=1, replica_groups={{0,64,128,192,256,320,384,448},{8,72,136,200,264,328,392,456},{16,80,14..., dimensions={0} | all-to-all | bytes 393216 | tf_op jit(solution)/shard_map/all_to_all | solution.py:45
  128.3 0.1 broadcast_in_dim.30
  128.5 0.0 copy-start
  128.5 0.0 copy-start.1
  128.5 0.0 copy-start.2
  128.5 0.0 copy-start.3
  128.5 26.1 %all_to_all.39.src = f32[8,8,48,128]{3,2,1,0:T(8,128)S(1)} all-to-all(f32[8,8,48,128]{3,2,1,0:T(8,128)S(1)} %broadcast_in_dim.30), channel_id=1, replica_groups={{0,8,16,24,32,40,48,56},{64,72,80,88,96,104,112,120},{128,136,144,152,1..., dimensions={0} | all-to-all | bytes 3145728 | tf_op jit(solution)/shard_map/all_to_all | solution.py:45
  154.6 4.6 %collective-permute-start.1 = (f32[8,8,48,128]{3,2,1,0:T(8,128)S(1)}, f32[8,8,48,128]{3,2,1,0:T(8,128)S(1)}, u32[]{:S(2)}, u32[]{:S(2)}) collective-permute-start(f32[8,8,48,128]{3,2,1,0:T(8,128)S(1)} %all_to_all.39.src), channel_id=1, source_target_pairs={{0,4},{4,0},{1,5},{5,1},{2,6},{6,2},{3,7},{7,3},{8,12},{12,8},{9,1... | collective-permute-start | bytes 4718600 | tf_op jit(solution)/shard_map/ppermute | solution.py:256
  159.2 1.6 shard_map.113
  160.8 1.4 collective-permute-done.1.src
  162.2 1.5 shard_map.114
  (11 shorter events, 0.1 us)
Async XLA Ops:
  11.2 13.0 %collective-permute-start = (f32[8,8,48,128]{3,2,1,0:T(8,128)}, f32[8,8,48,128]{3,2,1,0:T(8,128)S(1)}, u32[]{:S(2)}, u32[]{:S(2)}) collective-permute-start(f32[8,8,48,128]{3,2,1,0:T(8,128)} %shard_map.110), channel_id=1, source_target_pairs={{0,4},{4,0},{1,5},{5,1},{2,6},{6,2},{3,7},{7,3},{8,12},{12,8},{9,1... | collective-permute-start | bytes 4718600 | tf_op jit(solution)/shard_map/ppermute | solution.py:256
  27.0 28.1 %all-to-all-start = ((f32[8,8,48,128]{3,2,1,0:T(8,128)}), f32[8,8,48,128]{3,2,1,0:T(8,128)S(1)}, u32[]{:S(2)}, u32[]{:S(2)}) async-start(f32[8,8,48,128]{3,2,1,0:T(8,128)} %add.3), calls=%async_computation | async-start | bytes 3145728 | tf_op jit(solution)/shard_map/all_to_all | solution.py:45
  31.6 34.0 %all-gather.3.cloned.1.call-start = ((), (), s32[]{:S(2)}) async-start(), calls=%async_computation.7 | async-start | bytes 1179648 | tf_op jit(solution)/shard_map/all_gather | solution.py:278
  55.8 15.5 %all-to-all-start.1 = ((f32[8,48,128]{2,1,0:T(8,128)}), f32[8,48,128]{2,1,0:T(8,128)S(1)}, u32[]{:S(2)}, u32[]{:S(2)}) async-start(f32[8,48,128]{2,1,0:T(8,128)} %reduce_sum.27), calls=%async_computation.1 | async-start | bytes 393216 | tf_op jit(solution)/shard_map/all_to_all | solution.py:45
  62.7 50.2 %copy-start.4 = (s32[2]{0:T(128)S(1)}, s32[2]{0:T(128)}, u32[]{:S(2)}) copy-start(s32[2]{0:T(128)} %pad_add_fusion.core_ref.where_ref) | copy-start | bytes 28
  71.3 0.7 copy-start.5
  128.5 30.7 %copy-start = (bf16[1,64,8192]{2,1,0:T(8,128)(2,1)S(1)}, bf16[1,64,8192]{2,1,0:T(8,128)(2,1)}, u32[]{:S(2)}) copy-start(bf16[1,64,8192]{2,1,0:T(8,128)(2,1)} %param.9) | copy-start | bytes 3145732
  128.5 30.7 %copy-start.1 = (bf16[1,64,8192]{2,1,0:T(8,128)(2,1)S(1)}, bf16[1,64,8192]{2,1,0:T(8,128)(2,1)}, u32[]{:S(2)}) copy-start(bf16[1,64,8192]{2,1,0:T(8,128)(2,1)} %param.10) | copy-start | bytes 3145732
  128.5 30.7 %copy-start.2 = (bf16[1,32,8192]{2,1,0:T(8,128)(2,1)S(1)}, bf16[1,32,8192]{2,1,0:T(8,128)(2,1)}, u32[]{:S(2)}) copy-start(bf16[1,32,8192]{2,1,0:T(8,128)(2,1)} %param.6) | copy-start | bytes 1572868
  128.5 30.7 %copy-start.3 = (bf16[1,32,8192]{2,1,0:T(8,128)(2,1)S(1)}, bf16[1,32,8192]{2,1,0:T(8,128)(2,1)}, u32[]{:S(2)}) copy-start(bf16[1,32,8192]{2,1,0:T(8,128)(2,1)} %param.7) | copy-start | bytes 1572868
  154.6 7.6 %collective-permute-start.1 = (f32[8,8,48,128]{3,2,1,0:T(8,128)S(1)}, f32[8,8,48,128]{3,2,1,0:T(8,128)S(1)}, u32[]{:S(2)}, u32[]{:S(2)}) collective-permute-start(f32[8,8,48,128]{3,2,1,0:T(8,128)S(1)} %all_to_all.39.src), channel_id=1, source_target_pairs={{0,4},{4,0},{1,5},{5,1},{2,6},{6,2},{3,7},{7,3},{8,12},{12,8},{9,1... | collective-permute-start | bytes 4718600 | tf_op jit(solution)/shard_map/ppermute | solution.py:256
Sparse Core Ops, SparseCore 0:
  35.2 30.4 all-gather.2

commit v3 on v2

--- a/solution.py
+++ b/solution.py
@@ -16,9 +16,7 @@
 WIDTH = 8192
 CHUNK = 2048
 CHUNKS = WIDTH // CHUNK
-QPAD = 256
 MIB = 1024 * 1024
-SEND_VMEM, KEEP_VMEM, FACTOR_VMEM = 62, 59, 63.25
 
 
 def device_of(z, y, core, x):
@@ -50,57 +48,40 @@
     return jnp.where(owner == 0, y, z), jnp.where(owner == 0, z, y)
 
 
-def merge_half(owner, sources, bufs, sems, out):
+def merge_kernel(gq, eq, gd, ed, send, keep, bq, cq, bd, cd, sems):
     f32 = jnp.float32
     copies = []
     for ch in range(CHUNKS):
         cols = pl.ds(ch * CHUNK, CHUNK)
-        part = []
-        for a, (src, buf) in enumerate(zip(sources, bufs)):
-            n = buf.shape[0]
-            rows = pl.ds(pl.multiple_of(owner * n, n), n)
-            part.append(pltpu.make_async_copy(src.at[rows, cols], buf.at[:, cols], sems.at[ch, a]))
-        copies.append(part)
-        for c in part:
+        pairs = ((gq, bq), (eq, cq), (gd, bd), (ed, cd))
+        copies.append([
+            pltpu.make_async_copy(src.at[:, cols], buf.at[:, cols], sems.at[ch, a])
+            for a, (src, buf) in enumerate(pairs)
+        ])
+        for c in copies[-1]:
             c.start()
-    gq, eq, gd, ed = bufs
+    core = lax.axis_index("core")
     per = CHUNK // LANES
     for ch in range(CHUNKS):
         for c in copies[ch]:
             c.wait()
-        for block in range(ch * per, (ch + 1) * per):
-            i, j = slot(owner, block)
-            cols = pl.ds(block * LANES, LANES)
-            out[i, j, 0:QH, :] = gq[:, cols].astype(f32) + eq[:, cols].astype(f32)
-            out[i, j, QH:HALF, :] = gd[:, cols].astype(f32) + ed[:, cols].astype(f32)
-
-
-def send_kernel(core_ref, gq, eq, gd, ed, out, bq, cq, bd, cd, sems):
-    merge_half(1 - core_ref[0], (gq, eq, gd, ed), (bq, cq, bd, cd), sems, out)
-
-
-def keep_kernel(core_ref, gq, eq, gd, ed, qq, qd, out, qpack, bq, cq, bd, cd, sems, qbuf, qsems):
-    q_copies = [pltpu.make_async_copy(r, qbuf.at[k], qsems.at[k]) for k, r in enumerate((qq, qd))]
-    for c in q_copies:
-        c.start()
-    qpack[16:QPAD, :] = jnp.zeros((QPAD - 16, LANES), jnp.float32)
-    for c in q_copies:
-        c.wait()
-    qpack[0:16, :] = jnp.concatenate([qbuf[0], qbuf[1]], axis=1)
-    merge_half(core_ref[0], (gq, eq, gd, ed), (bq, cq, bd, cd), sems, out)
-
-
-def factor_kernel(parts, q_all, s_ref, f_ref, qbuf, qsems):
-    copies = [pltpu.make_async_copy(q_all.at[g, 0:16], qbuf.at[g], qsems.at[g]) for g in range(8)]
-    for c in copies:
-        c.start()
+        for out, owner in ((send, 1 - core), (keep, core)):
+            rq = pl.ds(pl.multiple_of(owner * QH, QH), QH)
+            rd = pl.ds(pl.multiple_of(owner * DH, DH), DH)
+            for block in range(ch * per, (ch + 1) * per):
+                i, j = slot(owner, block)
+                cols = pl.ds(block * LANES, LANES)
+                out[i, j, 0:QH, :] = bq[rq, cols].astype(f32) + cq[rq, cols].astype(f32)
+                out[i, j, QH:HALF, :] = bd[rd, cols].astype(f32) + cd[rd, cols].astype(f32)
+
+
+def factor_kernel(parts, q_all, s_ref, f_ref):
     s = parts[0]
     for i in range(1, 8):
         s = s + parts[i]
     s_ref[...] = s
-    for c in copies:
-        c.wait()
-    r = jnp.dot(s, qbuf[...].reshape(LANES, LANES), precision=HIGH, preferred_element_type=jnp.float32)
+    q = q_all[...].reshape(LANES, LANES)
+    r = jnp.dot(s, q, precision=HIGH, preferred_element_type=jnp.float32)
     low = jnp.concatenate([r[0:QH], pltpu.roll(r[40:48], RANK, 1)], axis=0)
     lane = lax.broadcasted_iota(jnp.int32, (PACK, LANES), 1)
     packed = jnp.where(lane < RANK, low, r[QH:40])
@@ -166,8 +147,8 @@
     return lax.dot_general(a, b, (dims, ((), ())), precision=HIGH, preferred_element_type=jnp.float32)
 
 
-def solve_kernel(where_ref, all_ref, basis_q, basis_d, qn_q, qn_d, approx, qn_scratch):
-    core, x = where_ref[0], where_ref[1]
+def solve_kernel(all_ref, basis_q, basis_d, qn_q, qn_d, approx, qn_scratch):
+    core, x = lax.axis_index("core"), lax.axis_index("x")
     f_rows, s_rows = [], []
     for g in range(8):
         fq, fd = unpack_factor(all_ref[g, 0:PACK])
@@ -222,12 +203,12 @@
         c.wait()
 
 
-def own_error_kernel(core_ref, gq, eq, gd, ed, src, out_q, out_d, buf_q, buf_d, sems):
-    error_half(core_ref[0], gq, eq, gd, ed, src, out_q, out_d, buf_q, buf_d, sems)
-
-
-def other_error_kernel(core_ref, gq, eq, gd, ed, src, in_q, in_d, out_q, out_d, buf_q, buf_d, sems):
-    error_half(1 - core_ref[0], gq, eq, gd, ed, src, out_q, out_d, buf_q, buf_d, sems)
+def own_error_kernel(gq, eq, gd, ed, src, out_q, out_d, buf_q, buf_d, sems):
+    error_half(lax.axis_index("core"), gq, eq, gd, ed, src, out_q, out_d, buf_q, buf_d, sems)
+
+
+def other_error_kernel(gq, eq, gd, ed, src, in_q, in_d, out_q, out_d, buf_q, buf_d, sems):
+    error_half(1 - lax.axis_index("core"), gq, eq, gd, ed, src, out_q, out_d, buf_q, buf_d, sems)
 
 
 def shape(*dims, dtype=jnp.float32):
@@ -235,11 +216,10 @@
 
 
 VM = pl.BlockSpec(memory_space=pltpu.VMEM)
-SM = pl.BlockSpec(memory_space=pltpu.SMEM)
 HB = pl.BlockSpec(memory_space=pltpu.HBM)
 
 
-def call(kernel, in_specs, out_shape, out_specs, scratch=(), moved=0, aliases=None, vmem=24):
+def call(kernel, in_specs, out_shape, out_specs, scratch=(), moved=0, aliases=None):
     return pl.pallas_call(
         kernel,
         out_shape=out_shape,
@@ -248,7 +228,7 @@
         scratch_shapes=list(scratch),
         input_output_aliases=aliases or {},
         cost_estimate=pl.CostEstimate(flops=moved, bytes_accessed=moved, transcendentals=0),
-        compiler_params=pltpu.CompilerParams(vmem_limit_bytes=int(vmem * MIB)),
+        compiler_params=pltpu.CompilerParams(vmem_limit_bytes=24 * MIB),
     )
 
 
@@ -257,35 +237,28 @@
 
 
 def on_device(grad_query, error_query, q_query, grad_down, error_down, q_down):
-    core = lax.axis_index("core").astype(jnp.int32)
-    place = jnp.stack([core, lax.axis_index("x").astype(jnp.int32)])
     half = shape(8, 8, HALF, LANES)
     bf16 = jnp.bfloat16
-    dma = pltpu.SemaphoreType.DMA
-    half_bufs = [pltpu.VMEM((n, WIDTH), bf16) for n in (QH, QH, DH, DH)] + [dma((CHUNKS, 4))]
     grads = (grad_query[0], error_query[0], grad_down[0], error_down[0])
-    send = call(send_kernel, [SM] + [HB] * 4, half, VM, half_bufs, 3 << 20, vmem=SEND_VMEM)(place, *grads)
+    qpack = jnp.concatenate([q_query.T, q_down.T], axis=1)
+    q_all = lax.all_to_all(
+        jnp.broadcast_to(qpack[None], (8, 16, LANES)), ("core", "x"), 0, 0, tiled=True
+    )
+    buffers = [pltpu.VMEM((n, WIDTH), bf16) for n in (2 * QH, 2 * QH, 2 * DH, 2 * DH)]
+    send, keep = call(
+        merge_kernel,
+        [HB] * 4,
+        (half, half),
+        (VM, VM),
+        buffers + [pltpu.SemaphoreType.DMA((CHUNKS, 4))],
+        moved=6 << 20,
+    )(*[pltpu.with_memory_space_constraint(g, pltpu.HBM) for g in grads])
     other = swap_cores(send)
-    keep, qpack = call(
-        keep_kernel,
-        [SM] + [HB] * 6,
-        (half, shape(QPAD, LANES)),
-        (VM, VM),
-        half_bufs + [pltpu.VMEM((2, 16, RANK), jnp.float32), dma((2,))],
-        3 << 20,
-        vmem=KEEP_VMEM,
-    )(place, *grads, q_query.T, q_down.T)
-    q_all = lax.all_gather(qpack[None], ("core", "x"), axis=0, tiled=True)
+    keep, other, q_all = lax.optimization_barrier((keep, other, q_all))
     part = exchange(keep + other, WIDE)
     part = exchange(jnp.sum(part, axis=0), NARROW)
     s_own, f = call(
-        factor_kernel,
-        [VM, HB],
-        (shape(HALF, LANES), shape(8, PACK, LANES)),
-        (VM, VM),
-        [pltpu.VMEM((8, 16, LANES), jnp.float32), dma((8,))],
-        1 << 18,
-        vmem=FACTOR_VMEM,
+        factor_kernel, [VM, VM], (shape(HALF, LANES), shape(8, PACK, LANES)), (VM, VM), moved=1 << 18
     )(part, q_all)
     f = exchange(f, NARROW)
     f = jnp.broadcast_to(jnp.sum(f, axis=0)[None], (8, PACK, LANES))
@@ -296,21 +269,21 @@
     )
     basis_q, basis_d, qn_q, qn_d, approx = call(
         solve_kernel,
-        [SM, VM],
+        [VM],
         (shape(2 * QH, RANK), shape(2 * DH, RANK), shape(16, RANK), shape(16, RANK), shape(8, HALF, LANES)),
         (VM,) * 5,
         [pltpu.VMEM((2, LANES, LANES), jnp.float32)],
-        1 << 20,
-    )(place, both)
+        moved=1 << 20,
+    )(both)
     approx = exchange(approx, NARROW)
     own = exchange(jnp.broadcast_to(approx[None], (8, 8, HALF, LANES)), WIDE)
     other = swap_cores(own)
     errors = (shape(2 * QH, WIDTH, dtype=bf16), shape(2 * DH, WIDTH, dtype=bf16))
-    bufs = [pltpu.VMEM((n, WIDTH), bf16) for n in (QH, DH)] + [dma((CHUNKS, 2))]
-    first = call(own_error_kernel, [SM] + [VM] * 5, errors, (HB, HB), bufs, 4 << 20)(place, *grads, own)
+    bufs = [pltpu.VMEM((n, WIDTH), bf16) for n in (QH, DH)] + [pltpu.SemaphoreType.DMA((CHUNKS, 2))]
+    first = call(own_error_kernel, [VM] * 5, errors, (HB, HB), bufs, 4 << 20)(*grads, own)
     err_q, err_d = call(
-        other_error_kernel, [SM] + [VM] * 5 + [HB] * 2, errors, (HB, HB), bufs, 4 << 20, {6: 0, 7: 1}
-    )(place, *grads, other, *first)
+        other_error_kernel, [VM] * 5 + [HB] * 2, errors, (HB, HB), bufs, 4 << 20, {5: 0, 6: 1}
+    )(*grads, other, *first)
     return (err_q[None], basis_q, qn_q.T, err_d[None], basis_d, qn_d.T)
 
 

time: 171 us -> 150 us (0.88)
  blocking collectives: 74.5 us -> 125 us
  waiting for transfers between devices: 33.4 us -> 1.95 us
  between operations: 14.2 us -> 0.81 us
  starting transfers between devices: 24.9 us -> 13.4 us
  Pallas kernels: 17.9 us -> 8.26 us
  other arithmetic: 4.86 us -> 0.4 us
    all_to_all x4 -> x6, blocking collectives: 59.8 us -> 102 us  [exchange(): return lax.all_to_all(x, AXES, 0, 0, axis_index_groups=groups, tiled=True)]
    all_to_all x2 -> x0, waiting for transfers between devices: 28.3 us -> none  [exchange(): return lax.all_to_all(x, AXES, 0, 0, axis_index_groups=groups, tiled=True)]
    all_to_all x2 -> x0, starting transfers between devices: 11.5 us -> none  [exchange(): return lax.all_to_all(x, AXES, 0, 0, axis_index_groups=groups, tiled=True)]
    pallas_call x6 -> x5, Pallas kernels: 17.9 us -> 8.26 us  [the longest x1 3.9 us: on_device(): call(solve_kernel, [VM], (shape(2 * QH, RANK), shape(2 * DH, RANK), shape...]
    all_to_all x0 -> x1, blocking collectives: none -> 7.33 us  [on_device(): lax.all_to_all(jnp.broadcast_to(qpack[None], (8, 16, LANES)), ('core', 'x...]
    all_gather x1 -> x0, waiting for transfers between devices: 3.01 us -> none  [on_device(): q_all = lax.all_gather(qpack[None], ('core', 'x'), axis=0, tiled=True)]
    add x1, other arithmetic: 2.75 us -> 0.21 us  [on_device(): part = exchange(keep + other, WIDE)]
  transfers between devices with their start and end apart: 5 -> 2, of which waited for: 4 -> 1; matrix products, arithmetic and copies ran while one was open for 0% -> 0% of each run, Pallas kernels for 3% -> 1%
where the time goes in v3:
time: 150 us
  blocking collectives  125 us (83%)
  starting transfers between devices  13.4 us (9%)
  Pallas kernels  8.26 us (6%)
  waiting for transfers between devices  1.95 us (1%)
    all_to_all x6, blocking collectives, exchange(): return lax.all_to_all(x, AXES, 0, 0, axis_index_groups=groups, tiled=True)  102 us
    all_to_all x1, blocking collectives, on_device(): lax.all_to_all(jnp.broadcast_to(both[None], (8, PACK + HALF, LANES)), ('c...  15.4 us
    ppermute x2, starting transfers between devices, swap_cores(): return lax.ppermute(x, 'core', [(0, 1), (1, 0)])  13.4 us
    all_to_all x1, blocking collectives, on_device(): lax.all_to_all(jnp.broadcast_to(qpack[None], (8, 16, LANES)), ('core', 'x...  7.33 us
    pallas_call x1, Pallas kernels, on_device(): call(solve_kernel, [VM], (shape(2 * QH, RANK), shape(2 * DH, RANK), shape...  3.9 us
  transfers between devices with their start and end apart: 2, of which 1 were waited for; matrix products, arithmetic and copies ran while one was open for 0% of the time, Pallas kernels for 1%

profile of v3, /device:TPU:1, one launch (start us, length us, event | category | flops | bytes accessed | tf_op | source)
XLA Modules:
  0.0 149.7 jit_solution(10742157464157868536)
XLA Ops:
  0.6 0.0 copy-start.4
  0.6 0.0 copy-start.5
  0.7 2.1 %shard_map.109 = (f32[8,8,48,128]{3,2,1,0:T(8,128)S(1)}, f32[8,8,48,128]{3,2,1,0:T(8,128)S(1)}) custom-call(bf16[32,8192]{1,0:T(8,128)(2,1)} %bitcast.16, bf16[32,8192]{1,0:T(8,128)(2,1)} %bitcast.19, bf16[64,8192]{1,0:T(8,128)(2,1)} %bitcast.10, bf16[64,8192]{1,0:T(8,128)(2,1)} %bitcast.13), custom_call_target="tpu_custom_call" | custom-call | flops 6291456 | bytes 6291456 | tf_op jit(solution)/shard_map/pallas_call | solution.py:248
  2.8 8.8 %collective-permute-start = (f32[8,8,48,128]{3,2,1,0:T(8,128)S(1)}, f32[8,8,48,128]{3,2,1,0:T(8,128)S(1)}, u32[]{:S(2)}, u32[]{:S(2)}) collective-permute-start(f32[8,8,48,128]{3,2,1,0:T(8,128)S(1)} %get-tuple-element.23), channel_id=1, source_target_pairs={{0,4},{4,0},{1,5},{5,1},{2,6},{6,2},{3,7},{7,3},{8,12},{12,8},{9,1... | collective-permute-start | bytes 4718600 | tf_op jit(solution)/shard_map/ppermute | solution.py:236
  11.6 0.0 copy-done.4
  11.6 0.0 copy-done.5
  11.6 0.1 pad_maximum_fusion.1
  11.7 7.3 %all_to_all.40.q_all = f32[8,16,128]{2,1,0:T(8,128)S(1)} all-to-all(f32[8,16,128]{2,1,0:T(8,128)S(1)} %broadcast_in_dim.12), channel_id=1, replica_groups=mesh['z'=8,'y'=8,'core'=2,'x'=4] {'core','x'}, dimensions={0} | all-to-all | bytes 131072 | tf_op jit(solution)/shard_map/all_to_all | solution.py:244
  19.0 0.0 collective-permute-done
  19.0 0.2 add.3
  19.2 29.7 %all_to_all.41 = f32[8,8,48,128]{3,2,1,0:T(8,128)S(1)} all-to-all(f32[8,8,48,128]{3,2,1,0:T(8,128)S(1)} %add.3), channel_id=1, replica_groups={{0,8,16,24,32,40,48,56},{64,72,80,88,96,104,112,120},{128,136,144,152,1..., dimensions={0} | all-to-all | bytes 3145728 | tf_op jit(solution)/shard_map/all_to_all | solution.py:43
  48.9 0.1 reduce_sum.27
  49.0 15.2 %all_to_all.42.parts = f32[8,48,128]{2,1,0:T(8,128)S(1)} all-to-all(f32[8,48,128]{2,1,0:T(8,128)S(1)} %reduce_sum.27), channel_id=1, replica_groups={{0,64,128,192,256,320,384,448},{8,72,136,200,264,328,392,456},{16,80,14..., dimensions={0} | all-to-all | bytes 393216 | tf_op jit(solution)/shard_map/all_to_all | solution.py:43
  64.2 0.2 shard_map.110
  64.5 10.0 %all_to_all.43 = f32[8,24,128]{2,1,0:T(8,128)S(1)} all-to-all(f32[8,24,128]{2,1,0:T(8,128)S(1)} %get-tuple-element.27), channel_id=1, replica_groups={{0,64,128,192,256,320,384,448},{8,72,136,200,264,328,392,456},{16,80,14..., dimensions={0} | all-to-all | bytes 196608 | tf_op jit(solution)/shard_map/all_to_all | solution.py:43
  74.5 10.0 %all_to_all.44 = f32[8,24,128]{2,1,0:T(8,128)S(1)} all-to-all(f32[8,24,128]{2,1,0:T(8,128)S(1)} %broadcast_in_dim.13), channel_id=1, replica_groups={{0,8,16,24,32,40,48,56},{64,72,80,88,96,104,112,120},{128,136,144,152,1..., dimensions={0} | all-to-all | bytes 196608 | tf_op jit(solution)/shard_map/all_to_all | solution.py:43
  84.5 15.4 %all_to_all.45.all_ref = f32[8,72,128]{2,1,0:T(8,128)S(1)} all-to-all(f32[8,72,128]{2,1,0:T(8,128)S(1)} %broadcast_in_dim.14), channel_id=1, replica_groups=mesh['z'=8,'y'=8,'core'=2,'x'=4] {'core','x'}, dimensions={0} | all-to-all | bytes 589824 | tf_op jit(solution)/shard_map/all_to_all | solution.py:267
  99.9 3.9 %shard_map.111 = (f32[32,64]{1,0:T(8,128)}, f32[64,64]{1,0:T(8,128)}, f32[16,64]{1,0:T(8,128)}, f32[16,64]{1,0:T(8,128)}, f32[8,48,128]{2,1,0:T(8,128)S(1)}) custom-call(f32[8,72,128]{2,1,0:T(8,128)S(1)} %all_to_all.45.all_ref), custom_call_target="tpu_custom_call" | custom-call | flops 1048576 | bytes 1048576 | tf_op jit(solution)/shard_map/pallas_call | solution.py:270
  103.8 11.0 %all_to_all.46 = f32[8,48,128]{2,1,0:T(8,128)S(1)} all-to-all(f32[8,48,128]{2,1,0:T(8,128)S(1)} %get-tuple-element.29), channel_id=1, replica_groups={{0,64,128,192,256,320,384,448},{8,72,136,200,264,328,392,456},{16,80,14..., dimensions={0} | all-to-all | bytes 393216 | tf_op jit(solution)/shard_map/all_to_all | solution.py:43
  114.8 0.1 broadcast_in_dim.15
  114.9 0.0 copy-start
  115.0 0.0 copy-start.1
  115.0 0.0 copy-start.2
  115.0 0.0 copy-start.3
  115.0 26.1 %all_to_all.47.src = f32[8,8,48,128]{3,2,1,0:T(8,128)S(1)} all-to-all(f32[8,8,48,128]{3,2,1,0:T(8,128)S(1)} %broadcast_in_dim.15), channel_id=1, replica_groups={{0,8,16,24,32,40,48,56},{64,72,80,88,96,104,112,120},{128,136,144,152,1..., dimensions={0} | all-to-all | bytes 3145728 | tf_op jit(solution)/shard_map/all_to_all | solution.py:43
  141.1 4.6 %collective-permute-start.1 = (f32[8,8,48,128]{3,2,1,0:T(8,128)S(1)}, f32[8,8,48,128]{3,2,1,0:T(8,128)S(1)}, u32[]{:S(2)}, u32[]{:S(2)}) collective-permute-start(f32[8,8,48,128]{3,2,1,0:T(8,128)S(1)} %all_to_all.47.src), channel_id=1, source_target_pairs={{0,4},{4,0},{1,5},{5,1},{2,6},{6,2},{3,7},{7,3},{8,12},{12,8},{9,1... | collective-permute-start | bytes 4718600 | tf_op jit(solution)/shard_map/ppermute | solution.py:236
  145.7 0.0 copy-done
  145.7 0.0 copy-done.1
  145.7 0.0 copy-done.2
  145.7 1.0 shard_map.112
  146.7 1.9 %collective-permute-done.1.src = f32[8,8,48,128]{3,2,1,0:T(8,128)S(1)} collective-permute-done((f32[8,8,48,128]{3,2,1,0:T(8,128)S(1)}, f32[8,8,48,128]{3,2,1,0:T(8,128)S(1)}, u32[]{:S(2)}, u32[]{:S(2)}) %collective-permute-start.1) | collective-permute-done | bytes 1572896 | tf_op jit(solution)/shard_map/ppermute | solution.py:236
  148.7 1.0 shard_map.113
  (7 shorter events, 0.1 us)
Async XLA Ops:
  0.6 10.9 %copy-start.4 = (f32[64,16]{0,1:T(8,128)S(1)}, f32[64,16]{0,1:T(8,128)}, u32[]{:S(2)}) copy-start(f32[64,16]{0,1:T(8,128)} %param.11) | copy-start | bytes 12292
  0.6 10.9 %copy-start.5 = (f32[64,16]{0,1:T(8,128)S(1)}, f32[64,16]{0,1:T(8,128)}, u32[]{:S(2)}) copy-start(f32[64,16]{0,1:T(8,128)} %param.8) | copy-start | bytes 12292
  2.8 16.2 %collective-permute-start = (f32[8,8,48,128]{3,2,1,0:T(8,128)S(1)}, f32[8,8,48,128]{3,2,1,0:T(8,128)S(1)}, u32[]{:S(2)}, u32[]{:S(2)}) collective-permute-start(f32[8,8,48,128]{3,2,1,0:T(8,128)S(1)} %get-tuple-element.23), channel_id=1, source_target_pairs={{0,4},{4,0},{1,5},{5,1},{2,6},{6,2},{3,7},{7,3},{8,12},{12,8},{9,1... | collective-permute-start | bytes 4718600 | tf_op jit(solution)/shard_map/ppermute | solution.py:236
  114.9 30.7 %copy-start = (bf16[1,64,8192]{2,1,0:T(8,128)(2,1)S(1)}, bf16[1,64,8192]{2,1,0:T(8,128)(2,1)}, u32[]{:S(2)}) copy-start(bf16[1,64,8192]{2,1,0:T(8,128)(2,1)} %param.9) | copy-start | bytes 3145732
  115.0 30.7 %copy-start.1 = (bf16[1,64,8192]{2,1,0:T(8,128)(2,1)S(1)}, bf16[1,64,8192]{2,1,0:T(8,128)(2,1)}, u32[]{:S(2)}) copy-start(bf16[1,64,8192]{2,1,0:T(8,128)(2,1)} %param.10) | copy-start | bytes 3145732
  115.0 30.7 %copy-start.2 = (bf16[1,32,8192]{2,1,0:T(8,128)(2,1)S(1)}, bf16[1,32,8192]{2,1,0:T(8,128)(2,1)}, u32[]{:S(2)}) copy-start(bf16[1,32,8192]{2,1,0:T(8,128)(2,1)} %param.6) | copy-start | bytes 1572868
  115.0 30.7 %copy-start.3 = (bf16[1,32,8192]{2,1,0:T(8,128)(2,1)S(1)}, bf16[1,32,8192]{2,1,0:T(8,128)(2,1)}, u32[]{:S(2)}) copy-start(bf16[1,32,8192]{2,1,0:T(8,128)(2,1)} %param.7) | copy-start | bytes 1572868
  141.1 7.6 %collective-permute-start.1 = (f32[8,8,48,128]{3,2,1,0:T(8,128)S(1)}, f32[8,8,48,128]{3,2,1,0:T(8,128)S(1)}, u32[]{:S(2)}, u32[]{:S(2)}) collective-permute-start(f32[8,8,48,128]{3,2,1,0:T(8,128)S(1)} %all_to_all.47.src), channel_id=1, source_target_pairs={{0,4},{4,0},{1,5},{5,1},{2,6},{6,2},{3,7},{7,3},{8,12},{12,8},{9,1... | collective-permute-start | bytes 4718600 | tf_op jit(solution)/shard_map/ppermute | solution.py:236

commit v4 on v3

--- a/solution.py
+++ b/solution.py
@@ -80,8 +80,9 @@
     for i in range(1, 8):
         s = s + parts[i]
     s_ref[...] = s
-    q = q_all[...].reshape(LANES, LANES)
-    r = jnp.dot(s, q, precision=HIGH, preferred_element_type=jnp.float32)
+    core, x = lax.axis_index("core"), lax.axis_index("x")
+    q = [q_all[(a - x + NX) % NX, (c + core) % NC] for c in range(NC) for a in range(NX)]
+    r = jnp.dot(s, jnp.concatenate(q, axis=0), precision=HIGH, preferred_element_type=jnp.float32)
     low = jnp.concatenate([r[0:QH], pltpu.roll(r[40:48], RANK, 1)], axis=0)
     lane = lax.broadcasted_iota(jnp.int32, (PACK, LANES), 1)
     packed = jnp.where(lane < RANK, low, r[QH:40])
@@ -240,10 +241,6 @@
     half = shape(8, 8, HALF, LANES)
     bf16 = jnp.bfloat16
     grads = (grad_query[0], error_query[0], grad_down[0], error_down[0])
-    qpack = jnp.concatenate([q_query.T, q_down.T], axis=1)
-    q_all = lax.all_to_all(
-        jnp.broadcast_to(qpack[None], (8, 16, LANES)), ("core", "x"), 0, 0, tiled=True
-    )
     buffers = [pltpu.VMEM((n, WIDTH), bf16) for n in (2 * QH, 2 * QH, 2 * DH, 2 * DH)]
     send, keep = call(
         merge_kernel,
@@ -254,8 +251,14 @@
         moved=6 << 20,
     )(*[pltpu.with_memory_space_constraint(g, pltpu.HBM) for g in grads])
     other = swap_cores(send)
-    keep, other, q_all = lax.optimization_barrier((keep, other, q_all))
-    part = exchange(keep + other, WIDE)
+    qpack = jnp.concatenate([q_query.T, q_down.T], axis=1)
+    total, qpack = lax.optimization_barrier((keep + other, qpack))
+    part = exchange(total, WIDE)
+    qpack = jnp.stack([qpack, swap_cores(qpack)])
+    q_all = jnp.stack([qpack] + [
+        lax.ppermute(qpack, "x", [((x + k) % NX, x) for x in range(NX)]) for k in range(1, NX)
+    ])
+    part, q_all = lax.optimization_barrier((part, q_all))
     part = exchange(jnp.sum(part, axis=0), NARROW)
     s_own, f = call(
         factor_kernel, [VM, VM], (shape(HALF, LANES), shape(8, PACK, LANES)), (VM, VM), moved=1 << 18

time: 150 us -> 147 us (0.980)
  blocking collectives: 125 us -> 89.2 us
  starting transfers between devices: 13.4 us -> 31.1 us
  waiting for transfers between devices: 1.95 us -> 15.2 us
    all_to_all x6 -> x5, blocking collectives: 102 us -> 72.2 us  [exchange(): return lax.all_to_all(x, AXES, 0, 0, axis_index_groups=groups, tiled=True)]
    ppermute x0 -> x3, starting transfers between devices: none -> 11.1 us  [on_device(): lax.ppermute(qpack, 'x', [((x + k) % NX, x) for x in range(NX)])]
    all_to_all x0 -> x1, waiting for transfers between devices: none -> 8.35 us  [exchange(): return lax.all_to_all(x, AXES, 0, 0, axis_index_groups=groups, tiled=True)]
    all_to_all x1 -> x0, blocking collectives: 7.33 us -> none  [on_device(): lax.all_to_all(jnp.broadcast_to(qpack[None], (8, 16, LANES)), ('core', 'x...]
    all_to_all x0 -> x1, starting transfers between devices: none -> 4.66 us  [exchange(): return lax.all_to_all(x, AXES, 0, 0, axis_index_groups=groups, tiled=True)]
    ppermute x2 -> x3, waiting for transfers between devices: 1.95 us -> 6.01 us  [swap_cores(): return lax.ppermute(x, 'core', [(0, 1), (1, 0)])]
    ppermute x2 -> x3, starting transfers between devices: 13.4 us -> 15.3 us  [swap_cores(): return lax.ppermute(x, 'core', [(0, 1), (1, 0)])]
    all_to_all x1, blocking collectives: 15.4 us -> 17 us  [on_device(): lax.all_to_all(jnp.broadcast_to(both[None], (8, PACK + HALF, LANES)), ('c...]
  transfers between devices with their start and end apart: 2 -> 7, of which waited for: 1 -> 5; matrix products, arithmetic and copies ran while one was open for 0% -> 0% of each run, Pallas kernels for 1% -> 1%
where the time goes in v4:
time: 147 us; the launch traced here: 146 us
  blocking collectives  89.2 us (61%)
  starting transfers between devices  31.1 us (21%)
  waiting for transfers between devices  15.2 us (10%)
  Pallas kernels  8.28 us (6%)
  other arithmetic  1.56 us (1%)
    all_to_all x5, blocking collectives, exchange(): return lax.all_to_all(x, AXES, 0, 0, axis_index_groups=groups, tiled=True)  72.2 us
    all_to_all x1, blocking collectives, on_device(): lax.all_to_all(jnp.broadcast_to(both[None], (8, PACK + HALF, LANES)), ('c...  17 us
    ppermute x3, starting transfers between devices, swap_cores(): return lax.ppermute(x, 'core', [(0, 1), (1, 0)])  15.3 us
    ppermute x3, starting transfers between devices, on_device(): lax.ppermute(qpack, 'x', [((x + k) % NX, x) for x in range(NX)])  11.1 us
    all_to_all x1, waiting for transfers between devices, exchange(): return lax.all_to_all(x, AXES, 0, 0, axis_index_groups=groups, tiled=True)  8.35 us
    ppermute x3, waiting for transfers between devices, swap_cores(): return lax.ppermute(x, 'core', [(0, 1), (1, 0)])  6.01 us
    all_to_all x1, starting transfers between devices, exchange(): return lax.all_to_all(x, AXES, 0, 0, axis_index_groups=groups, tiled=True)  4.66 us
    pallas_call x1, Pallas kernels, on_device(): call(solve_kernel, [VM], (shape(2 * QH, RANK), shape(2 * DH, RANK), shape...  3.9 us
  transfers between devices with their start and end apart: 7, of which 5 were waited for; matrix products, arithmetic and copies ran while one was open for 0% of the time, Pallas kernels for 1%

profile of v4, /device:TPU:1, one launch (start us, length us, event | category | flops | bytes accessed | tf_op | source)
XLA Modules:
  0.0 146.4 jit_solution(6640681025990557429)
XLA Ops:
  0.7 2.1 %shard_map.109 = (f32[8,8,48,128]{3,2,1,0:T(8,128)S(1)}, f32[8,8,48,128]{3,2,1,0:T(8,128)S(1)}) custom-call(bf16[32,8192]{1,0:T(8,128)(2,1)} %bitcast.23, bf16[32,8192]{1,0:T(8,128)(2,1)} %bitcast.26, bf16[64,8192]{1,0:T(8,128)(2,1)} %bitcast.17, bf16[64,8192]{1,0:T(8,128)(2,1)} %bitcast.20), custom_call_target="tpu_custom_call" | custom-call | flops 6291456 | bytes 6291456 | tf_op jit(solution)/shard_map/pallas_call | solution.py:245
  2.8 8.8 %collective-permute-start = (f32[8,8,48,128]{3,2,1,0:T(8,128)S(1)}, f32[8,8,48,128]{3,2,1,0:T(8,128)S(1)}, u32[]{:S(2)}, u32[]{:S(2)}) collective-permute-start(f32[8,8,48,128]{3,2,1,0:T(8,128)S(1)} %get-tuple-element.24), channel_id=1, source_target_pairs={{0,4},{4,0},{1,5},{5,1},{2,6},{6,2},{3,7},{7,3},{8,12},{12,8},{9,1... | collective-permute-start | bytes 4718600 | tf_op jit(solution)/shard_map/ppermute | solution.py:237
  11.6 0.1 pad_maximum_fusion.3
  11.7 2.9 %collective-permute-done = f32[8,8,48,128]{3,2,1,0:T(8,128)S(1)} collective-permute-done((f32[8,8,48,128]{3,2,1,0:T(8,128)S(1)}, f32[8,8,48,128]{3,2,1,0:T(8,128)S(1)}, u32[]{:S(2)}, u32[]{:S(2)}) %collective-permute-start) | collective-permute-done | bytes 1572896 | tf_op jit(solution)/shard_map/ppermute | solution.py:237
  14.6 1.4 add.3
  15.9 4.7 %all-to-all-start = ((f32[8,8,48,128]{3,2,1,0:T(8,128)}), f32[8,8,48,128]{3,2,1,0:T(8,128)S(1)}, u32[]{:S(2)}, u32[]{:S(2)}) async-start(f32[8,8,48,128]{3,2,1,0:T(8,128)} %add.3), calls=%async_computation | async-start | bytes 3145728 | tf_op jit(solution)/shard_map/all_to_all | solution.py:43
  20.6 1.9 %collective-permute-start.1 = (f32[16,128]{1,0:T(8,128)S(1)}, f32[16,128]{1,0:T(8,128)S(1)}, u32[]{:S(2)}, u32[]{:S(2)}) collective-permute-start(f32[16,128]{1,0:T(8,128)S(1)} %pad_maximum_fusion.3), channel_id=1, source_target_pairs={{0,4},{4,0},{1,5},{5,1},{2,6},{6,2},{3,7},{7,3},{8,12},{12,8},{9,1... | collective-permute-start | bytes 24584 | tf_op jit(solution)/shard_map/ppermute | solution.py:237
  22.5 1.1 collective-permute-done.1
  23.7 4.6 %collective-permute-start.3 = (f32[2,16,128]{2,1,0:T(8,128)S(1)}, f32[2,16,128]{2,1,0:T(8,128)S(1)}, u32[]{:S(2)}, u32[]{:S(2)}) collective-permute-start(f32[2,16,128]{2,1,0:T(8,128)S(1)} %get-tuple-element.41), channel_id=1, source_target_pairs={{2,0},{3,1},{0,2},{1,3},{6,4},{7,5},{4,6},{5,7},{10,8},{11,9},{8,1... | collective-permute-start | bytes 49160 | tf_op jit(solution)/shard_map/ppermute | solution.py:259
  28.3 2.2 %collective-permute-start.4 = (f32[2,16,128]{2,1,0:T(8,128)S(1)}, f32[2,16,128]{2,1,0:T(8,128)S(1)}, u32[]{:S(2)}, u32[]{:S(2)}) collective-permute-start(f32[2,16,128]{2,1,0:T(8,128)S(1)} %get-tuple-element.41), channel_id=1, source_target_pairs={{3,0},{0,1},{1,2},{2,3},{7,4},{4,5},{5,6},{6,7},{11,8},{8,9},{9,10... | collective-permute-start | bytes 49160 | tf_op jit(solution)/shard_map/ppermute | solution.py:259
  30.5 4.3 %collective-permute-start.2 = (f32[2,16,128]{2,1,0:T(8,128)S(1)}, f32[2,16,128]{2,1,0:T(8,128)S(1)}, u32[]{:S(2)}, u32[]{:S(2)}) collective-permute-start(f32[2,16,128]{2,1,0:T(8,128)S(1)} %get-tuple-element.41), channel_id=1, source_target_pairs={{1,0},{2,1},{3,2},{0,3},{5,4},{6,5},{7,6},{4,7},{9,8},{10,9},{11,1... | collective-permute-start | bytes 49160 | tf_op jit(solution)/shard_map/ppermute | solution.py:259
  34.8 0.0 collective-permute-done.3
  34.8 0.8 collective-permute-done.2
  35.7 8.4 %all-to-all-done = f32[8,8,48,128]{3,2,1,0:T(8,128)S(1)} async-done(((f32[8,8,48,128]{3,2,1,0:T(8,128)}), f32[8,8,48,128]{3,2,1,0:T(8,128)S(1)}, u32[]{:S(2)}, u32[]{:S(2)}) %all-to-all-start) | async-done | bytes 1572896 | tf_op jit(solution)/shard_map/all_to_all | solution.py:43
  44.0 0.1 reduce_sum.27
  44.1 15.2 %all_to_all.35.parts = f32[8,48,128]{2,1,0:T(8,128)S(1)} all-to-all(f32[8,48,128]{2,1,0:T(8,128)S(1)} %reduce_sum.27), channel_id=1, replica_groups={{0,64,128,192,256,320,384,448},{8,72,136,200,264,328,392,456},{16,80,14..., dimensions={0} | all-to-all | bytes 393216 | tf_op jit(solution)/shard_map/all_to_all | solution.py:43
  59.4 0.2 shard_map.110
  59.6 10.0 %all_to_all.36 = f32[8,24,128]{2,1,0:T(8,128)S(1)} all-to-all(f32[8,24,128]{2,1,0:T(8,128)S(1)} %get-tuple-element.29), channel_id=1, replica_groups={{0,64,128,192,256,320,384,448},{8,72,136,200,264,328,392,456},{16,80,14..., dimensions={0} | all-to-all | bytes 196608 | tf_op jit(solution)/shard_map/all_to_all | solution.py:43
  69.6 10.0 %all_to_all.37 = f32[8,24,128]{2,1,0:T(8,128)S(1)} all-to-all(f32[8,24,128]{2,1,0:T(8,128)S(1)} %broadcast_in_dim.10), channel_id=1, replica_groups={{0,8,16,24,32,40,48,56},{64,72,80,88,96,104,112,120},{128,136,144,152,1..., dimensions={0} | all-to-all | bytes 196608 | tf_op jit(solution)/shard_map/all_to_all | solution.py:43
  79.6 17.0 %all_to_all.38.all_ref = f32[8,72,128]{2,1,0:T(8,128)S(1)} all-to-all(f32[8,72,128]{2,1,0:T(8,128)S(1)} %broadcast_in_dim.11), channel_id=1, replica_groups=mesh['z'=8,'y'=8,'core'=2,'x'=4] {'core','x'}, dimensions={0} | all-to-all | bytes 589824 | tf_op jit(solution)/shard_map/all_to_all | solution.py:270
  96.6 3.9 %shard_map.111 = (f32[32,64]{1,0:T(8,128)}, f32[64,64]{1,0:T(8,128)}, f32[16,64]{1,0:T(8,128)}, f32[16,64]{1,0:T(8,128)}, f32[8,48,128]{2,1,0:T(8,128)S(1)}) custom-call(f32[8,72,128]{2,1,0:T(8,128)S(1)} %all_to_all.38.all_ref), custom_call_target="tpu_custom_call" | custom-call | flops 1048576 | bytes 1048576 | tf_op jit(solution)/shard_map/pallas_call | solution.py:273
  100.5 11.0 %all_to_all.39 = f32[8,48,128]{2,1,0:T(8,128)S(1)} all-to-all(f32[8,48,128]{2,1,0:T(8,128)S(1)} %get-tuple-element.31), channel_id=1, replica_groups={{0,64,128,192,256,320,384,448},{8,72,136,200,264,328,392,456},{16,80,14..., dimensions={0} | all-to-all | bytes 393216 | tf_op jit(solution)/shard_map/all_to_all | solution.py:43
  111.5 0.1 broadcast_in_dim.12
  111.6 0.0 copy-start
  111.6 0.0 copy-start.1
  111.6 0.0 copy-start.2
  111.7 0.0 copy-start.3
  111.7 26.1 %all_to_all.40.src = f32[8,8,48,128]{3,2,1,0:T(8,128)S(1)} all-to-all(f32[8,8,48,128]{3,2,1,0:T(8,128)S(1)} %broadcast_in_dim.12), channel_id=1, replica_groups={{0,8,16,24,32,40,48,56},{64,72,80,88,96,104,112,120},{128,136,144,152,1..., dimensions={0} | all-to-all | bytes 3145728 | tf_op jit(solution)/shard_map/all_to_all | solution.py:43
  137.7 4.6 %collective-permute-start.5 = (f32[8,8,48,128]{3,2,1,0:T(8,128)S(1)}, f32[8,8,48,128]{3,2,1,0:T(8,128)S(1)}, u32[]{:S(2)}, u32[]{:S(2)}) collective-permute-start(f32[8,8,48,128]{3,2,1,0:T(8,128)S(1)} %all_to_all.40.src), channel_id=1, source_target_pairs={{0,4},{4,0},{1,5},{5,1},{2,6},{6,2},{3,7},{7,3},{8,12},{12,8},{9,1... | collective-permute-start | bytes 4718600 | tf_op jit(solution)/shard_map/ppermute | solution.py:237
  142.4 1.0 shard_map.112
  143.4 1.9 %collective-permute-done.5.src = f32[8,8,48,128]{3,2,1,0:T(8,128)S(1)} collective-permute-done((f32[8,8,48,128]{3,2,1,0:T(8,128)S(1)}, f32[8,8,48,128]{3,2,1,0:T(8,128)S(1)}, u32[]{:S(2)}, u32[]{:S(2)}) %collective-permute-start.5) | collective-permute-done | bytes 1572896 | tf_op jit(solution)/shard_map/ppermute | solution.py:237
  145.3 1.0 shard_map.113
  (16 shorter events, 0.1 us)
Async XLA Ops:
  0.6 10.9 %copy-start.4 = (f32[64,16]{0,1:T(8,128)S(1)}, f32[64,16]{0,1:T(8,128)}, u32[]{:S(2)}) copy-start(f32[64,16]{0,1:T(8,128)} %param.11) | copy-start | bytes 12292
  0.6 10.9 %copy-start.5 = (f32[64,16]{0,1:T(8,128)S(1)}, f32[64,16]{0,1:T(8,128)}, u32[]{:S(2)}) copy-start(f32[64,16]{0,1:T(8,128)} %param.8) | copy-start | bytes 12292
  2.8 11.8 %collective-permute-start = (f32[8,8,48,128]{3,2,1,0:T(8,128)S(1)}, f32[8,8,48,128]{3,2,1,0:T(8,128)S(1)}, u32[]{:S(2)}, u32[]{:S(2)}) collective-permute-start(f32[8,8,48,128]{3,2,1,0:T(8,128)S(1)} %get-tuple-element.24), channel_id=1, source_target_pairs={{0,4},{4,0},{1,5},{5,1},{2,6},{6,2},{3,7},{7,3},{8,12},{12,8},{9,1... | collective-permute-start | bytes 4718600 | tf_op jit(solution)/shard_map/ppermute | solution.py:237
  15.9 28.1 %all-to-all-start = ((f32[8,8,48,128]{3,2,1,0:T(8,128)}), f32[8,8,48,128]{3,2,1,0:T(8,128)S(1)}, u32[]{:S(2)}, u32[]{:S(2)}) async-start(f32[8,8,48,128]{3,2,1,0:T(8,128)} %add.3), calls=%async_computation | async-start | bytes 3145728 | tf_op jit(solution)/shard_map/all_to_all | solution.py:43
  20.6 3.1 %collective-permute-start.1 = (f32[16,128]{1,0:T(8,128)S(1)}, f32[16,128]{1,0:T(8,128)S(1)}, u32[]{:S(2)}, u32[]{:S(2)}) collective-permute-start(f32[16,128]{1,0:T(8,128)S(1)} %pad_maximum_fusion.3), channel_id=1, source_target_pairs={{0,4},{4,0},{1,5},{5,1},{2,6},{6,2},{3,7},{7,3},{8,12},{12,8},{9,1... | collective-permute-start | bytes 24584 | tf_op jit(solution)/shard_map/ppermute | solution.py:237
  23.7 11.2 %collective-permute-start.3 = (f32[2,16,128]{2,1,0:T(8,128)S(1)}, f32[2,16,128]{2,1,0:T(8,128)S(1)}, u32[]{:S(2)}, u32[]{:S(2)}) collective-permute-start(f32[2,16,128]{2,1,0:T(8,128)S(1)} %get-tuple-element.41), channel_id=1, source_target_pairs={{2,0},{3,1},{0,2},{1,3},{6,4},{7,5},{4,6},{5,7},{10,8},{11,9},{8,1... | collective-permute-start | bytes 49160 | tf_op jit(solution)/shard_map/ppermute | solution.py:259
  28.3 6.5 %collective-permute-start.4 = (f32[2,16,128]{2,1,0:T(8,128)S(1)}, f32[2,16,128]{2,1,0:T(8,128)S(1)}, u32[]{:S(2)}, u32[]{:S(2)}) collective-permute-start(f32[2,16,128]{2,1,0:T(8,128)S(1)} %get-tuple-element.41), channel_id=1, source_target_pairs={{3,0},{0,1},{1,2},{2,3},{7,4},{4,5},{5,6},{6,7},{11,8},{8,9},{9,10... | collective-permute-start | bytes 49160 | tf_op jit(solution)/shard_map/ppermute | solution.py:259
  30.5 5.1 %collective-permute-start.2 = (f32[2,16,128]{2,1,0:T(8,128)S(1)}, f32[2,16,128]{2,1,0:T(8,128)S(1)}, u32[]{:S(2)}, u32[]{:S(2)}) collective-permute-start(f32[2,16,128]{2,1,0:T(8,128)S(1)} %get-tuple-element.41), channel_id=1, source_target_pairs={{1,0},{2,1},{3,2},{0,3},{5,4},{6,5},{7,6},{4,7},{9,8},{10,9},{11,1... | collective-permute-start | bytes 49160 | tf_op jit(solution)/shard_map/ppermute | solution.py:259
  111.6 30.7 %copy-start = (bf16[1,64,8192]{2,1,0:T(8,128)(2,1)S(1)}, bf16[1,64,8192]{2,1,0:T(8,128)(2,1)}, u32[]{:S(2)}) copy-start(bf16[1,64,8192]{2,1,0:T(8,128)(2,1)} %param.9) | copy-start | bytes 3145732
  111.6 30.7 %copy-start.1 = (bf16[1,64,8192]{2,1,0:T(8,128)(2,1)S(1)}, bf16[1,64,8192]{2,1,0:T(8,128)(2,1)}, u32[]{:S(2)}) copy-start(bf16[1,64,8192]{2,1,0:T(8,128)(2,1)} %param.10) | copy-start | bytes 3145732
  111.6 30.7 %copy-start.2 = (bf16[1,32,8192]{2,1,0:T(8,128)(2,1)S(1)}, bf16[1,32,8192]{2,1,0:T(8,128)(2,1)}, u32[]{:S(2)}) copy-start(bf16[1,32,8192]{2,1,0:T(8,128)(2,1)} %param.6) | copy-start | bytes 1572868
  111.7 30.7 %copy-start.3 = (bf16[1,32,8192]{2,1,0:T(8,128)(2,1)S(1)}, bf16[1,32,8192]{2,1,0:T(8,128)(2,1)}, u32[]{:S(2)}) copy-start(bf16[1,32,8192]{2,1,0:T(8,128)(2,1)} %param.7) | copy-start | bytes 1572868
  137.7 7.6 %collective-permute-start.5 = (f32[8,8,48,128]{3,2,1,0:T(8,128)S(1)}, f32[8,8,48,128]{3,2,1,0:T(8,128)S(1)}, u32[]{:S(2)}, u32[]{:S(2)}) collective-permute-start(f32[8,8,48,128]{3,2,1,0:T(8,128)S(1)} %all_to_all.40.src), channel_id=1, source_target_pairs={{0,4},{4,0},{1,5},{5,1},{2,6},{6,2},{3,7},{7,3},{8,12},{12,8},{9,1... | collective-permute-start | bytes 4718600 | tf_op jit(solution)/shard_map/ppermute | solution.py:237

commit v5 on v4

--- a/solution.py
+++ b/solution.py
@@ -48,31 +48,46 @@
     return jnp.where(owner == 0, y, z), jnp.where(owner == 0, z, y)
 
 
-def merge_kernel(gq, eq, gd, ed, send, keep, bq, cq, bd, cd, sems):
+def merge_half(owner, sources, out, bufs, sems):
     f32 = jnp.float32
     copies = []
     for ch in range(CHUNKS):
         cols = pl.ds(ch * CHUNK, CHUNK)
-        pairs = ((gq, bq), (eq, cq), (gd, bd), (ed, cd))
-        copies.append([
-            pltpu.make_async_copy(src.at[:, cols], buf.at[:, cols], sems.at[ch, a])
-            for a, (src, buf) in enumerate(pairs)
-        ])
-        for c in copies[-1]:
-            c.start()
-    core = lax.axis_index("core")
+        part = []
+        for a, (src, buf) in enumerate(zip(sources, bufs)):
+            n = buf.shape[0]
+            rows = pl.ds(pl.multiple_of(owner * n, n), n)
+            part.append(pltpu.make_async_copy(src.at[rows, cols], buf.at[:, cols], sems.at[ch, a]))
+            part[-1].start()
+        copies.append(part)
+    gq, eq, gd, ed = bufs
     per = CHUNK // LANES
     for ch in range(CHUNKS):
         for c in copies[ch]:
             c.wait()
-        for out, owner in ((send, 1 - core), (keep, core)):
-            rq = pl.ds(pl.multiple_of(owner * QH, QH), QH)
-            rd = pl.ds(pl.multiple_of(owner * DH, DH), DH)
-            for block in range(ch * per, (ch + 1) * per):
-                i, j = slot(owner, block)
-                cols = pl.ds(block * LANES, LANES)
-                out[i, j, 0:QH, :] = bq[rq, cols].astype(f32) + cq[rq, cols].astype(f32)
-                out[i, j, QH:HALF, :] = bd[rd, cols].astype(f32) + cd[rd, cols].astype(f32)
+        for block in range(ch * per, (ch + 1) * per):
+            i, j = slot(owner, block)
+            cols = pl.ds(block * LANES, LANES)
+            out[i, j, 0:QH, :] = gq[:, cols].astype(f32) + eq[:, cols].astype(f32)
+            out[i, j, QH:HALF, :] = gd[:, cols].astype(f32) + ed[:, cols].astype(f32)
+
+
+def send_kernel(gq, eq, gd, ed, out, bq, cq, bd, cd, sems):
+    merge_half(1 - lax.axis_index("core"), (gq, eq, gd, ed), out, (bq, cq, bd, cd), sems)
+
+
+def keep_kernel(gq, eq, gd, ed, out, bq, cq, bd, cd, sems):
+    merge_half(lax.axis_index("core"), (gq, eq, gd, ed), out, (bq, cq, bd, cd), sems)
+
+
+def sum_kernel(a, b, out, buf, sems):
+    copies = []
+    for i in range(8):
+        buf[i] = a[i] + b[i]
+        copies.append(pltpu.make_async_copy(buf.at[i], out.at[i], sems.at[i]))
+        copies[-1].start()
+    for c in copies:
+        c.wait()
 
 
 def factor_kernel(parts, q_all, s_ref, f_ref):
@@ -241,18 +256,15 @@
     half = shape(8, 8, HALF, LANES)
     bf16 = jnp.bfloat16
     grads = (grad_query[0], error_query[0], grad_down[0], error_down[0])
-    buffers = [pltpu.VMEM((n, WIDTH), bf16) for n in (2 * QH, 2 * QH, 2 * DH, 2 * DH)]
-    send, keep = call(
-        merge_kernel,
-        [HB] * 4,
-        (half, half),
-        (VM, VM),
-        buffers + [pltpu.SemaphoreType.DMA((CHUNKS, 4))],
-        moved=6 << 20,
-    )(*[pltpu.with_memory_space_constraint(g, pltpu.HBM) for g in grads])
-    other = swap_cores(send)
+    buffers = [pltpu.VMEM((n, WIDTH), bf16) for n in (QH, QH, DH, DH)]
+    buffers.append(pltpu.SemaphoreType.DMA((CHUNKS, 4)))
+    pinned = [pltpu.with_memory_space_constraint(g, pltpu.HBM) for g in grads]
+    other = swap_cores(call(send_kernel, [HB] * 4, half, VM, buffers, 3 << 20)(*pinned))
+    keep = call(keep_kernel, [HB] * 4, half, VM, buffers, 3 << 20)(*pinned)
+    staged = [pltpu.VMEM((8, 8, HALF, LANES), jnp.float32), pltpu.SemaphoreType.DMA((8,))]
+    total = call(sum_kernel, [VM] * 2, half, HB, staged, 5 << 20)(keep, other)
     qpack = jnp.concatenate([q_query.T, q_down.T], axis=1)
-    total, qpack = lax.optimization_barrier((keep + other, qpack))
+    total, qpack = lax.optimization_barrier((total, qpack))
     part = exchange(total, WIDE)
     qpack = jnp.stack([qpack, swap_cores(qpack)])
     q_all = jnp.stack([qpack] + [

time: 147 us -> 146 us (level)
  Pallas kernels: 8.28 us -> 10.7 us
  waiting for transfers between devices: 15.2 us -> 13.5 us
    pallas_call x1 -> x3, Pallas kernels: 2.11 us -> 4.53 us  [the longest x1 1.65 us: on_device(): call(send_kernel, [HB] * 4, half, VM, buffers, 3 << 20)(*pinned)]
    ppermute x3, waiting for transfers between devices: 6.01 us -> 4.35 us  [swap_cores(): return lax.ppermute(x, 'core', [(0, 1), (1, 0)])]
  transfers between devices with their start and end apart: 7 -> 7, of which waited for: 5 -> 5; matrix products, arithmetic and copies ran while one was open for 0% -> 0% of each run, Pallas kernels for 1% -> 2%
where the time goes in v5:
time: 146 us
  blocking collectives  89.2 us (61%)
  starting transfers between devices  31.1 us (21%)
  waiting for transfers between devices  13.5 us (9%)
  Pallas kernels  10.7 us (7%)
    all_to_all x5, blocking collectives, exchange(): return lax.all_to_all(x, AXES, 0, 0, axis_index_groups=groups, tiled=True)  72.2 us
    all_to_all x1, blocking collectives, on_device(): lax.all_to_all(jnp.broadcast_to(both[None], (8, PACK + HALF, LANES)), ('c...  17 us
    ppermute x3, starting transfers between devices, swap_cores(): return lax.ppermute(x, 'core', [(0, 1), (1, 0)])  15.3 us
    ppermute x3, starting transfers between devices, on_device(): lax.ppermute(qpack, 'x', [((x + k) % NX, x) for x in range(NX)])  11.1 us
    all_to_all x1, waiting for transfers between devices, exchange(): return lax.all_to_all(x, AXES, 0, 0, axis_index_groups=groups, tiled=True)  8.35 us
    all_to_all x1, starting transfers between devices, exchange(): return lax.all_to_all(x, AXES, 0, 0, axis_index_groups=groups, tiled=True)  4.67 us
    ppermute x3, waiting for transfers between devices, swap_cores(): return lax.ppermute(x, 'core', [(0, 1), (1, 0)])  4.35 us
    pallas_call x1, Pallas kernels, on_device(): call(solve_kernel, [VM], (shape(2 * QH, RANK), shape(2 * DH, RANK), shape...  3.9 us
  transfers between devices with their start and end apart: 7, of which 5 were waited for; matrix products, arithmetic and copies ran while one was open for 0% of the time, Pallas kernels for 2%

profile of v5, /device:TPU:1, one launch (start us, length us, event | category | flops | bytes accessed | tf_op | source)
XLA Modules:
  0.0 145.8 jit_solution(1301657122484335278)
XLA Ops:
  0.6 1.6 %shard_map.110 = f32[8,8,48,128]{3,2,1,0:T(8,128)S(1)} custom-call(bf16[32,8192]{1,0:T(8,128)(2,1)} %bitcast.25, bf16[32,8192]{1,0:T(8,128)(2,1)} %bitcast.29, bf16[64,8192]{1,0:T(8,128)(2,1)} %bitcast.17, bf16[64,8192]{1,0:T(8,128)(2,1)} %bitcast.21), custom_call_target="tpu_custom_call" | custom-call | flops 3145728 | bytes 3145728 | tf_op jit(solution)/shard_map/pallas_call | solution.py:262
  2.3 0.0 copy-start.4
  2.3 0.0 copy-start.5
  2.3 8.8 %collective-permute-start = (f32[8,8,48,128]{3,2,1,0:T(8,128)S(1)}, f32[8,8,48,128]{3,2,1,0:T(8,128)S(1)}, u32[]{:S(2)}, u32[]{:S(2)}) collective-permute-start(f32[8,8,48,128]{3,2,1,0:T(8,128)S(1)} %shard_map.110), channel_id=1, source_target_pairs={{0,4},{4,0},{1,5},{5,1},{2,6},{6,2},{3,7},{7,3},{8,12},{12,8},{9,1... | collective-permute-start | bytes 4718600 | tf_op jit(solution)/shard_map/ppermute | solution.py:252
  11.1 1.6 %shard_map.109.a = f32[8,8,48,128]{3,2,1,0:T(8,128)S(1)} custom-call(bf16[32,8192]{1,0:T(8,128)(2,1)} %bitcast.26, bf16[32,8192]{1,0:T(8,128)(2,1)} %bitcast.30, bf16[64,8192]{1,0:T(8,128)(2,1)} %bitcast.18, bf16[64,8192]{1,0:T(8,128)(2,1)} %bitcast.22), custom_call_target="tpu_custom_call" | custom-call | flops 3145728 | bytes 3145728 | tf_op jit(solution)/shard_map/pallas_call | solution.py:263
  12.8 0.1 pad_maximum_fusion.3
  12.9 1.3 collective-permute-done.b
  14.1 1.2 shard_map.111
  15.4 4.7 %all-to-all-start = ((f32[8,8,48,128]{3,2,1,0:T(8,128)}), f32[8,8,48,128]{3,2,1,0:T(8,128)S(1)}, u32[]{:S(2)}, u32[]{:S(2)}) async-start(f32[8,8,48,128]{3,2,1,0:T(8,128)} %shard_map.111), calls=%async_computation | async-start | bytes 3145728 | tf_op jit(solution)/shard_map/all_to_all | solution.py:43
  20.0 1.9 %collective-permute-start.1 = (f32[16,128]{1,0:T(8,128)S(1)}, f32[16,128]{1,0:T(8,128)S(1)}, u32[]{:S(2)}, u32[]{:S(2)}) collective-permute-start(f32[16,128]{1,0:T(8,128)S(1)} %pad_maximum_fusion.3), channel_id=1, source_target_pairs={{0,4},{4,0},{1,5},{5,1},{2,6},{6,2},{3,7},{7,3},{8,12},{12,8},{9,1... | collective-permute-start | bytes 24584 | tf_op jit(solution)/shard_map/ppermute | solution.py:252
  22.0 1.1 collective-permute-done.1
  23.1 4.6 %collective-permute-start.3 = (f32[2,16,128]{2,1,0:T(8,128)S(1)}, f32[2,16,128]{2,1,0:T(8,128)S(1)}, u32[]{:S(2)}, u32[]{:S(2)}) collective-permute-start(f32[2,16,128]{2,1,0:T(8,128)S(1)} %get-tuple-element.37), channel_id=1, source_target_pairs={{2,0},{3,1},{0,2},{1,3},{6,4},{7,5},{4,6},{5,7},{10,8},{11,9},{8,1... | collective-permute-start | bytes 49160 | tf_op jit(solution)/shard_map/ppermute | solution.py:271
  27.8 2.2 %collective-permute-start.4 = (f32[2,16,128]{2,1,0:T(8,128)S(1)}, f32[2,16,128]{2,1,0:T(8,128)S(1)}, u32[]{:S(2)}, u32[]{:S(2)}) collective-permute-start(f32[2,16,128]{2,1,0:T(8,128)S(1)} %get-tuple-element.37), channel_id=1, source_target_pairs={{3,0},{0,1},{1,2},{2,3},{7,4},{4,5},{5,6},{6,7},{11,8},{8,9},{9,10... | collective-permute-start | bytes 49160 | tf_op jit(solution)/shard_map/ppermute | solution.py:271
  30.0 4.3 %collective-permute-start.2 = (f32[2,16,128]{2,1,0:T(8,128)S(1)}, f32[2,16,128]{2,1,0:T(8,128)S(1)}, u32[]{:S(2)}, u32[]{:S(2)}) collective-permute-start(f32[2,16,128]{2,1,0:T(8,128)S(1)} %get-tuple-element.37), channel_id=1, source_target_pairs={{1,0},{2,1},{3,2},{0,3},{5,4},{6,5},{7,6},{4,7},{9,8},{10,9},{11,1... | collective-permute-start | bytes 49160 | tf_op jit(solution)/shard_map/ppermute | solution.py:271
  34.3 0.8 collective-permute-done.2
  35.1 8.4 %all-to-all-done = f32[8,8,48,128]{3,2,1,0:T(8,128)S(1)} async-done(((f32[8,8,48,128]{3,2,1,0:T(8,128)}), f32[8,8,48,128]{3,2,1,0:T(8,128)S(1)}, u32[]{:S(2)}, u32[]{:S(2)}) %all-to-all-start) | async-done | bytes 1572896 | tf_op jit(solution)/shard_map/all_to_all | solution.py:43
  43.5 0.1 reduce_sum.27
  43.6 15.2 %all_to_all.35.parts = f32[8,48,128]{2,1,0:T(8,128)S(1)} all-to-all(f32[8,48,128]{2,1,0:T(8,128)S(1)} %reduce_sum.27), channel_id=1, replica_groups={{0,64,128,192,256,320,384,448},{8,72,136,200,264,328,392,456},{16,80,14..., dimensions={0} | all-to-all | bytes 393216 | tf_op jit(solution)/shard_map/all_to_all | solution.py:43
  58.8 0.2 shard_map.112
  59.1 10.0 %all_to_all.36 = f32[8,24,128]{2,1,0:T(8,128)S(1)} all-to-all(f32[8,24,128]{2,1,0:T(8,128)S(1)} %get-tuple-element.25), channel_id=1, replica_groups={{0,64,128,192,256,320,384,448},{8,72,136,200,264,328,392,456},{16,80,14..., dimensions={0} | all-to-all | bytes 196608 | tf_op jit(solution)/shard_map/all_to_all | solution.py:43
  69.0 10.0 %all_to_all.37 = f32[8,24,128]{2,1,0:T(8,128)S(1)} all-to-all(f32[8,24,128]{2,1,0:T(8,128)S(1)} %broadcast_in_dim.10), channel_id=1, replica_groups={{0,8,16,24,32,40,48,56},{64,72,80,88,96,104,112,120},{128,136,144,152,1..., dimensions={0} | all-to-all | bytes 196608 | tf_op jit(solution)/shard_map/all_to_all | solution.py:43
  79.1 17.0 %all_to_all.38.all_ref = f32[8,72,128]{2,1,0:T(8,128)S(1)} all-to-all(f32[8,72,128]{2,1,0:T(8,128)S(1)} %broadcast_in_dim.11), channel_id=1, replica_groups=mesh['z'=8,'y'=8,'core'=2,'x'=4] {'core','x'}, dimensions={0} | all-to-all | bytes 589824 | tf_op jit(solution)/shard_map/all_to_all | solution.py:282
  96.0 3.9 %shard_map.113 = (f32[32,64]{1,0:T(8,128)}, f32[64,64]{1,0:T(8,128)}, f32[16,64]{1,0:T(8,128)}, f32[16,64]{1,0:T(8,128)}, f32[8,48,128]{2,1,0:T(8,128)S(1)}) custom-call(f32[8,72,128]{2,1,0:T(8,128)S(1)} %all_to_all.38.all_ref), custom_call_target="tpu_custom_call" | custom-call | flops 1048576 | bytes 1048576 | tf_op jit(solution)/shard_map/pallas_call | solution.py:285
  99.9 11.0 %all_to_all.39 = f32[8,48,128]{2,1,0:T(8,128)S(1)} all-to-all(f32[8,48,128]{2,1,0:T(8,128)S(1)} %get-tuple-element.27), channel_id=1, replica_groups={{0,64,128,192,256,320,384,448},{8,72,136,200,264,328,392,456},{16,80,14..., dimensions={0} | all-to-all | bytes 393216 | tf_op jit(solution)/shard_map/all_to_all | solution.py:43
  110.9 0.1 broadcast_in_dim.12
  111.1 0.0 copy-start
  111.1 0.0 copy-start.3
  111.1 26.1 %all_to_all.40.src = f32[8,8,48,128]{3,2,1,0:T(8,128)S(1)} all-to-all(f32[8,8,48,128]{3,2,1,0:T(8,128)S(1)} %broadcast_in_dim.12), channel_id=1, replica_groups={{0,8,16,24,32,40,48,56},{64,72,80,88,96,104,112,120},{128,136,144,152,1..., dimensions={0} | all-to-all | bytes 3145728 | tf_op jit(solution)/shard_map/all_to_all | solution.py:43
  137.2 4.6 %collective-permute-start.5 = (f32[8,8,48,128]{3,2,1,0:T(8,128)S(1)}, f32[8,8,48,128]{3,2,1,0:T(8,128)S(1)}, u32[]{:S(2)}, u32[]{:S(2)}) collective-permute-start(f32[8,8,48,128]{3,2,1,0:T(8,128)S(1)} %all_to_all.40.src), channel_id=1, source_target_pairs={{0,4},{4,0},{1,5},{5,1},{2,6},{6,2},{3,7},{7,3},{8,12},{12,8},{9,1... | collective-permute-start | bytes 4718600 | tf_op jit(solution)/shard_map/ppermute | solution.py:252
  141.8 1.0 shard_map.114
  142.8 1.9 %collective-permute-done.5.src = f32[8,8,48,128]{3,2,1,0:T(8,128)S(1)} collective-permute-done((f32[8,8,48,128]{3,2,1,0:T(8,128)S(1)}, f32[8,8,48,128]{3,2,1,0:T(8,128)S(1)}, u32[]{:S(2)}, u32[]{:S(2)}) %collective-permute-start.5) | collective-permute-done | bytes 1572896 | tf_op jit(solution)/shard_map/ppermute | solution.py:252
  144.8 1.0 shard_map.115
  (17 shorter events, 0.1 us)
Async XLA Ops:
  2.3 10.5 %copy-start.4 = (f32[64,16]{0,1:T(8,128)S(1)}, f32[64,16]{0,1:T(8,128)}, u32[]{:S(2)}) copy-start(f32[64,16]{0,1:T(8,128)} %param.11) | copy-start | bytes 12292
  2.3 10.5 %copy-start.5 = (f32[64,16]{0,1:T(8,128)S(1)}, f32[64,16]{0,1:T(8,128)}, u32[]{:S(2)}) copy-start(f32[64,16]{0,1:T(8,128)} %param.8) | copy-start | bytes 12292
  2.3 11.8 %collective-permute-start = (f32[8,8,48,128]{3,2,1,0:T(8,128)S(1)}, f32[8,8,48,128]{3,2,1,0:T(8,128)S(1)}, u32[]{:S(2)}, u32[]{:S(2)}) collective-permute-start(f32[8,8,48,128]{3,2,1,0:T(8,128)S(1)} %shard_map.110), channel_id=1, source_target_pairs={{0,4},{4,0},{1,5},{5,1},{2,6},{6,2},{3,7},{7,3},{8,12},{12,8},{9,1... | collective-permute-start | bytes 4718600 | tf_op jit(solution)/shard_map/ppermute | solution.py:252
  15.4 28.1 %all-to-all-start = ((f32[8,8,48,128]{3,2,1,0:T(8,128)}), f32[8,8,48,128]{3,2,1,0:T(8,128)S(1)}, u32[]{:S(2)}, u32[]{:S(2)}) async-start(f32[8,8,48,128]{3,2,1,0:T(8,128)} %shard_map.111), calls=%async_computation | async-start | bytes 3145728 | tf_op jit(solution)/shard_map/all_to_all | solution.py:43
  20.0 3.1 %collective-permute-start.1 = (f32[16,128]{1,0:T(8,128)S(1)}, f32[16,128]{1,0:T(8,128)S(1)}, u32[]{:S(2)}, u32[]{:S(2)}) collective-permute-start(f32[16,128]{1,0:T(8,128)S(1)} %pad_maximum_fusion.3), channel_id=1, source_target_pairs={{0,4},{4,0},{1,5},{5,1},{2,6},{6,2},{3,7},{7,3},{8,12},{12,8},{9,1... | collective-permute-start | bytes 24584 | tf_op jit(solution)/shard_map/ppermute | solution.py:252
  23.1 11.2 %collective-permute-start.3 = (f32[2,16,128]{2,1,0:T(8,128)S(1)}, f32[2,16,128]{2,1,0:T(8,128)S(1)}, u32[]{:S(2)}, u32[]{:S(2)}) collective-permute-start(f32[2,16,128]{2,1,0:T(8,128)S(1)} %get-tuple-element.37), channel_id=1, source_target_pairs={{2,0},{3,1},{0,2},{1,3},{6,4},{7,5},{4,6},{5,7},{10,8},{11,9},{8,1... | collective-permute-start | bytes 49160 | tf_op jit(solution)/shard_map/ppermute | solution.py:271
  27.8 6.5 %collective-permute-start.4 = (f32[2,16,128]{2,1,0:T(8,128)S(1)}, f32[2,16,128]{2,1,0:T(8,128)S(1)}, u32[]{:S(2)}, u32[]{:S(2)}) collective-permute-start(f32[2,16,128]{2,1,0:T(8,128)S(1)} %get-tuple-element.37), channel_id=1, source_target_pairs={{3,0},{0,1},{1,2},{2,3},{7,4},{4,5},{5,6},{6,7},{11,8},{8,9},{9,10... | collective-permute-start | bytes 49160 | tf_op jit(solution)/shard_map/ppermute | solution.py:271
  30.0 5.1 %collective-permute-start.2 = (f32[2,16,128]{2,1,0:T(8,128)S(1)}, f32[2,16,128]{2,1,0:T(8,128)S(1)}, u32[]{:S(2)}, u32[]{:S(2)}) collective-permute-start(f32[2,16,128]{2,1,0:T(8,128)S(1)} %get-tuple-element.37), channel_id=1, source_target_pairs={{1,0},{2,1},{3,2},{0,3},{5,4},{6,5},{7,6},{4,7},{9,8},{10,9},{11,1... | collective-permute-start | bytes 49160 | tf_op jit(solution)/shard_map/ppermute | solution.py:271
  111.1 30.7 %copy-start = (bf16[1,64,8192]{2,1,0:T(8,128)(2,1)S(1)}, bf16[1,64,8192]{2,1,0:T(8,128)(2,1)}, u32[]{:S(2)}) copy-start(bf16[1,64,8192]{2,1,0:T(8,128)(2,1)} %param.9) | copy-start | bytes 3145732
  111.1 30.7 %copy-start.1 = (bf16[1,64,8192]{2,1,0:T(8,128)(2,1)S(1)}, bf16[1,64,8192]{2,1,0:T(8,128)(2,1)}, u32[]{:S(2)}) copy-start(bf16[1,64,8192]{2,1,0:T(8,128)(2,1)} %param.10) | copy-start | bytes 3145732
  111.1 30.7 %copy-start.2 = (bf16[1,32,8192]{2,1,0:T(8,128)(2,1)S(1)}, bf16[1,32,8192]{2,1,0:T(8,128)(2,1)}, u32[]{:S(2)}) copy-start(bf16[1,32,8192]{2,1,0:T(8,128)(2,1)} %param.6) | copy-start | bytes 1572868
  111.1 30.7 %copy-start.3 = (bf16[1,32,8192]{2,1,0:T(8,128)(2,1)S(1)}, bf16[1,32,8192]{2,1,0:T(8,128)(2,1)}, u32[]{:S(2)}) copy-start(bf16[1,32,8192]{2,1,0:T(8,128)(2,1)} %param.7) | copy-start | bytes 1572868
  137.2 7.6 %collective-permute-start.5 = (f32[8,8,48,128]{3,2,1,0:T(8,128)S(1)}, f32[8,8,48,128]{3,2,1,0:T(8,128)S(1)}, u32[]{:S(2)}, u32[]{:S(2)}) collective-permute-start(f32[8,8,48,128]{3,2,1,0:T(8,128)S(1)} %all_to_all.40.src), channel_id=1, source_target_pairs={{0,4},{4,0},{1,5},{5,1},{2,6},{6,2},{3,7},{7,3},{8,12},{12,8},{9,1... | collective-permute-start | bytes 4718600 | tf_op jit(solution)/shard_map/ppermute | solution.py:252

commit v6 on v5

--- a/solution.py
+++ b/solution.py
@@ -23,7 +23,7 @@
     return ((z * NY + y) * NC + core) * NX + x
 
 
-def split_groups(core_along_y):
+def ring_groups(core_along_y):
     groups = []
     for core in range(NC):
         for x in range(NX):
@@ -35,17 +35,41 @@
     return groups
 
 
-WIDE = split_groups(0)
-NARROW = split_groups(1)
+def near_groups():
+    groups = []
+    for core in range(NC):
+        for x in range(NX):
+            for z in range(core, NZ + core, 2):
+                for y in range(core, NY + core, 2):
+                    block = [((z + i) % NZ, (y + j) % NY) for i in range(2) for j in range(2)]
+                    block.sort(key=lambda zy: (zy[0] % 2, zy[1] % 2))
+                    groups.append([device_of(z_, y_, core, x) for z_, y_ in block])
+    return groups
+
+
+def far_groups():
+    return [
+        [device_of(z, y, core, x) for z in range(a, NZ, 2) for y in range(b, NY, 2)]
+        for core in range(NC)
+        for x in range(NX)
+        for a in range(2)
+        for b in range(2)
+    ]
+
+
+RING_A = ring_groups(1)
+RING_B = ring_groups(0)
+NEAR = near_groups()
+FAR = far_groups()
 
 
 def exchange(x, groups):
     return lax.all_to_all(x, AXES, 0, 0, axis_index_groups=groups, tiled=True)
 
 
-def slot(owner, block):
+def slot(block):
     z, y = divmod(block, NY)
-    return jnp.where(owner == 0, y, z), jnp.where(owner == 0, z, y)
+    return z % 2 * 2 + y % 2, z // 2 * 4 + y // 2
 
 
 def merge_half(owner, sources, out, bufs, sems):
@@ -66,7 +90,7 @@
         for c in copies[ch]:
             c.wait()
         for block in range(ch * per, (ch + 1) * per):
-            i, j = slot(owner, block)
+            i, j = slot(block)
             cols = pl.ds(block * LANES, LANES)
             out[i, j, 0:QH, :] = gq[:, cols].astype(f32) + eq[:, cols].astype(f32)
             out[i, j, QH:HALF, :] = gd[:, cols].astype(f32) + ed[:, cols].astype(f32)
@@ -80,19 +104,9 @@
     merge_half(lax.axis_index("core"), (gq, eq, gd, ed), out, (bq, cq, bd, cd), sems)
 
 
-def sum_kernel(a, b, out, buf, sems):
-    copies = []
-    for i in range(8):
-        buf[i] = a[i] + b[i]
-        copies.append(pltpu.make_async_copy(buf.at[i], out.at[i], sems.at[i]))
-        copies[-1].start()
-    for c in copies:
-        c.wait()
-
-
 def factor_kernel(parts, q_all, s_ref, f_ref):
     s = parts[0]
-    for i in range(1, 8):
+    for i in range(1, 16):
         s = s + parts[i]
     s_ref[...] = s
     core, x = lax.axis_index("core"), lax.axis_index("x")
@@ -192,7 +206,7 @@
         basis_d[c * DH:(c + 1) * DH, :] = pltpu.roll(b[QH:HALF], RANK, 1)[:, 0:RANK]
     mine = jnp.where(core == 0, halves[0], halves[1])
     a = contract(mine, qn, lanes)
-    for i in range(8):
+    for i in range(16):
         approx[i] = a
 
 
@@ -204,7 +218,7 @@
     copies = []
     for ch in range(CHUNKS):
         for block in range(ch * per, (ch + 1) * per):
-            i, j = slot(owner, block)
+            i, j = slot(block)
             cols = pl.ds(block * LANES, LANES)
             mq = gq[rq, cols].astype(f32) + eq[rq, cols].astype(f32)
             md = gd[rd, cols].astype(f32) + ed[rd, cols].astype(f32)
@@ -253,7 +267,7 @@
 
 
 def on_device(grad_query, error_query, q_query, grad_down, error_down, q_down):
-    half = shape(8, 8, HALF, LANES)
+    half = shape(4, 16, HALF, LANES)
     bf16 = jnp.bfloat16
     grads = (grad_query[0], error_query[0], grad_down[0], error_down[0])
     buffers = [pltpu.VMEM((n, WIDTH), bf16) for n in (QH, QH, DH, DH)]
@@ -261,23 +275,21 @@
     pinned = [pltpu.with_memory_space_constraint(g, pltpu.HBM) for g in grads]
     other = swap_cores(call(send_kernel, [HB] * 4, half, VM, buffers, 3 << 20)(*pinned))
     keep = call(keep_kernel, [HB] * 4, half, VM, buffers, 3 << 20)(*pinned)
-    staged = [pltpu.VMEM((8, 8, HALF, LANES), jnp.float32), pltpu.SemaphoreType.DMA((8,))]
-    total = call(sum_kernel, [VM] * 2, half, HB, staged, 5 << 20)(keep, other)
     qpack = jnp.concatenate([q_query.T, q_down.T], axis=1)
-    total, qpack = lax.optimization_barrier((total, qpack))
-    part = exchange(total, WIDE)
     qpack = jnp.stack([qpack, swap_cores(qpack)])
+    total, qpack = lax.optimization_barrier((keep + other, qpack))
+    part = exchange(total, NEAR)
     q_all = jnp.stack([qpack] + [
         lax.ppermute(qpack, "x", [((x + k) % NX, x) for x in range(NX)]) for k in range(1, NX)
     ])
     part, q_all = lax.optimization_barrier((part, q_all))
-    part = exchange(jnp.sum(part, axis=0), NARROW)
+    part = exchange(jnp.sum(part, axis=0), FAR)
     s_own, f = call(
         factor_kernel, [VM, VM], (shape(HALF, LANES), shape(8, PACK, LANES)), (VM, VM), moved=1 << 18
     )(part, q_all)
-    f = exchange(f, NARROW)
+    f = exchange(f, RING_A)
     f = jnp.broadcast_to(jnp.sum(f, axis=0)[None], (8, PACK, LANES))
-    f = jnp.sum(exchange(f, WIDE), axis=0)
+    f = jnp.sum(exchange(f, RING_B), axis=0)
     both = jnp.concatenate([f, s_own], axis=0)
     both = lax.all_to_all(
         jnp.broadcast_to(both[None], (8, PACK + HALF, LANES)), ("core", "x"), 0, 0, tiled=True
@@ -285,13 +297,13 @@
     basis_q, basis_d, qn_q, qn_d, approx = call(
         solve_kernel,
         [VM],
-        (shape(2 * QH, RANK), shape(2 * DH, RANK), shape(16, RANK), shape(16, RANK), shape(8, HALF, LANES)),
+        (shape(2 * QH, RANK), shape(2 * DH, RANK), shape(16, RANK), shape(16, RANK), shape(16, HALF, LANES)),
         (VM,) * 5,
         [pltpu.VMEM((2, LANES, LANES), jnp.float32)],
         moved=1 << 20,
     )(both)
-    approx = exchange(approx, NARROW)
-    own = exchange(jnp.broadcast_to(approx[None], (8, 8, HALF, LANES)), WIDE)
+    approx = exchange(approx, FAR)
+    own = exchange(jnp.broadcast_to(approx[None], half.shape), NEAR)
     other = swap_cores(own)
     errors = (shape(2 * QH, WIDTH, dtype=bf16), shape(2 * DH, WIDTH, dtype=bf16))
     bufs = [pltpu.VMEM((n, WIDTH), bf16) for n in (QH, DH)] + [pltpu.SemaphoreType.DMA((CHUNKS, 2))]

time: 146 us -> 144 us (0.986)
  waiting for transfers between devices: 13.5 us -> 3.1 us
  blocking collectives: 89.2 us -> 96 us
    all_to_all x1, waiting for transfers between devices: 8.35 us -> 0.29 us  [exchange(): return lax.all_to_all(x, AXES, 0, 0, axis_index_groups=groups, tiled=True)]
    all_to_all x5, blocking collectives: 72.2 us -> 79.1 us  [exchange(): return lax.all_to_all(x, AXES, 0, 0, axis_index_groups=groups, tiled=True)]
    all_to_all x1, starting transfers between devices: 4.67 us -> 7.56 us  [exchange(): return lax.all_to_all(x, AXES, 0, 0, axis_index_groups=groups, tiled=True)]
    ppermute x3, waiting for transfers between devices: 4.35 us -> 1.98 us  [swap_cores(): return lax.ppermute(x, 'core', [(0, 1), (1, 0)])]
    ppermute x3, starting transfers between devices: 15.3 us -> 13.2 us  [swap_cores(): return lax.ppermute(x, 'core', [(0, 1), (1, 0)])]
  transfers between devices with their start and end apart: 7 -> 7, of which waited for: 5 -> 3; matrix products, arithmetic and copies ran while one was open for 0% -> 0% of each run, Pallas kernels for 2% -> 2%
where the time goes in v6:
time: 144 us; the launch traced here: 143 us
  blocking collectives  96 us (67%)
  starting transfers between devices  31.9 us (22%)
  Pallas kernels  9.41 us (7%)
  waiting for transfers between devices  3.1 us (2%)
  other arithmetic  1.63 us (1%)
    all_to_all x5, blocking collectives, exchange(): return lax.all_to_all(x, AXES, 0, 0, axis_index_groups=groups, tiled=True)  79.1 us
    all_to_all x1, blocking collectives, on_device(): lax.all_to_all(jnp.broadcast_to(both[None], (8, PACK + HALF, LANES)), ('c...  16.8 us
    ppermute x3, starting transfers between devices, swap_cores(): return lax.ppermute(x, 'core', [(0, 1), (1, 0)])  13.2 us
    ppermute x3, starting transfers between devices, on_device(): lax.ppermute(qpack, 'x', [((x + k) % NX, x) for x in range(NX)])  11.1 us
    all_to_all x1, starting transfers between devices, exchange(): return lax.all_to_all(x, AXES, 0, 0, axis_index_groups=groups, tiled=True)  7.56 us
    pallas_call x1, Pallas kernels, on_device(): call(solve_kernel, [VM], (shape(2 * QH, RANK), shape(2 * DH, RANK), shape...  3.9 us
  transfers between devices with their start and end apart: 7, of which 3 were waited for; matrix products, arithmetic and copies ran while one was open for 0% of the time, Pallas kernels for 2%

profile of v6, /device:TPU:1, one launch (start us, length us, event | category | flops | bytes accessed | tf_op | source)
XLA Modules:
  0.0 143.1 jit_solution(17081101171188563241)
XLA Ops:
  0.7 1.6 %shard_map.110 = f32[4,16,48,128]{3,2,1,0:T(8,128)S(1)} custom-call(bf16[32,8192]{1,0:T(8,128)(2,1)} %bitcast.25, bf16[32,8192]{1,0:T(8,128)(2,1)} %bitcast.29, bf16[64,8192]{1,0:T(8,128)(2,1)} %bitcast.17, bf16[64,8192]{1,0:T(8,128)(2,1)} %bitcast.21), custom_call_target="tpu_custom_call" | custom-call | flops 3145728 | bytes 3145728 | tf_op jit(solution)/shard_map/pallas_call | solution.py:276
  2.3 8.8 %collective-permute-start = (f32[4,16,48,128]{3,2,1,0:T(8,128)S(1)}, f32[4,16,48,128]{3,2,1,0:T(8,128)S(1)}, u32[]{:S(2)}, u32[]{:S(2)}) collective-permute-start(f32[4,16,48,128]{3,2,1,0:T(8,128)S(1)} %shard_map.110), channel_id=1, source_target_pairs={{0,4},{4,0},{1,5},{5,1},{2,6},{6,2},{3,7},{7,3},{8,12},{12,8},{9,1... | collective-permute-start | bytes 4718600 | tf_op jit(solution)/shard_map/ppermute | solution.py:266
  11.1 0.1 pad_maximum_fusion.3
  11.2 1.9 %collective-permute-start.1 = (f32[16,128]{1,0:T(8,128)S(1)}, f32[16,128]{1,0:T(8,128)S(1)}, u32[]{:S(2)}, u32[]{:S(2)}) collective-permute-start(f32[16,128]{1,0:T(8,128)S(1)} %pad_maximum_fusion.3), channel_id=1, source_target_pairs={{0,4},{4,0},{1,5},{5,1},{2,6},{6,2},{3,7},{7,3},{8,12},{12,8},{9,1... | collective-permute-start | bytes 24584 | tf_op jit(solution)/shard_map/ppermute | solution.py:266
  13.1 0.1 fusion
  13.2 1.6 %shard_map.109 = f32[4,16,48,128]{3,2,1,0:T(8,128)S(1)} custom-call(bf16[32,8192]{1,0:T(8,128)(2,1)} %bitcast.26, bf16[32,8192]{1,0:T(8,128)(2,1)} %bitcast.30, bf16[64,8192]{1,0:T(8,128)(2,1)} %bitcast.18, bf16[64,8192]{1,0:T(8,128)(2,1)} %bitcast.22), custom_call_target="tpu_custom_call" | custom-call | flops 3145728 | bytes 3145728 | tf_op jit(solution)/shard_map/pallas_call | solution.py:277
  14.8 0.0 collective-permute-done.1
  14.9 1.3 add.3
  16.2 7.6 %all-to-all-start = ((f32[4,16,48,128]{3,2,1,0:T(8,128)}), f32[4,16,48,128]{3,2,1,0:T(8,128)S(1)}, u32[]{:S(2)}, u32[]{:S(2)}) async-start(f32[4,16,48,128]{3,2,1,0:T(8,128)} %add.3), calls=%async_computation | async-start | bytes 3145728 | tf_op jit(solution)/shard_map/all_to_all | solution.py:67
  23.8 4.6 %collective-permute-start.3 = (f32[2,16,128]{2,1,0:T(8,128)S(1)}, f32[2,16,128]{2,1,0:T(8,128)S(1)}, u32[]{:S(2)}, u32[]{:S(2)}) collective-permute-start(f32[2,16,128]{2,1,0:T(8,128)S(1)} %pad_maximum_fusion.2), channel_id=1, source_target_pairs={{2,0},{3,1},{0,2},{1,3},{6,4},{7,5},{4,6},{5,7},{10,8},{11,9},{8,1... | collective-permute-start | bytes 49160 | tf_op jit(solution)/shard_map/ppermute | solution.py:283
  28.4 2.2 %collective-permute-start.4 = (f32[2,16,128]{2,1,0:T(8,128)S(1)}, f32[2,16,128]{2,1,0:T(8,128)S(1)}, u32[]{:S(2)}, u32[]{:S(2)}) collective-permute-start(f32[2,16,128]{2,1,0:T(8,128)S(1)} %pad_maximum_fusion.2), channel_id=1, source_target_pairs={{3,0},{0,1},{1,2},{2,3},{7,4},{4,5},{5,6},{6,7},{11,8},{8,9},{9,10... | collective-permute-start | bytes 49160 | tf_op jit(solution)/shard_map/ppermute | solution.py:283
  30.6 4.3 %collective-permute-start.2 = (f32[2,16,128]{2,1,0:T(8,128)S(1)}, f32[2,16,128]{2,1,0:T(8,128)S(1)}, u32[]{:S(2)}, u32[]{:S(2)}) collective-permute-start(f32[2,16,128]{2,1,0:T(8,128)S(1)} %pad_maximum_fusion.2), channel_id=1, source_target_pairs={{1,0},{2,1},{3,2},{0,3},{5,4},{6,5},{7,6},{4,7},{9,8},{10,9},{11,1... | collective-permute-start | bytes 49160 | tf_op jit(solution)/shard_map/ppermute | solution.py:283
  34.9 0.8 collective-permute-done.2
  35.8 0.3 all-to-all-done
  36.1 0.1 reduce_sum.27
  36.2 20.4 %all_to_all.35.parts = f32[16,48,128]{2,1,0:T(8,128)S(1)} all-to-all(f32[16,48,128]{2,1,0:T(8,128)S(1)} %reduce_sum.27), channel_id=1, replica_groups={{0,16,32,48,128,144,160,176,256,272,288,304,384,400,416,432},{8,24,40,5..., dimensions={0} | all-to-all | bytes 786432 | tf_op jit(solution)/shard_map/all_to_all | solution.py:67
  56.6 0.2 shard_map.111
  56.8 13.6 %all_to_all.36 = f32[8,24,128]{2,1,0:T(8,128)S(1)} all-to-all(f32[8,24,128]{2,1,0:T(8,128)S(1)} %get-tuple-element.25), channel_id=1, replica_groups={{0,64,128,192,256,320,384,448},{8,72,136,200,264,328,392,456},{16,80,14..., dimensions={0} | all-to-all | bytes 196608 | tf_op jit(solution)/shard_map/all_to_all | solution.py:67
  70.5 10.0 %all_to_all.37 = f32[8,24,128]{2,1,0:T(8,128)S(1)} all-to-all(f32[8,24,128]{2,1,0:T(8,128)S(1)} %broadcast_in_dim.10), channel_id=1, replica_groups={{0,8,16,24,32,40,48,56},{64,72,80,88,96,104,112,120},{128,136,144,152,1..., dimensions={0} | all-to-all | bytes 196608 | tf_op jit(solution)/shard_map/all_to_all | solution.py:67
  80.5 16.8 %all_to_all.38.all_ref = f32[8,72,128]{2,1,0:T(8,128)S(1)} all-to-all(f32[8,72,128]{2,1,0:T(8,128)S(1)} %broadcast_in_dim.11), channel_id=1, replica_groups=mesh['z'=8,'y'=8,'core'=2,'x'=4] {'core','x'}, dimensions={0} | all-to-all | bytes 589824 | tf_op jit(solution)/shard_map/all_to_all | solution.py:294
  97.3 3.9 %shard_map.112 = (f32[32,64]{1,0:T(8,128)}, f32[64,64]{1,0:T(8,128)}, f32[16,64]{1,0:T(8,128)}, f32[16,64]{1,0:T(8,128)}, f32[16,48,128]{2,1,0:T(8,128)S(1)}) custom-call(f32[8,72,128]{2,1,0:T(8,128)S(1)} %all_to_all.38.all_ref), custom_call_target="tpu_custom_call" | custom-call | flops 1048576 | bytes 1048576 | tf_op jit(solution)/shard_map/pallas_call | solution.py:297
  101.2 18.5 %all_to_all.39 = f32[16,48,128]{2,1,0:T(8,128)S(1)} all-to-all(f32[16,48,128]{2,1,0:T(8,128)S(1)} %get-tuple-element.27), channel_id=1, replica_groups={{0,16,32,48,128,144,160,176,256,272,288,304,384,400,416,432},{8,24,40,5..., dimensions={0} | all-to-all | bytes 786432 | tf_op jit(solution)/shard_map/all_to_all | solution.py:67
  119.7 0.1 broadcast_in_dim.12
  119.8 0.0 copy-start
  119.8 0.0 copy-start.1
  119.8 0.0 copy-start.2
  119.8 0.0 copy-start.3
  119.8 16.7 %all_to_all.40.src = f32[4,16,48,128]{3,2,1,0:T(8,128)S(1)} all-to-all(f32[4,16,48,128]{3,2,1,0:T(8,128)S(1)} %broadcast_in_dim.12), channel_id=1, replica_groups={{0,8,64,72},{16,24,80,88},{32,40,96,104},{48,56,112,120},{128,136,192,2..., dimensions={0} | all-to-all | bytes 3145728 | tf_op jit(solution)/shard_map/all_to_all | solution.py:67
  136.6 2.5 %collective-permute-start.5 = (f32[4,16,48,128]{3,2,1,0:T(8,128)S(1)}, f32[4,16,48,128]{3,2,1,0:T(8,128)S(1)}, u32[]{:S(2)}, u32[]{:S(2)}) collective-permute-start(f32[4,16,48,128]{3,2,1,0:T(8,128)S(1)} %all_to_all.40.src), channel_id=1, source_target_pairs={{0,4},{4,0},{1,5},{5,1},{2,6},{6,2},{3,7},{7,3},{8,12},{12,8},{9,1... | collective-permute-start | bytes 4718600 | tf_op jit(solution)/shard_map/ppermute | solution.py:266
  139.1 1.0 shard_map.113
  140.1 2.0 %collective-permute-done.5.src = f32[4,16,48,128]{3,2,1,0:T(8,128)S(1)} collective-permute-done((f32[4,16,48,128]{3,2,1,0:T(8,128)S(1)}, f32[4,16,48,128]{3,2,1,0:T(8,128)S(1)}, u32[]{:S(2)}, u32[]{:S(2)}) %collective-permute-start.5) | collective-permute-done | bytes 1572896 | tf_op jit(solution)/shard_map/ppermute | solution.py:266
  142.1 1.0 shard_map.114
  (18 shorter events, 0.1 us)
Async XLA Ops:
  0.6 10.5 %copy-start.4 = (f32[64,16]{0,1:T(8,128)S(1)}, f32[64,16]{0,1:T(8,128)}, u32[]{:S(2)}) copy-start(f32[64,16]{0,1:T(8,128)} %param.11) | copy-start | bytes 12292
  0.6 10.5 %copy-start.5 = (f32[64,16]{0,1:T(8,128)S(1)}, f32[64,16]{0,1:T(8,128)}, u32[]{:S(2)}) copy-start(f32[64,16]{0,1:T(8,128)} %param.8) | copy-start | bytes 12292
  2.3 12.6 %collective-permute-start = (f32[4,16,48,128]{3,2,1,0:T(8,128)S(1)}, f32[4,16,48,128]{3,2,1,0:T(8,128)S(1)}, u32[]{:S(2)}, u32[]{:S(2)}) collective-permute-start(f32[4,16,48,128]{3,2,1,0:T(8,128)S(1)} %shard_map.110), channel_id=1, source_target_pairs={{0,4},{4,0},{1,5},{5,1},{2,6},{6,2},{3,7},{7,3},{8,12},{12,8},{9,1... | collective-permute-start | bytes 4718600 | tf_op jit(solution)/shard_map/ppermute | solution.py:266
  11.2 3.6 %collective-permute-start.1 = (f32[16,128]{1,0:T(8,128)S(1)}, f32[16,128]{1,0:T(8,128)S(1)}, u32[]{:S(2)}, u32[]{:S(2)}) collective-permute-start(f32[16,128]{1,0:T(8,128)S(1)} %pad_maximum_fusion.3), channel_id=1, source_target_pairs={{0,4},{4,0},{1,5},{5,1},{2,6},{6,2},{3,7},{7,3},{8,12},{12,8},{9,1... | collective-permute-start | bytes 24584 | tf_op jit(solution)/shard_map/ppermute | solution.py:266
  16.2 19.9 %all-to-all-start = ((f32[4,16,48,128]{3,2,1,0:T(8,128)}), f32[4,16,48,128]{3,2,1,0:T(8,128)S(1)}, u32[]{:S(2)}, u32[]{:S(2)}) async-start(f32[4,16,48,128]{3,2,1,0:T(8,128)} %add.3), calls=%async_computation | async-start | bytes 3145728 | tf_op jit(solution)/shard_map/all_to_all | solution.py:67
  23.8 11.2 %collective-permute-start.3 = (f32[2,16,128]{2,1,0:T(8,128)S(1)}, f32[2,16,128]{2,1,0:T(8,128)S(1)}, u32[]{:S(2)}, u32[]{:S(2)}) collective-permute-start(f32[2,16,128]{2,1,0:T(8,128)S(1)} %pad_maximum_fusion.2), channel_id=1, source_target_pairs={{2,0},{3,1},{0,2},{1,3},{6,4},{7,5},{4,6},{5,7},{10,8},{11,9},{8,1... | collective-permute-start | bytes 49160 | tf_op jit(solution)/shard_map/ppermute | solution.py:283
  28.4 6.5 %collective-permute-start.4 = (f32[2,16,128]{2,1,0:T(8,128)S(1)}, f32[2,16,128]{2,1,0:T(8,128)S(1)}, u32[]{:S(2)}, u32[]{:S(2)}) collective-permute-start(f32[2,16,128]{2,1,0:T(8,128)S(1)} %pad_maximum_fusion.2), channel_id=1, source_target_pairs={{3,0},{0,1},{1,2},{2,3},{7,4},{4,5},{5,6},{6,7},{11,8},{8,9},{9,10... | collective-permute-start | bytes 49160 | tf_op jit(solution)/shard_map/ppermute | solution.py:283
  30.6 5.1 %collective-permute-start.2 = (f32[2,16,128]{2,1,0:T(8,128)S(1)}, f32[2,16,128]{2,1,0:T(8,128)S(1)}, u32[]{:S(2)}, u32[]{:S(2)}) collective-permute-start(f32[2,16,128]{2,1,0:T(8,128)S(1)} %pad_maximum_fusion.2), channel_id=1, source_target_pairs={{1,0},{2,1},{3,2},{0,3},{5,4},{6,5},{7,6},{4,7},{9,8},{10,9},{11,1... | collective-permute-start | bytes 49160 | tf_op jit(solution)/shard_map/ppermute | solution.py:283
  119.8 19.3 %copy-start = (bf16[1,64,8192]{2,1,0:T(8,128)(2,1)S(1)}, bf16[1,64,8192]{2,1,0:T(8,128)(2,1)}, u32[]{:S(2)}) copy-start(bf16[1,64,8192]{2,1,0:T(8,128)(2,1)} %param.9) | copy-start | bytes 3145732
  119.8 19.3 %copy-start.1 = (bf16[1,64,8192]{2,1,0:T(8,128)(2,1)S(1)}, bf16[1,64,8192]{2,1,0:T(8,128)(2,1)}, u32[]{:S(2)}) copy-start(bf16[1,64,8192]{2,1,0:T(8,128)(2,1)} %param.10) | copy-start | bytes 3145732
  119.8 19.3 %copy-start.2 = (bf16[1,32,8192]{2,1,0:T(8,128)(2,1)S(1)}, bf16[1,32,8192]{2,1,0:T(8,128)(2,1)}, u32[]{:S(2)}) copy-start(bf16[1,32,8192]{2,1,0:T(8,128)(2,1)} %param.6) | copy-start | bytes 1572868
  119.8 19.3 %copy-start.3 = (bf16[1,32,8192]{2,1,0:T(8,128)(2,1)S(1)}, bf16[1,32,8192]{2,1,0:T(8,128)(2,1)}, u32[]{:S(2)}) copy-start(bf16[1,32,8192]{2,1,0:T(8,128)(2,1)} %param.7) | copy-start | bytes 1572868
  136.6 5.5 %collective-permute-start.5 = (f32[4,16,48,128]{3,2,1,0:T(8,128)S(1)}, f32[4,16,48,128]{3,2,1,0:T(8,128)S(1)}, u32[]{:S(2)}, u32[]{:S(2)}) collective-permute-start(f32[4,16,48,128]{3,2,1,0:T(8,128)S(1)} %all_to_all.40.src), channel_id=1, source_target_pairs={{0,4},{4,0},{1,5},{5,1},{2,6},{6,2},{3,7},{7,3},{8,12},{12,8},{9,1... | collective-permute-start | bytes 4718600 | tf_op jit(solution)/shard_map/ppermute | solution.py:266

commit v7 on v6

--- a/solution.py
+++ b/solution.py
@@ -14,8 +14,9 @@
 PACK = HALF // 2
 HIGH = lax.Precision.HIGHEST
 WIDTH = 8192
-CHUNK = 2048
+CHUNK = 4096
 CHUNKS = WIDTH // CHUNK
+ROWS = NZ * NY * HALF
 MIB = 1024 * 1024
 
 
@@ -91,13 +92,20 @@
             c.wait()
         for block in range(ch * per, (ch + 1) * per):
             i, j = slot(block)
+            at = (i * 16 + j) * HALF
             cols = pl.ds(block * LANES, LANES)
-            out[i, j, 0:QH, :] = gq[:, cols].astype(f32) + eq[:, cols].astype(f32)
-            out[i, j, QH:HALF, :] = gd[:, cols].astype(f32) + ed[:, cols].astype(f32)
-
-
-def send_kernel(gq, eq, gd, ed, out, bq, cq, bd, cd, sems):
+            out[at:at + QH, :] = gq[:, cols].astype(f32) + eq[:, cols].astype(f32)
+            out[at + QH:at + HALF, :] = gd[:, cols].astype(f32) + ed[:, cols].astype(f32)
+
+
+def send_kernel(gq, eq, gd, ed, qq, qd, out, bq, cq, bd, cd, sems, qbuf, qsems):
+    copies = [pltpu.make_async_copy(r, qbuf.at[k], qsems.at[k]) for k, r in enumerate((qq, qd))]
+    for c in copies:
+        c.start()
     merge_half(1 - lax.axis_index("core"), (gq, eq, gd, ed), out, (bq, cq, bd, cd), sems)
+    for c in copies:
+        c.wait()
+    out[ROWS:ROWS + 16, :] = jnp.concatenate([qbuf[0], qbuf[1]], axis=1)
 
 
 def keep_kernel(gq, eq, gd, ed, out, bq, cq, bd, cd, sems):
@@ -273,11 +281,16 @@
     buffers = [pltpu.VMEM((n, WIDTH), bf16) for n in (QH, QH, DH, DH)]
     buffers.append(pltpu.SemaphoreType.DMA((CHUNKS, 4)))
     pinned = [pltpu.with_memory_space_constraint(g, pltpu.HBM) for g in grads]
-    other = swap_cores(call(send_kernel, [HB] * 4, half, VM, buffers, 3 << 20)(*pinned))
-    keep = call(keep_kernel, [HB] * 4, half, VM, buffers, 3 << 20)(*pinned)
+    pinned_q = [pltpu.with_memory_space_constraint(q.T, pltpu.HBM) for q in (q_query, q_down)]
+    q_buffers = [pltpu.VMEM((2, 16, RANK), jnp.float32), pltpu.SemaphoreType.DMA((2,))]
+    sent = call(
+        send_kernel, [HB] * 6, shape(ROWS + 16, LANES), VM, buffers + q_buffers, moved=3 << 20
+    )(*pinned, *pinned_q)
+    other = swap_cores(sent)
+    keep = call(keep_kernel, [HB] * 4, shape(ROWS, LANES), VM, buffers, moved=3 << 20)(*pinned)
     qpack = jnp.concatenate([q_query.T, q_down.T], axis=1)
-    qpack = jnp.stack([qpack, swap_cores(qpack)])
-    total, qpack = lax.optimization_barrier((keep + other, qpack))
+    qpack = jnp.stack([qpack, other[ROWS:]])
+    total, qpack = lax.optimization_barrier(((keep + other[:ROWS]).reshape(half.shape), qpack))
     part = exchange(total, NEAR)
     q_all = jnp.stack([qpack] + [
         lax.ppermute(qpack, "x", [((x + k) % NX, x) for x in range(NX)]) for k in range(1, NX)

time: 144 us -> 143 us (level)
  starting transfers between devices: 31.9 us -> 28.2 us
  waiting for transfers between devices: 3.1 us -> 6.49 us
    ppermute x3, waiting for transfers between devices: 0.83 us -> 3.16 us  [on_device(): lax.ppermute(qpack, 'x', [((x + k) % NX, x) for x in range(NX)])]
    ppermute x3 -> x2, starting transfers between devices: 13.2 us -> 11.3 us  [swap_cores(): return lax.ppermute(x, 'core', [(0, 1), (1, 0)])]
    ppermute x3, starting transfers between devices: 11.1 us -> 9.32 us  [on_device(): lax.ppermute(qpack, 'x', [((x + k) % NX, x) for x in range(NX)])]
    ppermute x3 -> x2, waiting for transfers between devices: 1.98 us -> 3.32 us  [swap_cores(): return lax.ppermute(x, 'core', [(0, 1), (1, 0)])]
  transfers between devices with their start and end apart: 7 -> 6, of which waited for: 3 -> 4; matrix products, arithmetic and copies ran while one was open for 0% -> 0% of each run, Pallas kernels for 2% -> 2%
where the time goes in v7:
time: 143 us; the launch traced here: 142 us
  blocking collectives  95.5 us (67%)
  starting transfers between devices  28.2 us (20%)
  Pallas kernels  9.38 us (7%)
  waiting for transfers between devices  6.49 us (5%)
  other arithmetic  1.58 us (1%)
    all_to_all x5, blocking collectives, exchange(): return lax.all_to_all(x, AXES, 0, 0, axis_index_groups=groups, tiled=True)  78.3 us
    all_to_all x1, blocking collectives, on_device(): lax.all_to_all(jnp.broadcast_to(both[None], (8, PACK + HALF, LANES)), ('c...  17.2 us
    ppermute x2, starting transfers between devices, swap_cores(): return lax.ppermute(x, 'core', [(0, 1), (1, 0)])  11.3 us
    ppermute x3, starting transfers between devices, on_device(): lax.ppermute(qpack, 'x', [((x + k) % NX, x) for x in range(NX)])  9.32 us
    all_to_all x1, starting transfers between devices, exchange(): return lax.all_to_all(x, AXES, 0, 0, axis_index_groups=groups, tiled=True)  7.56 us
    pallas_call x1, Pallas kernels, on_device(): call(solve_kernel, [VM], (shape(2 * QH, RANK), shape(2 * DH, RANK), shape...  3.9 us
    ppermute x2, waiting for transfers between devices, swap_cores(): return lax.ppermute(x, 'core', [(0, 1), (1, 0)])  3.32 us
    ppermute x3, waiting for transfers between devices, on_device(): lax.ppermute(qpack, 'x', [((x + k) % NX, x) for x in range(NX)])  3.16 us
  transfers between devices with their start and end apart: 6, of which 4 were waited for; matrix products, arithmetic and copies ran while one was open for 0% of the time, Pallas kernels for 2%

profile of v7, /device:TPU:1, one launch (start us, length us, event | category | flops | bytes accessed | tf_op | source)
XLA Modules:
  0.0 142.1 jit_solution(4318935868037296585)
XLA Ops:
  0.6 1.7 %shard_map.110 = f32[3088,128]{1,0:T(8,128)S(1)} custom-call(bf16[32,8192]{1,0:T(8,128)(2,1)} %bitcast.27, bf16[32,8192]{1,0:T(8,128)(2,1)} %bitcast.31, bf16[64,8192]{1,0:T(8,128)(2,1)} %bitcast.19, bf16[64,8192]{1,0:T(8,128)(2,1)} %bitcast.23, f32[16,64]{1,0:T(8,128)} %bitcast.38, f32[16,64]{1,0:T(8,128)} %bitcast.40), custom_call_target="tpu_custom_call" | custom-call | flops 3145728 | bytes 3145728 | tf_op jit(solution)/shard_map/pallas_call | solution.py:286
  2.3 0.0 copy-start.4
  2.3 0.0 copy-start.5
  2.3 8.8 %collective-permute-start = (f32[3088,128]{1,0:T(8,128)S(1)}, f32[3088,128]{1,0:T(8,128)S(1)}, u32[]{:S(2)}, u32[]{:S(2)}) collective-permute-start(f32[3088,128]{1,0:T(8,128)S(1)} %shard_map.110), channel_id=1, source_target_pairs={{0,4},{4,0},{1,5},{5,1},{2,6},{6,2},{3,7},{7,3},{8,12},{12,8},{9,1... | collective-permute-start | bytes 4743176 | tf_op jit(solution)/shard_map/ppermute | solution.py:274
  11.1 1.6 %shard_map.109 = f32[3072,128]{1,0:T(8,128)S(1)} custom-call(bf16[32,8192]{1,0:T(8,128)(2,1)} %bitcast.28, bf16[32,8192]{1,0:T(8,128)(2,1)} %bitcast.32, bf16[64,8192]{1,0:T(8,128)(2,1)} %bitcast.20, bf16[64,8192]{1,0:T(8,128)(2,1)} %bitcast.24), custom_call_target="tpu_custom_call" | custom-call | flops 3145728 | bytes 3145728 | tf_op jit(solution)/shard_map/pallas_call | solution.py:290
  12.7 0.1 maximum_bitcast_fusion
  12.8 1.4 collective-permute-done
  14.2 1.4 slice_add_fusion
  15.5 7.6 %all-to-all-start = ((f32[4,16,48,128]{3,2,1,0:T(8,128)}), f32[4,16,48,128]{3,2,1,0:T(8,128)S(1)}, u32[]{:S(2)}, u32[]{:S(2)}) async-start(f32[4,16,48,128]{3,2,1,0:T(8,128)} %bitcast.6), calls=%async_computation | async-start | bytes 3145728 | tf_op jit(solution)/shard_map/all_to_all | solution.py:68
  23.1 4.4 %collective-permute-start.1 = (f32[2,16,128]{2,1,0:T(8,128)S(1)}, f32[2,16,128]{2,1,0:T(8,128)S(1)}, u32[]{:S(2)}, u32[]{:S(2)}) collective-permute-start(f32[2,16,128]{2,1,0:T(8,128)S(1)} %pad_maximum_fusion.2), channel_id=1, source_target_pairs={{1,0},{2,1},{3,2},{0,3},{5,4},{6,5},{7,6},{4,7},{9,8},{10,9},{11,1... | collective-permute-start | bytes 49160 | tf_op jit(solution)/shard_map/ppermute | solution.py:296
  27.5 2.4 %collective-permute-start.2 = (f32[2,16,128]{2,1,0:T(8,128)S(1)}, f32[2,16,128]{2,1,0:T(8,128)S(1)}, u32[]{:S(2)}, u32[]{:S(2)}) collective-permute-start(f32[2,16,128]{2,1,0:T(8,128)S(1)} %pad_maximum_fusion.2), channel_id=1, source_target_pairs={{2,0},{3,1},{0,2},{1,3},{6,4},{7,5},{4,6},{5,7},{10,8},{11,9},{8,1... | collective-permute-start | bytes 49160 | tf_op jit(solution)/shard_map/ppermute | solution.py:296
  29.9 2.5 %collective-permute-start.3 = (f32[2,16,128]{2,1,0:T(8,128)S(1)}, f32[2,16,128]{2,1,0:T(8,128)S(1)}, u32[]{:S(2)}, u32[]{:S(2)}) collective-permute-start(f32[2,16,128]{2,1,0:T(8,128)S(1)} %pad_maximum_fusion.2), channel_id=1, source_target_pairs={{3,0},{0,1},{1,2},{2,3},{7,4},{4,5},{5,6},{6,7},{11,8},{8,9},{9,10... | collective-permute-start | bytes 49160 | tf_op jit(solution)/shard_map/ppermute | solution.py:296
  32.4 1.0 collective-permute-done.2
  33.4 2.1 %collective-permute-done.3 = f32[2,16,128]{2,1,0:T(8,128)S(1)} collective-permute-done((f32[2,16,128]{2,1,0:T(8,128)S(1)}, f32[2,16,128]{2,1,0:T(8,128)S(1)}, u32[]{:S(2)}, u32[]{:S(2)}) %collective-permute-start.3) | collective-permute-done | bytes 16416 | tf_op jit(solution)/shard_map/ppermute | solution.py:296
  35.6 0.1 reduce_sum.27
  35.7 20.1 %all_to_all.35.parts = f32[16,48,128]{2,1,0:T(8,128)S(1)} all-to-all(f32[16,48,128]{2,1,0:T(8,128)S(1)} %reduce_sum.27), channel_id=1, replica_groups={{0,16,32,48,128,144,160,176,256,272,288,304,384,400,416,432},{8,24,40,5..., dimensions={0} | all-to-all | bytes 786432 | tf_op jit(solution)/shard_map/all_to_all | solution.py:68
  55.8 0.2 shard_map.111
  56.1 10.5 %all_to_all.36 = f32[8,24,128]{2,1,0:T(8,128)S(1)} all-to-all(f32[8,24,128]{2,1,0:T(8,128)S(1)} %get-tuple-element.25), channel_id=1, replica_groups={{0,64,128,192,256,320,384,448},{8,72,136,200,264,328,392,456},{16,80,14..., dimensions={0} | all-to-all | bytes 196608 | tf_op jit(solution)/shard_map/all_to_all | solution.py:68
  66.6 12.5 %all_to_all.37 = f32[8,24,128]{2,1,0:T(8,128)S(1)} all-to-all(f32[8,24,128]{2,1,0:T(8,128)S(1)} %broadcast_in_dim.10), channel_id=1, replica_groups={{0,8,16,24,32,40,48,56},{64,72,80,88,96,104,112,120},{128,136,144,152,1..., dimensions={0} | all-to-all | bytes 196608 | tf_op jit(solution)/shard_map/all_to_all | solution.py:68
  79.2 17.2 %all_to_all.38.all_ref = f32[8,72,128]{2,1,0:T(8,128)S(1)} all-to-all(f32[8,72,128]{2,1,0:T(8,128)S(1)} %broadcast_in_dim.11), channel_id=1, replica_groups=mesh['z'=8,'y'=8,'core'=2,'x'=4] {'core','x'}, dimensions={0} | all-to-all | bytes 589824 | tf_op jit(solution)/shard_map/all_to_all | solution.py:307
  96.3 3.9 %shard_map.112 = (f32[32,64]{1,0:T(8,128)}, f32[64,64]{1,0:T(8,128)}, f32[16,64]{1,0:T(8,128)}, f32[16,64]{1,0:T(8,128)}, f32[16,48,128]{2,1,0:T(8,128)S(1)}) custom-call(f32[8,72,128]{2,1,0:T(8,128)S(1)} %all_to_all.38.all_ref), custom_call_target="tpu_custom_call" | custom-call | flops 1048576 | bytes 1048576 | tf_op jit(solution)/shard_map/pallas_call | solution.py:310
  100.2 18.5 %all_to_all.39 = f32[16,48,128]{2,1,0:T(8,128)S(1)} all-to-all(f32[16,48,128]{2,1,0:T(8,128)S(1)} %get-tuple-element.27), channel_id=1, replica_groups={{0,16,32,48,128,144,160,176,256,272,288,304,384,400,416,432},{8,24,40,5..., dimensions={0} | all-to-all | bytes 786432 | tf_op jit(solution)/shard_map/all_to_all | solution.py:68
  118.7 0.1 broadcast_in_dim.12
  118.8 0.0 copy-start
  118.8 0.0 copy-start.1
  118.8 0.0 copy-start.2
  118.9 0.0 copy-start.3
  118.9 16.7 %all_to_all.40.src = f32[4,16,48,128]{3,2,1,0:T(8,128)S(1)} all-to-all(f32[4,16,48,128]{3,2,1,0:T(8,128)S(1)} %broadcast_in_dim.12), channel_id=1, replica_groups={{0,8,64,72},{16,24,80,88},{32,40,96,104},{48,56,112,120},{128,136,192,2..., dimensions={0} | all-to-all | bytes 3145728 | tf_op jit(solution)/shard_map/all_to_all | solution.py:68
  135.6 2.5 %collective-permute-start.4 = (f32[4,16,48,128]{3,2,1,0:T(8,128)S(1)}, f32[4,16,48,128]{3,2,1,0:T(8,128)S(1)}, u32[]{:S(2)}, u32[]{:S(2)}) collective-permute-start(f32[4,16,48,128]{3,2,1,0:T(8,128)S(1)} %all_to_all.40.src), channel_id=1, source_target_pairs={{0,4},{4,0},{1,5},{5,1},{2,6},{6,2},{3,7},{7,3},{8,12},{12,8},{9,1... | collective-permute-start | bytes 4718600 | tf_op jit(solution)/shard_map/ppermute | solution.py:274
  138.2 1.0 shard_map.113
  139.2 2.0 %collective-permute-done.4.src = f32[4,16,48,128]{3,2,1,0:T(8,128)S(1)} collective-permute-done((f32[4,16,48,128]{3,2,1,0:T(8,128)S(1)}, f32[4,16,48,128]{3,2,1,0:T(8,128)S(1)}, u32[]{:S(2)}, u32[]{:S(2)}) %collective-permute-start.4) | collective-permute-done | bytes 1572896 | tf_op jit(solution)/shard_map/ppermute | solution.py:274
  141.1 1.0 shard_map.114
  (16 shorter events, 0.1 us)
Async XLA Ops:
  2.3 10.4 %copy-start.4 = (f32[64,16]{0,1:T(8,128)S(1)}, f32[64,16]{0,1:T(8,128)}, u32[]{:S(2)}) copy-start(f32[64,16]{0,1:T(8,128)} %param.8) | copy-start | bytes 12292
  2.3 10.4 %copy-start.5 = (f32[64,16]{0,1:T(8,128)S(1)}, f32[64,16]{0,1:T(8,128)}, u32[]{:S(2)}) copy-start(f32[64,16]{0,1:T(8,128)} %param.11) | copy-start | bytes 12292
  2.3 11.8 %collective-permute-start = (f32[3088,128]{1,0:T(8,128)S(1)}, f32[3088,128]{1,0:T(8,128)S(1)}, u32[]{:S(2)}, u32[]{:S(2)}) collective-permute-start(f32[3088,128]{1,0:T(8,128)S(1)} %shard_map.110), channel_id=1, source_target_pairs={{0,4},{4,0},{1,5},{5,1},{2,6},{6,2},{3,7},{7,3},{8,12},{12,8},{9,1... | collective-permute-start | bytes 4743176 | tf_op jit(solution)/shard_map/ppermute | solution.py:274
  15.5 20.1 %all-to-all-start = ((f32[4,16,48,128]{3,2,1,0:T(8,128)}), f32[4,16,48,128]{3,2,1,0:T(8,128)S(1)}, u32[]{:S(2)}, u32[]{:S(2)}) async-start(f32[4,16,48,128]{3,2,1,0:T(8,128)} %bitcast.6), calls=%async_computation | async-start | bytes 3145728 | tf_op jit(solution)/shard_map/all_to_all | solution.py:68
  23.1 9.3 %collective-permute-start.1 = (f32[2,16,128]{2,1,0:T(8,128)S(1)}, f32[2,16,128]{2,1,0:T(8,128)S(1)}, u32[]{:S(2)}, u32[]{:S(2)}) collective-permute-start(f32[2,16,128]{2,1,0:T(8,128)S(1)} %pad_maximum_fusion.2), channel_id=1, source_target_pairs={{1,0},{2,1},{3,2},{0,3},{5,4},{6,5},{7,6},{4,7},{9,8},{10,9},{11,1... | collective-permute-start | bytes 49160 | tf_op jit(solution)/shard_map/ppermute | solution.py:296
  27.5 6.0 %collective-permute-start.2 = (f32[2,16,128]{2,1,0:T(8,128)S(1)}, f32[2,16,128]{2,1,0:T(8,128)S(1)}, u32[]{:S(2)}, u32[]{:S(2)}) collective-permute-start(f32[2,16,128]{2,1,0:T(8,128)S(1)} %pad_maximum_fusion.2), channel_id=1, source_target_pairs={{2,0},{3,1},{0,2},{1,3},{6,4},{7,5},{4,6},{5,7},{10,8},{11,9},{8,1... | collective-permute-start | bytes 49160 | tf_op jit(solution)/shard_map/ppermute | solution.py:296
  29.9 5.7 %collective-permute-start.3 = (f32[2,16,128]{2,1,0:T(8,128)S(1)}, f32[2,16,128]{2,1,0:T(8,128)S(1)}, u32[]{:S(2)}, u32[]{:S(2)}) collective-permute-start(f32[2,16,128]{2,1,0:T(8,128)S(1)} %pad_maximum_fusion.2), channel_id=1, source_target_pairs={{3,0},{0,1},{1,2},{2,3},{7,4},{4,5},{5,6},{6,7},{11,8},{8,9},{9,10... | collective-permute-start | bytes 49160 | tf_op jit(solution)/shard_map/ppermute | solution.py:296
  118.8 19.3 %copy-start = (bf16[1,64,8192]{2,1,0:T(8,128)(2,1)S(1)}, bf16[1,64,8192]{2,1,0:T(8,128)(2,1)}, u32[]{:S(2)}) copy-start(bf16[1,64,8192]{2,1,0:T(8,128)(2,1)} %param.9) | copy-start | bytes 3145732
  118.8 19.3 %copy-start.1 = (bf16[1,64,8192]{2,1,0:T(8,128)(2,1)S(1)}, bf16[1,64,8192]{2,1,0:T(8,128)(2,1)}, u32[]{:S(2)}) copy-start(bf16[1,64,8192]{2,1,0:T(8,128)(2,1)} %param.10) | copy-start | bytes 3145732
  118.8 19.3 %copy-start.2 = (bf16[1,32,8192]{2,1,0:T(8,128)(2,1)S(1)}, bf16[1,32,8192]{2,1,0:T(8,128)(2,1)}, u32[]{:S(2)}) copy-start(bf16[1,32,8192]{2,1,0:T(8,128)(2,1)} %param.6) | copy-start | bytes 1572868
  118.9 19.3 %copy-start.3 = (bf16[1,32,8192]{2,1,0:T(8,128)(2,1)S(1)}, bf16[1,32,8192]{2,1,0:T(8,128)(2,1)}, u32[]{:S(2)}) copy-start(bf16[1,32,8192]{2,1,0:T(8,128)(2,1)} %param.7) | copy-start | bytes 1572868
  135.6 5.5 %collective-permute-start.4 = (f32[4,16,48,128]{3,2,1,0:T(8,128)S(1)}, f32[4,16,48,128]{3,2,1,0:T(8,128)S(1)}, u32[]{:S(2)}, u32[]{:S(2)}) collective-permute-start(f32[4,16,48,128]{3,2,1,0:T(8,128)S(1)} %all_to_all.40.src), channel_id=1, source_target_pairs={{0,4},{4,0},{1,5},{5,1},{2,6},{6,2},{3,7},{7,3},{8,12},{12,8},{9,1... | collective-permute-start | bytes 4718600 | tf_op jit(solution)/shard_map/ppermute | solution.py:274

commit v8 on v7

--- a/solution.py
+++ b/solution.py
@@ -118,7 +118,8 @@
         s = s + parts[i]
     s_ref[...] = s
     core, x = lax.axis_index("core"), lax.axis_index("x")
-    q = [q_all[(a - x + NX) % NX, (c + core) % NC] for c in range(NC) for a in range(NX)]
+    high, low = x // 2, x % 2
+    q = [q_all[(a // 2 + high) % 2, (a + low) % 2, (c + core) % NC] for c in range(NC) for a in range(NX)]
     r = jnp.dot(s, jnp.concatenate(q, axis=0), precision=HIGH, preferred_element_type=jnp.float32)
     low = jnp.concatenate([r[0:QH], pltpu.roll(r[40:48], RANK, 1)], axis=0)
     lane = lax.broadcasted_iota(jnp.int32, (PACK, LANES), 1)
@@ -292,9 +293,8 @@
     qpack = jnp.stack([qpack, other[ROWS:]])
     total, qpack = lax.optimization_barrier(((keep + other[:ROWS]).reshape(half.shape), qpack))
     part = exchange(total, NEAR)
-    q_all = jnp.stack([qpack] + [
-        lax.ppermute(qpack, "x", [((x + k) % NX, x) for x in range(NX)]) for k in range(1, NX)
-    ])
+    q_all = jnp.stack([qpack, lax.ppermute(qpack, "x", [(x, x ^ 1) for x in range(NX)])])
+    q_all = jnp.stack([q_all, lax.ppermute(q_all, "x", [(x, x ^ 2) for x in range(NX)])])
     part, q_all = lax.optimization_barrier((part, q_all))
     part = exchange(jnp.sum(part, axis=0), FAR)
     s_own, f = call(

time: 143 us -> 142 us (level)
  starting transfers between devices: 28.2 us -> 26.3 us
  waiting for transfers between devices: 6.49 us -> 8.14 us
    ppermute x3 -> x2, starting transfers between devices: 9.32 us -> 7.45 us  [the longest x1 4.35 us: on_device(): lax.ppermute(q_all, 'x', [(x, x ^ 2) for x in range(NX)])]
    all_to_all x1, blocking collectives: 17.2 us -> 15.3 us  [on_device(): lax.all_to_all(jnp.broadcast_to(both[None], (8, PACK + HALF, LANES)), ('c...]
    all_to_all x5, blocking collectives: 78.3 us -> 79.8 us  [exchange(): return lax.all_to_all(x, AXES, 0, 0, axis_index_groups=groups, tiled=True)]
    ppermute x3 -> x2, waiting for transfers between devices: 3.16 us -> 3.45 us  [the longest x1 1.8 us: on_device(): lax.ppermute(q_all, 'x', [(x, x ^ 2) for x in range(NX)])]
  transfers between devices with their start and end apart: 6 -> 5, of which waited for: 4 -> 5; matrix products, arithmetic and copies ran while one was open for 0% -> 0% of each run, Pallas kernels for 2% -> 2%
where the time goes in v8:
time: 142 us
  blocking collectives  95.1 us (67%)
  starting transfers between devices  26.3 us (19%)
  Pallas kernels  9.4 us (7%)
  waiting for transfers between devices  8.14 us (6%)
  other arithmetic  1.58 us (1%)
    all_to_all x5, blocking collectives, exchange(): return lax.all_to_all(x, AXES, 0, 0, axis_index_groups=groups, tiled=True)  79.8 us
    all_to_all x1, blocking collectives, on_device(): lax.all_to_all(jnp.broadcast_to(both[None], (8, PACK + HALF, LANES)), ('c...  15.3 us
    ppermute x2, starting transfers between devices, swap_cores(): return lax.ppermute(x, 'core', [(0, 1), (1, 0)])  11.3 us
    all_to_all x1, starting transfers between devices, exchange(): return lax.all_to_all(x, AXES, 0, 0, axis_index_groups=groups, tiled=True)  7.56 us
    ppermute x1, starting transfers between devices, on_device(): lax.ppermute(q_all, 'x', [(x, x ^ 2) for x in range(NX)])  4.35 us
    pallas_call x1, Pallas kernels, on_device(): call(solve_kernel, [VM], (shape(2 * QH, RANK), shape(2 * DH, RANK), shape...  3.9 us
    ppermute x2, waiting for transfers between devices, swap_cores(): return lax.ppermute(x, 'core', [(0, 1), (1, 0)])  3.32 us
    ppermute x1, starting transfers between devices, on_device(): lax.ppermute(qpack, 'x', [(x, x ^ 1) for x in range(NX)])  3.11 us
  transfers between devices with their start and end apart: 5, of which 5 were waited for; matrix products, arithmetic and copies ran while one was open for 0% of the time, Pallas kernels for 2%

profile of v8, /device:TPU:1, one launch (start us, length us, event | category | flops | bytes accessed | tf_op | source)
XLA Modules:
  0.0 141.6 jit_solution(16536992540333974995)
XLA Ops:
  0.6 1.7 %shard_map.110 = f32[3088,128]{1,0:T(8,128)S(1)} custom-call(bf16[32,8192]{1,0:T(8,128)(2,1)} %bitcast.28, bf16[32,8192]{1,0:T(8,128)(2,1)} %bitcast.32, bf16[64,8192]{1,0:T(8,128)(2,1)} %bitcast.20, bf16[64,8192]{1,0:T(8,128)(2,1)} %bitcast.24, f32[16,64]{1,0:T(8,128)} %bitcast.39, f32[16,64]{1,0:T(8,128)} %bitcast.41), custom_call_target="tpu_custom_call" | custom-call | flops 3145728 | bytes 3145728 | tf_op jit(solution)/shard_map/pallas_call | solution.py:287
  2.3 0.0 copy-start.4
  2.3 0.0 copy-start.5
  2.3 8.8 %collective-permute-start = (f32[3088,128]{1,0:T(8,128)S(1)}, f32[3088,128]{1,0:T(8,128)S(1)}, u32[]{:S(2)}, u32[]{:S(2)}) collective-permute-start(f32[3088,128]{1,0:T(8,128)S(1)} %shard_map.110), channel_id=1, source_target_pairs={{0,4},{4,0},{1,5},{5,1},{2,6},{6,2},{3,7},{7,3},{8,12},{12,8},{9,1... | collective-permute-start | bytes 4743176 | tf_op jit(solution)/shard_map/ppermute | solution.py:275
  11.1 1.6 %shard_map.109 = f32[3072,128]{1,0:T(8,128)S(1)} custom-call(bf16[32,8192]{1,0:T(8,128)(2,1)} %bitcast.29, bf16[32,8192]{1,0:T(8,128)(2,1)} %bitcast.33, bf16[64,8192]{1,0:T(8,128)(2,1)} %bitcast.21, bf16[64,8192]{1,0:T(8,128)(2,1)} %bitcast.25), custom_call_target="tpu_custom_call" | custom-call | flops 3145728 | bytes 3145728 | tf_op jit(solution)/shard_map/pallas_call | solution.py:291
  12.7 0.1 maximum_bitcast_fusion
  12.8 1.4 collective-permute-done
  14.2 1.4 slice_add_fusion
  15.5 7.6 %all-to-all-start = ((f32[4,16,48,128]{3,2,1,0:T(8,128)}), f32[4,16,48,128]{3,2,1,0:T(8,128)S(1)}, u32[]{:S(2)}, u32[]{:S(2)}) async-start(f32[4,16,48,128]{3,2,1,0:T(8,128)} %bitcast.6), calls=%async_computation | async-start | bytes 3145728 | tf_op jit(solution)/shard_map/all_to_all | solution.py:68
  23.1 3.1 %collective-permute-start.1 = (f32[2,16,128]{2,1,0:T(8,128)S(1)}, f32[2,16,128]{2,1,0:T(8,128)S(1)}, u32[]{:S(2)}, u32[]{:S(2)}) collective-permute-start(f32[2,16,128]{2,1,0:T(8,128)S(1)} %pad_maximum_fusion.3), channel_id=1, source_target_pairs={{0,1},{1,0},{2,3},{3,2},{4,5},{5,4},{6,7},{7,6},{8,9},{9,8},{10,11... | collective-permute-start | bytes 49160 | tf_op jit(solution)/shard_map/ppermute | solution.py:296
  26.2 1.7 %collective-permute-done.1 = f32[2,16,128]{2,1,0:T(8,128)S(1)} collective-permute-done((f32[2,16,128]{2,1,0:T(8,128)S(1)}, f32[2,16,128]{2,1,0:T(8,128)S(1)}, u32[]{:S(2)}, u32[]{:S(2)}) %collective-permute-start.1) | collective-permute-done | bytes 16416 | tf_op jit(solution)/shard_map/ppermute | solution.py:296
  27.8 4.3 %collective-permute-start.2 = (f32[2,2,16,128]{3,2,1,0:T(8,128)S(1)}, f32[2,2,16,128]{3,2,1,0:T(8,128)S(1)}, u32[]{:S(2)}, u32[]{:S(2)}) collective-permute-start(f32[2,2,16,128]{3,2,1,0:T(8,128)S(1)} %get-tuple-element.37), channel_id=1, source_target_pairs={{0,2},{1,3},{2,0},{3,1},{4,6},{5,7},{6,4},{7,5},{8,10},{9,11},{10,... | collective-permute-start | bytes 98312 | tf_op jit(solution)/shard_map/ppermute | solution.py:297
  32.2 1.8 %collective-permute-done.2 = f32[2,2,16,128]{3,2,1,0:T(8,128)S(1)} collective-permute-done((f32[2,2,16,128]{3,2,1,0:T(8,128)S(1)}, f32[2,2,16,128]{3,2,1,0:T(8,128)S(1)}, u32[]{:S(2)}, u32[]{:S(2)}) %collective-permute-start.2) | collective-permute-done | bytes 32800 | tf_op jit(solution)/shard_map/ppermute | solution.py:297
  34.0 1.4 all-to-all-done
  35.4 0.1 reduce_sum.27
  35.5 21.6 %all_to_all.35.parts = f32[16,48,128]{2,1,0:T(8,128)S(1)} all-to-all(f32[16,48,128]{2,1,0:T(8,128)S(1)} %reduce_sum.27), channel_id=1, replica_groups={{0,16,32,48,128,144,160,176,256,272,288,304,384,400,416,432},{8,24,40,5..., dimensions={0} | all-to-all | bytes 786432 | tf_op jit(solution)/shard_map/all_to_all | solution.py:68
  57.1 0.3 shard_map.111
  57.4 11.6 %all_to_all.36 = f32[8,24,128]{2,1,0:T(8,128)S(1)} all-to-all(f32[8,24,128]{2,1,0:T(8,128)S(1)} %get-tuple-element.25), channel_id=1, replica_groups={{0,64,128,192,256,320,384,448},{8,72,136,200,264,328,392,456},{16,80,14..., dimensions={0} | all-to-all | bytes 196608 | tf_op jit(solution)/shard_map/all_to_all | solution.py:68
  69.1 11.3 %all_to_all.37 = f32[8,24,128]{2,1,0:T(8,128)S(1)} all-to-all(f32[8,24,128]{2,1,0:T(8,128)S(1)} %broadcast_in_dim.10), channel_id=1, replica_groups={{0,8,16,24,32,40,48,56},{64,72,80,88,96,104,112,120},{128,136,144,152,1..., dimensions={0} | all-to-all | bytes 196608 | tf_op jit(solution)/shard_map/all_to_all | solution.py:68
  80.5 15.3 %all_to_all.38.all_ref = f32[8,72,128]{2,1,0:T(8,128)S(1)} all-to-all(f32[8,72,128]{2,1,0:T(8,128)S(1)} %broadcast_in_dim.11), channel_id=1, replica_groups=mesh['z'=8,'y'=8,'core'=2,'x'=4] {'core','x'}, dimensions={0} | all-to-all | bytes 589824 | tf_op jit(solution)/shard_map/all_to_all | solution.py:307
  95.8 3.9 %shard_map.112 = (f32[32,64]{1,0:T(8,128)}, f32[64,64]{1,0:T(8,128)}, f32[16,64]{1,0:T(8,128)}, f32[16,64]{1,0:T(8,128)}, f32[16,48,128]{2,1,0:T(8,128)S(1)}) custom-call(f32[8,72,128]{2,1,0:T(8,128)S(1)} %all_to_all.38.all_ref), custom_call_target="tpu_custom_call" | custom-call | flops 1048576 | bytes 1048576 | tf_op jit(solution)/shard_map/pallas_call | solution.py:310
  99.7 18.5 %all_to_all.39 = f32[16,48,128]{2,1,0:T(8,128)S(1)} all-to-all(f32[16,48,128]{2,1,0:T(8,128)S(1)} %get-tuple-element.27), channel_id=1, replica_groups={{0,16,32,48,128,144,160,176,256,272,288,304,384,400,416,432},{8,24,40,5..., dimensions={0} | all-to-all | bytes 786432 | tf_op jit(solution)/shard_map/all_to_all | solution.py:68
  118.1 0.1 broadcast_in_dim.12
  118.3 0.0 copy-start
  118.3 0.0 copy-start.1
  118.3 0.0 copy-start.2
  118.3 0.0 copy-start.3
  118.3 16.7 %all_to_all.40.src = f32[4,16,48,128]{3,2,1,0:T(8,128)S(1)} all-to-all(f32[4,16,48,128]{3,2,1,0:T(8,128)S(1)} %broadcast_in_dim.12), channel_id=1, replica_groups={{0,8,64,72},{16,24,80,88},{32,40,96,104},{48,56,112,120},{128,136,192,2..., dimensions={0} | all-to-all | bytes 3145728 | tf_op jit(solution)/shard_map/all_to_all | solution.py:68
  135.0 2.5 %collective-permute-start.3 = (f32[4,16,48,128]{3,2,1,0:T(8,128)S(1)}, f32[4,16,48,128]{3,2,1,0:T(8,128)S(1)}, u32[]{:S(2)}, u32[]{:S(2)}) collective-permute-start(f32[4,16,48,128]{3,2,1,0:T(8,128)S(1)} %all_to_all.40.src), channel_id=1, source_target_pairs={{0,4},{4,0},{1,5},{5,1},{2,6},{6,2},{3,7},{7,3},{8,12},{12,8},{9,1... | collective-permute-start | bytes 4718600 | tf_op jit(solution)/shard_map/ppermute | solution.py:275
  137.6 1.0 shard_map.113
  138.6 2.0 %collective-permute-done.3.src = f32[4,16,48,128]{3,2,1,0:T(8,128)S(1)} collective-permute-done((f32[4,16,48,128]{3,2,1,0:T(8,128)S(1)}, f32[4,16,48,128]{3,2,1,0:T(8,128)S(1)}, u32[]{:S(2)}, u32[]{:S(2)}) %collective-permute-start.3) | collective-permute-done | bytes 1572896 | tf_op jit(solution)/shard_map/ppermute | solution.py:275
  140.6 1.0 shard_map.114
  (15 shorter events, 0.1 us)
Async XLA Ops:
  2.3 10.4 %copy-start.4 = (f32[64,16]{0,1:T(8,128)S(1)}, f32[64,16]{0,1:T(8,128)}, u32[]{:S(2)}) copy-start(f32[64,16]{0,1:T(8,128)} %param.8) | copy-start | bytes 12292
  2.3 10.4 %copy-start.5 = (f32[64,16]{0,1:T(8,128)S(1)}, f32[64,16]{0,1:T(8,128)}, u32[]{:S(2)}) copy-start(f32[64,16]{0,1:T(8,128)} %param.11) | copy-start | bytes 12292
  2.3 11.8 %collective-permute-start = (f32[3088,128]{1,0:T(8,128)S(1)}, f32[3088,128]{1,0:T(8,128)S(1)}, u32[]{:S(2)}, u32[]{:S(2)}) collective-permute-start(f32[3088,128]{1,0:T(8,128)S(1)} %shard_map.110), channel_id=1, source_target_pairs={{0,4},{4,0},{1,5},{5,1},{2,6},{6,2},{3,7},{7,3},{8,12},{12,8},{9,1... | collective-permute-start | bytes 4743176 | tf_op jit(solution)/shard_map/ppermute | solution.py:275
  15.5 19.9 %all-to-all-start = ((f32[4,16,48,128]{3,2,1,0:T(8,128)}), f32[4,16,48,128]{3,2,1,0:T(8,128)S(1)}, u32[]{:S(2)}, u32[]{:S(2)}) async-start(f32[4,16,48,128]{3,2,1,0:T(8,128)} %bitcast.6), calls=%async_computation | async-start | bytes 3145728 | tf_op jit(solution)/shard_map/all_to_all | solution.py:68
  23.1 4.8 %collective-permute-start.1 = (f32[2,16,128]{2,1,0:T(8,128)S(1)}, f32[2,16,128]{2,1,0:T(8,128)S(1)}, u32[]{:S(2)}, u32[]{:S(2)}) collective-permute-start(f32[2,16,128]{2,1,0:T(8,128)S(1)} %pad_maximum_fusion.3), channel_id=1, source_target_pairs={{0,1},{1,0},{2,3},{3,2},{4,5},{5,4},{6,7},{7,6},{8,9},{9,8},{10,11... | collective-permute-start | bytes 49160 | tf_op jit(solution)/shard_map/ppermute | solution.py:296
  27.8 6.2 %collective-permute-start.2 = (f32[2,2,16,128]{3,2,1,0:T(8,128)S(1)}, f32[2,2,16,128]{3,2,1,0:T(8,128)S(1)}, u32[]{:S(2)}, u32[]{:S(2)}) collective-permute-start(f32[2,2,16,128]{3,2,1,0:T(8,128)S(1)} %get-tuple-element.37), channel_id=1, source_target_pairs={{0,2},{1,3},{2,0},{3,1},{4,6},{5,7},{6,4},{7,5},{8,10},{9,11},{10,... | collective-permute-start | bytes 98312 | tf_op jit(solution)/shard_map/ppermute | solution.py:297
  118.3 19.3 %copy-start = (bf16[1,64,8192]{2,1,0:T(8,128)(2,1)S(1)}, bf16[1,64,8192]{2,1,0:T(8,128)(2,1)}, u32[]{:S(2)}) copy-start(bf16[1,64,8192]{2,1,0:T(8,128)(2,1)} %param.9) | copy-start | bytes 3145732
  118.3 19.3 %copy-start.1 = (bf16[1,64,8192]{2,1,0:T(8,128)(2,1)S(1)}, bf16[1,64,8192]{2,1,0:T(8,128)(2,1)}, u32[]{:S(2)}) copy-start(bf16[1,64,8192]{2,1,0:T(8,128)(2,1)} %param.10) | copy-start | bytes 3145732
  118.3 19.3 %copy-start.2 = (bf16[1,32,8192]{2,1,0:T(8,128)(2,1)S(1)}, bf16[1,32,8192]{2,1,0:T(8,128)(2,1)}, u32[]{:S(2)}) copy-start(bf16[1,32,8192]{2,1,0:T(8,128)(2,1)} %param.6) | copy-start | bytes 1572868
  118.3 19.3 %copy-start.3 = (bf16[1,32,8192]{2,1,0:T(8,128)(2,1)S(1)}, bf16[1,32,8192]{2,1,0:T(8,128)(2,1)}, u32[]{:S(2)}) copy-start(bf16[1,32,8192]{2,1,0:T(8,128)(2,1)} %param.7) | copy-start | bytes 1572868
  135.0 5.5 %collective-permute-start.3 = (f32[4,16,48,128]{3,2,1,0:T(8,128)S(1)}, f32[4,16,48,128]{3,2,1,0:T(8,128)S(1)}, u32[]{:S(2)}, u32[]{:S(2)}) collective-permute-start(f32[4,16,48,128]{3,2,1,0:T(8,128)S(1)} %all_to_all.40.src), channel_id=1, source_target_pairs={{0,4},{4,0},{1,5},{5,1},{2,6},{6,2},{3,7},{7,3},{8,12},{12,8},{9,1... | collective-permute-start | bytes 4718600 | tf_op jit(solution)/shard_map/ppermute | solution.py:275

commit v9 on v8

--- a/solution.py
+++ b/solution.py
@@ -17,6 +17,8 @@
 CHUNK = 4096
 CHUNKS = WIDTH // CHUNK
 ROWS = NZ * NY * HALF
+SUM_PARTS = 3
+SUM_ROWS = ROWS // SUM_PARTS
 MIB = 1024 * 1024
 
 
@@ -110,6 +112,19 @@
 
 def keep_kernel(gq, eq, gd, ed, out, bq, cq, bd, cd, sems):
     merge_half(lax.axis_index("core"), (gq, eq, gd, ed), out, (bq, cq, bd, cd), sems)
+
+
+def sum_kernel(a, b, out, buf, sems):
+    copies = []
+    for k in range(SUM_PARTS):
+        for i in range(k * SUM_ROWS, (k + 1) * SUM_ROWS, 256):
+            part = pl.ds(i, 256)
+            buf[part, :] = a[part, :] + b[part, :]
+        part = pl.ds(k * SUM_ROWS, SUM_ROWS)
+        copies.append(pltpu.make_async_copy(buf.at[part], out.at[part], sems.at[k]))
+        copies[-1].start()
+    for c in copies:
+        c.wait()
 
 
 def factor_kernel(parts, q_all, s_ref, f_ref):
@@ -289,9 +304,10 @@
     )(*pinned, *pinned_q)
     other = swap_cores(sent)
     keep = call(keep_kernel, [HB] * 4, shape(ROWS, LANES), VM, buffers, moved=3 << 20)(*pinned)
-    qpack = jnp.concatenate([q_query.T, q_down.T], axis=1)
-    qpack = jnp.stack([qpack, other[ROWS:]])
-    total, qpack = lax.optimization_barrier(((keep + other[:ROWS]).reshape(half.shape), qpack))
+    qpack = jnp.stack([sent[ROWS:], other[ROWS:]])
+    staged = [pltpu.VMEM((ROWS, LANES), jnp.float32), pltpu.SemaphoreType.DMA((SUM_PARTS,))]
+    total = call(sum_kernel, [VM] * 2, shape(ROWS, LANES), HB, staged, 5 << 20)(keep, other)
+    total, qpack = lax.optimization_barrier((total.reshape(half.shape), qpack))
     part = exchange(total, NEAR)
     q_all = jnp.stack([qpack, lax.ppermute(qpack, "x", [(x, x ^ 1) for x in range(NX)])])
     q_all = jnp.stack([q_all, lax.ppermute(q_all, "x", [(x, x ^ 2) for x in range(NX)])])

time: 142 us -> 142 us (level)
  other arithmetic: 1.58 us -> 0.15 us
where the time goes in v9:
time: 142 us; the launch traced here: 141 us
  blocking collectives  95.1 us (67%)
  starting transfers between devices  26.3 us (19%)
  Pallas kernels  10.6 us (7%)
  waiting for transfers between devices  8.23 us (6%)
    all_to_all x5, blocking collectives, exchange(): return lax.all_to_all(x, AXES, 0, 0, axis_index_groups=groups, tiled=True)  79.8 us
    all_to_all x1, blocking collectives, on_device(): lax.all_to_all(jnp.broadcast_to(both[None], (8, PACK + HALF, LANES)), ('c...  15.3 us
    ppermute x2, starting transfers between devices, swap_cores(): return lax.ppermute(x, 'core', [(0, 1), (1, 0)])  11.3 us
    all_to_all x1, starting transfers between devices, exchange(): return lax.all_to_all(x, AXES, 0, 0, axis_index_groups=groups, tiled=True)  7.57 us
    ppermute x1, starting transfers between devices, on_device(): lax.ppermute(q_all, 'x', [(x, x ^ 2) for x in range(NX)])  4.35 us
    pallas_call x1, Pallas kernels, on_device(): call(solve_kernel, [VM], (shape(2 * QH, RANK), shape(2 * DH, RANK), shape...  3.9 us
    ppermute x2, waiting for transfers between devices, swap_cores(): return lax.ppermute(x, 'core', [(0, 1), (1, 0)])  3.41 us
    ppermute x1, starting transfers between devices, on_device(): lax.ppermute(qpack, 'x', [(x, x ^ 1) for x in range(NX)])  3.11 us
  transfers between devices with their start and end apart: 5, of which 5 were waited for; matrix products, arithmetic and copies ran while one was open for 0% of the time, Pallas kernels for 2%

profile of v9, /device:TPU:1, one launch (start us, length us, event | category | flops | bytes accessed | tf_op | source)
XLA Modules:
  0.0 141.4 jit_solution(695256407709271166)
XLA Ops:
  0.6 1.7 %shard_map.110 = f32[3088,128]{1,0:T(8,128)S(1)} custom-call(bf16[32,8192]{1,0:T(8,128)(2,1)} %bitcast.28, bf16[32,8192]{1,0:T(8,128)(2,1)} %bitcast.32, bf16[64,8192]{1,0:T(8,128)(2,1)} %bitcast.20, bf16[64,8192]{1,0:T(8,128)(2,1)} %bitcast.24, f32[16,64]{1,0:T(8,128)} %bitcast.41, f32[16,64]{1,0:T(8,128)} %bitcast.42), custom_call_target="tpu_custom_call" | custom-call | flops 3145728 | bytes 3145728 | tf_op jit(solution)/shard_map/pallas_call | solution.py:302
  2.3 8.8 %collective-permute-start = (f32[3088,128]{1,0:T(8,128)S(1)}, f32[3088,128]{1,0:T(8,128)S(1)}, u32[]{:S(2)}, u32[]{:S(2)}) collective-permute-start(f32[3088,128]{1,0:T(8,128)S(1)} %shard_map.110), channel_id=1, source_target_pairs={{0,4},{4,0},{1,5},{5,1},{2,6},{6,2},{3,7},{7,3},{8,12},{12,8},{9,1... | collective-permute-start | bytes 4743176 | tf_op jit(solution)/shard_map/ppermute | solution.py:290
  11.1 1.6 %shard_map.109.a = f32[3072,128]{1,0:T(8,128)S(1)} custom-call(bf16[32,8192]{1,0:T(8,128)(2,1)} %bitcast.29, bf16[32,8192]{1,0:T(8,128)(2,1)} %bitcast.33, bf16[64,8192]{1,0:T(8,128)(2,1)} %bitcast.21, bf16[64,8192]{1,0:T(8,128)(2,1)} %bitcast.25), custom_call_target="tpu_custom_call" | custom-call | flops 3145728 | bytes 3145728 | tf_op jit(solution)/shard_map/pallas_call | solution.py:306
  12.7 1.4 %collective-permute-done.b = f32[3088,128]{1,0:T(8,128)S(1)} collective-permute-done((f32[3088,128]{1,0:T(8,128)S(1)}, f32[3088,128]{1,0:T(8,128)S(1)}, u32[]{:S(2)}, u32[]{:S(2)}) %collective-permute-start) | collective-permute-done | bytes 1581088 | tf_op jit(solution)/shard_map/ppermute | solution.py:290
  14.1 1.2 shard_map.111
  15.4 7.6 %all-to-all-start = ((f32[4,16,48,128]{3,2,1,0:T(8,128)}), f32[4,16,48,128]{3,2,1,0:T(8,128)S(1)}, u32[]{:S(2)}, u32[]{:S(2)}) async-start(f32[4,16,48,128]{3,2,1,0:T(8,128)} %bitcast.6), calls=%async_computation | async-start | bytes 3145728 | tf_op jit(solution)/shard_map/all_to_all | solution.py:70
  23.0 3.1 %collective-permute-start.1 = (f32[2,16,128]{2,1,0:T(8,128)S(1)}, f32[2,16,128]{2,1,0:T(8,128)S(1)}, u32[]{:S(2)}, u32[]{:S(2)}) collective-permute-start(f32[2,16,128]{2,1,0:T(8,128)S(1)} %pad_maximum_fusion.3), channel_id=1, source_target_pairs={{0,1},{1,0},{2,3},{3,2},{4,5},{5,4},{6,7},{7,6},{8,9},{9,8},{10,11... | collective-permute-start | bytes 49160 | tf_op jit(solution)/shard_map/ppermute | solution.py:312
  26.1 1.7 %collective-permute-done.1 = f32[2,16,128]{2,1,0:T(8,128)S(1)} collective-permute-done((f32[2,16,128]{2,1,0:T(8,128)S(1)}, f32[2,16,128]{2,1,0:T(8,128)S(1)}, u32[]{:S(2)}, u32[]{:S(2)}) %collective-permute-start.1) | collective-permute-done | bytes 16416 | tf_op jit(solution)/shard_map/ppermute | solution.py:312
  27.7 4.3 %collective-permute-start.2 = (f32[2,2,16,128]{3,2,1,0:T(8,128)S(1)}, f32[2,2,16,128]{3,2,1,0:T(8,128)S(1)}, u32[]{:S(2)}, u32[]{:S(2)}) collective-permute-start(f32[2,2,16,128]{3,2,1,0:T(8,128)S(1)} %get-tuple-element.37), channel_id=1, source_target_pairs={{0,2},{1,3},{2,0},{3,1},{4,6},{5,7},{6,4},{7,5},{8,10},{9,11},{10,... | collective-permute-start | bytes 98312 | tf_op jit(solution)/shard_map/ppermute | solution.py:313
  32.1 1.8 %collective-permute-done.2 = f32[2,2,16,128]{3,2,1,0:T(8,128)S(1)} collective-permute-done((f32[2,2,16,128]{3,2,1,0:T(8,128)S(1)}, f32[2,2,16,128]{3,2,1,0:T(8,128)S(1)}, u32[]{:S(2)}, u32[]{:S(2)}) %collective-permute-start.2) | collective-permute-done | bytes 32800 | tf_op jit(solution)/shard_map/ppermute | solution.py:313
  33.9 1.4 all-to-all-done
  35.3 0.1 reduce_sum.27
  35.4 21.6 %all_to_all.35.parts = f32[16,48,128]{2,1,0:T(8,128)S(1)} all-to-all(f32[16,48,128]{2,1,0:T(8,128)S(1)} %reduce_sum.27), channel_id=1, replica_groups={{0,16,32,48,128,144,160,176,256,272,288,304,384,400,416,432},{8,24,40,5..., dimensions={0} | all-to-all | bytes 786432 | tf_op jit(solution)/shard_map/all_to_all | solution.py:70
  57.0 0.3 shard_map.112
  57.3 11.6 %all_to_all.36 = f32[8,24,128]{2,1,0:T(8,128)S(1)} all-to-all(f32[8,24,128]{2,1,0:T(8,128)S(1)} %get-tuple-element.25), channel_id=1, replica_groups={{0,64,128,192,256,320,384,448},{8,72,136,200,264,328,392,456},{16,80,14..., dimensions={0} | all-to-all | bytes 196608 | tf_op jit(solution)/shard_map/all_to_all | solution.py:70
  69.0 11.3 %all_to_all.37 = f32[8,24,128]{2,1,0:T(8,128)S(1)} all-to-all(f32[8,24,128]{2,1,0:T(8,128)S(1)} %broadcast_in_dim.10), channel_id=1, replica_groups={{0,8,16,24,32,40,48,56},{64,72,80,88,96,104,112,120},{128,136,144,152,1..., dimensions={0} | all-to-all | bytes 196608 | tf_op jit(solution)/shard_map/all_to_all | solution.py:70
  80.3 15.3 %all_to_all.38.all_ref = f32[8,72,128]{2,1,0:T(8,128)S(1)} all-to-all(f32[8,72,128]{2,1,0:T(8,128)S(1)} %broadcast_in_dim.11), channel_id=1, replica_groups=mesh['z'=8,'y'=8,'core'=2,'x'=4] {'core','x'}, dimensions={0} | all-to-all | bytes 589824 | tf_op jit(solution)/shard_map/all_to_all | solution.py:323
  95.7 3.9 %shard_map.113 = (f32[32,64]{1,0:T(8,128)}, f32[64,64]{1,0:T(8,128)}, f32[16,64]{1,0:T(8,128)}, f32[16,64]{1,0:T(8,128)}, f32[16,48,128]{2,1,0:T(8,128)S(1)}) custom-call(f32[8,72,128]{2,1,0:T(8,128)S(1)} %all_to_all.38.all_ref), custom_call_target="tpu_custom_call" | custom-call | flops 1048576 | bytes 1048576 | tf_op jit(solution)/shard_map/pallas_call | solution.py:326
  99.6 18.4 %all_to_all.39 = f32[16,48,128]{2,1,0:T(8,128)S(1)} all-to-all(f32[16,48,128]{2,1,0:T(8,128)S(1)} %get-tuple-element.27), channel_id=1, replica_groups={{0,16,32,48,128,144,160,176,256,272,288,304,384,400,416,432},{8,24,40,5..., dimensions={0} | all-to-all | bytes 786432 | tf_op jit(solution)/shard_map/all_to_all | solution.py:70
  118.0 0.1 broadcast_in_dim.12
  118.1 0.0 copy-start
  118.1 0.0 copy-start.1
  118.2 0.0 copy-start.2
  118.2 0.0 copy-start.3
  118.2 16.7 %all_to_all.40.src = f32[4,16,48,128]{3,2,1,0:T(8,128)S(1)} all-to-all(f32[4,16,48,128]{3,2,1,0:T(8,128)S(1)} %broadcast_in_dim.12), channel_id=1, replica_groups={{0,8,64,72},{16,24,80,88},{32,40,96,104},{48,56,112,120},{128,136,192,2..., dimensions={0} | all-to-all | bytes 3145728 | tf_op jit(solution)/shard_map/all_to_all | solution.py:70
  134.9 2.5 %collective-permute-start.3 = (f32[4,16,48,128]{3,2,1,0:T(8,128)S(1)}, f32[4,16,48,128]{3,2,1,0:T(8,128)S(1)}, u32[]{:S(2)}, u32[]{:S(2)}) collective-permute-start(f32[4,16,48,128]{3,2,1,0:T(8,128)S(1)} %all_to_all.40.src), channel_id=1, source_target_pairs={{0,4},{4,0},{1,5},{5,1},{2,6},{6,2},{3,7},{7,3},{8,12},{12,8},{9,1... | collective-permute-start | bytes 4718600 | tf_op jit(solution)/shard_map/ppermute | solution.py:290
  137.4 0.0 copy-done
  137.4 0.0 copy-done.1
  137.5 0.0 copy-done.2
  137.5 1.0 shard_map.114
  138.5 2.0 %collective-permute-done.3.src = f32[4,16,48,128]{3,2,1,0:T(8,128)S(1)} collective-permute-done((f32[4,16,48,128]{3,2,1,0:T(8,128)S(1)}, f32[4,16,48,128]{3,2,1,0:T(8,128)S(1)}, u32[]{:S(2)}, u32[]{:S(2)}) %collective-permute-start.3) | collective-permute-done | bytes 1572896 | tf_op jit(solution)/shard_map/ppermute | solution.py:290
  140.5 1.0 shard_map.115
  (11 shorter events, 0.1 us)
Async XLA Ops:
  2.3 11.8 %collective-permute-start = (f32[3088,128]{1,0:T(8,128)S(1)}, f32[3088,128]{1,0:T(8,128)S(1)}, u32[]{:S(2)}, u32[]{:S(2)}) collective-permute-start(f32[3088,128]{1,0:T(8,128)S(1)} %shard_map.110), channel_id=1, source_target_pairs={{0,4},{4,0},{1,5},{5,1},{2,6},{6,2},{3,7},{7,3},{8,12},{12,8},{9,1... | collective-permute-start | bytes 4743176 | tf_op jit(solution)/shard_map/ppermute | solution.py:290
  15.4 19.9 %all-to-all-start = ((f32[4,16,48,128]{3,2,1,0:T(8,128)}), f32[4,16,48,128]{3,2,1,0:T(8,128)S(1)}, u32[]{:S(2)}, u32[]{:S(2)}) async-start(f32[4,16,48,128]{3,2,1,0:T(8,128)} %bitcast.6), calls=%async_computation | async-start | bytes 3145728 | tf_op jit(solution)/shard_map/all_to_all | solution.py:70
  23.0 4.8 %collective-permute-start.1 = (f32[2,16,128]{2,1,0:T(8,128)S(1)}, f32[2,16,128]{2,1,0:T(8,128)S(1)}, u32[]{:S(2)}, u32[]{:S(2)}) collective-permute-start(f32[2,16,128]{2,1,0:T(8,128)S(1)} %pad_maximum_fusion.3), channel_id=1, source_target_pairs={{0,1},{1,0},{2,3},{3,2},{4,5},{5,4},{6,7},{7,6},{8,9},{9,8},{10,11... | collective-permute-start | bytes 49160 | tf_op jit(solution)/shard_map/ppermute | solution.py:312
  27.7 6.2 %collective-permute-start.2 = (f32[2,2,16,128]{3,2,1,0:T(8,128)S(1)}, f32[2,2,16,128]{3,2,1,0:T(8,128)S(1)}, u32[]{:S(2)}, u32[]{:S(2)}) collective-permute-start(f32[2,2,16,128]{3,2,1,0:T(8,128)S(1)} %get-tuple-element.37), channel_id=1, source_target_pairs={{0,2},{1,3},{2,0},{3,1},{4,6},{5,7},{6,4},{7,5},{8,10},{9,11},{10,... | collective-permute-start | bytes 98312 | tf_op jit(solution)/shard_map/ppermute | solution.py:313
  118.1 19.3 %copy-start = (bf16[1,64,8192]{2,1,0:T(8,128)(2,1)S(1)}, bf16[1,64,8192]{2,1,0:T(8,128)(2,1)}, u32[]{:S(2)}) copy-start(bf16[1,64,8192]{2,1,0:T(8,128)(2,1)} %param.9) | copy-start | bytes 3145732
  118.1 19.3 %copy-start.1 = (bf16[1,64,8192]{2,1,0:T(8,128)(2,1)S(1)}, bf16[1,64,8192]{2,1,0:T(8,128)(2,1)}, u32[]{:S(2)}) copy-start(bf16[1,64,8192]{2,1,0:T(8,128)(2,1)} %param.10) | copy-start | bytes 3145732
  118.2 19.3 %copy-start.2 = (bf16[1,32,8192]{2,1,0:T(8,128)(2,1)S(1)}, bf16[1,32,8192]{2,1,0:T(8,128)(2,1)}, u32[]{:S(2)}) copy-start(bf16[1,32,8192]{2,1,0:T(8,128)(2,1)} %param.6) | copy-start | bytes 1572868
  118.2 19.3 %copy-start.3 = (bf16[1,32,8192]{2,1,0:T(8,128)(2,1)S(1)}, bf16[1,32,8192]{2,1,0:T(8,128)(2,1)}, u32[]{:S(2)}) copy-start(bf16[1,32,8192]{2,1,0:T(8,128)(2,1)} %param.7) | copy-start | bytes 1572868
  134.9 5.5 %collective-permute-start.3 = (f32[4,16,48,128]{3,2,1,0:T(8,128)S(1)}, f32[4,16,48,128]{3,2,1,0:T(8,128)S(1)}, u32[]{:S(2)}, u32[]{:S(2)}) collective-permute-start(f32[4,16,48,128]{3,2,1,0:T(8,128)S(1)} %all_to_all.40.src), channel_id=1, source_target_pairs={{0,4},{4,0},{1,5},{5,1},{2,6},{6,2},{3,7},{7,3},{8,12},{12,8},{9,1... | collective-permute-start | bytes 4718600 | tf_op jit(solution)/shard_map/ppermute | solution.py:290
